TPU v7x, 32 devices: a whole 2x2x4 slice. The times are simulated.
32 devices in a mesh: groups: 2 (over x), dom: 16 (over z, y, core).
Axes of the slice: x: 2, y: 2, z: 4, core: 2. Of those that a mesh axis runs over, the one named last changes fastest.
Arguments:
- fine_latent: bfloat16 [131072, 128], P(('groups', 'dom')), parts along dimension 0, may hold values from -6 to 6
- fine_edges: bfloat16 [524288, 128], P(('groups', 'dom')), parts along dimension 0, may hold values from -6 to 6
- fine_sender: int32 [524288], P(('groups', 'dom')), parts along dimension 0, may hold values from 0 to 6143
- fine_receiver: int32 [524288], P(('groups', 'dom')), parts along dimension 0, may hold values from 0 to 4095, as said below
- edge_count: int32 [32], P(('groups', 'dom')), parts along dimension 0, may hold values from 8192 to 16384, as said below
- fine_border: int32 [32, 2, 1024], P(('groups', 'dom')), parts along dimension 0, may hold values from 0 to 4095
- pool_rows: int32 [32, 2, 512], P(('groups', 'dom')), parts along dimension 0, may hold values from 0 to 4095
- pool_target: int32 [32, 2, 512], P(('groups', 'dom')), parts along dimension 0, may hold values from 0 to 511
- pool_weight: int32 [32, 2, 512], P(('groups', 'dom')), parts along dimension 0, may hold values from 0 to 4, as said below
- fine_parent: int32 [131072], P(('groups', 'dom')), parts along dimension 0, may hold values from 0 to 511, as said below
- fine_weight: int32 [131072], P(('groups', 'dom')), parts along dimension 0, may hold values from 1 to 4
- coarse_edges: bfloat16 [65536, 128], P(('groups', 'dom')), parts along dimension 0, may hold values from -6 to 6
- coarse_sender: int32 [65536], P(('groups', 'dom')), parts along dimension 0, may hold values from 0 to 767
- coarse_receiver: int32 [65536], P(('groups', 'dom')), parts along dimension 0, may hold values from 0 to 511, as said below
- coarse_border: int32 [32, 2, 128], P(('groups', 'dom')), parts along dimension 0, may hold values from 0 to 511
- coarse_parent: int32 [16384], P(('groups', 'dom')), parts along dimension 0, may hold values from 0 to 1023, as said below
- coarse_weight: int32 [16384], P(('groups', 'dom')), parts along dimension 0, may hold values from 1 to 4
- top_edges: bfloat16 [4096, 128], P('groups'), parts along dimension 0, may hold values from -6 to 6
- top_sender: int32 [4096], P('groups'), parts along dimension 0, may hold values from 0 to 1023
- top_receiver: int32 [4096], P('groups'), parts along dimension 0, may hold values from 0 to 1023, as said below
- edge_in: bfloat16 [3, 384, 128], replicated, may hold values from -0.3125 to 0.3125
- edge_out: bfloat16 [3, 128, 128], replicated, may hold values from -0.5 to 0.5
- node_in: bfloat16 [3, 256, 128], replicated, may hold values from -0.375 to 0.375
- node_out: bfloat16 [3, 128, 128], replicated, may hold values from -0.5 to 0.5
- norm_gain: float32 [3, 2, 128], replicated, may hold values from 0.1 to 1.9
Outputs:
- fine_out: bfloat16 [131072, 128], P(('groups', 'dom')), parts along dimension 0
- coarse_out: bfloat16 [16384, 128], P(('groups', 'dom')), parts along dimension 0
There are 2 independent parts, one for each index of `groups`. A program takes and returns all parts, laid end to end along the dimension named above; an argument that names none is the same for every part. Nothing has to cross between parts.
Inputs may be any that keep to these rules, and one draw needn't show every extreme that they name: `edge_count`: one partition of each mesh has all 16384 edge slots live. `pool_weight`: weight 0 marks an empty slot; for each owner and side the live slots come first; slots from a partition that does not exist are empty. One owner of each mesh receives all 512 slots live from both neighbours. `fine_parent`: every level-1 row of a partition is the parent of at least four of its fine rows. `coarse_parent`: A level-1 node of partition d has its parent among level-2 nodes (d - 1) * 64 to (d + 2) * 64 - 1; every level-2 node j is the parent of at least four level-1 nodes of partition j // 64. `fine_receiver`: A partition's fine edge slots come in aligned tiles of b = min(128, 16384) slots; the receivers of tile t lie among local rows t w to (t + 1) w - 1, with w = b * 4096 // 16384. `coarse_receiver`: A partition's level-1 edges come in aligned tiles of b = min(128, 2048) edges; the receivers of tile t lie among local rows t w to (t + 1) w - 1, with w = b * 512 // 2048. `top_receiver`: Level-2 edges come in aligned tiles of b = min(128, 2048) edges; the receivers of tile t lie among rows t w to (t + 1) w - 1, with w = b * 1024 // 2048.
All inputs are finite; a program needn't handle non-finite values.
Results may differ from a plain program's by a relative error of at most 0.011.
Values may be sent and summed in bfloat16 or wider, within the bound.
No kernel may reach another device: no remote copies, remote signals or barrier semaphores. Data moves between devices by JAX's collectives and lax.ppermute only.
A program may use at most 128 MiB of HBM per device.

v0:
```python
import jax
import jax.numpy as jnp
from jax import lax
from jax.sharding import PartitionSpec as P

epsilon = 1e-05


def with_halo(cells, sides, width):
    for axis, dim in sides:
        count = lax.axis_size(axis)
        ends = count - 1
        head = lax.slice_in_dim(cells, 0, width, axis=dim)
        tail = lax.slice_in_dim(cells, cells.shape[dim] - width, cells.shape[dim], axis=dim)
        cells = jnp.concatenate(
            [
                lax.ppermute(tail, axis, [(i, (i + 1) % count) for i in range(ends)]),
                cells,
                lax.ppermute(head, axis, [((i + 1) % count, i) for i in range(ends)]),
            ],
            axis=dim,
        )
    return cells


def layer_norm(values, gain_row):
    row_mean = jnp.mean(values, axis=-1, keepdims=True)
    centred = values - row_mean
    spread = jnp.mean(centred * centred, axis=-1, keepdims=True)
    return centred * lax.rsqrt(spread + epsilon) * gain_row


def graph_step(
    node_rows,
    sender_rows,
    receiver,
    edge_rows,
    live_mask,
    w_edge_in,
    w_edge_out,
    w_node_in,
    w_node_out,
    gains,
):
    edge_total = receiver.shape[0]
    node_total = node_rows.shape[0]
    width = node_rows.shape[1]
    tile_rows = min(128, edge_total)
    tile_count = edge_total // tile_rows
    window = node_total // tile_count
    offsets = jnp.arange(tile_count, dtype=jnp.int32) * window
    local_ids = receiver.reshape(tile_count, tile_rows) - offsets[:, None]
    picks = (local_ids[:, :, None] == jnp.arange(window, dtype=jnp.int32)[None, None, :]).astype(
        jnp.bfloat16
    )
    node_blocks = node_rows.reshape(tile_count, window, width)
    receiver_rows = (
        jnp.einsum("tew,twl->tel", picks, node_blocks, preferred_element_type=jnp.float32)
        .astype(jnp.bfloat16)
        .reshape(edge_total, width)
    )
    joined = jnp.concatenate([sender_rows, receiver_rows, edge_rows], axis=1)
    hidden = jax.nn.relu(jnp.dot(joined, w_edge_in, preferred_element_type=jnp.float32)).astype(
        jnp.bfloat16
    )
    message = (
        layer_norm(jnp.dot(hidden, w_edge_out, preferred_element_type=jnp.float32), gains[0])
        * live_mask[:, None]
    )
    summed = jnp.einsum(
        "tew,tel->twl",
        picks.astype(jnp.float32),
        message.reshape(tile_count, tile_rows, width),
        precision=lax.Precision.HIGHEST,
    )
    summed = summed.reshape(node_total, width).astype(jnp.bfloat16)
    joined_nodes = jnp.concatenate([node_rows, summed], axis=1)
    inner_rows = jax.nn.relu(
        jnp.dot(joined_nodes, w_node_in, preferred_element_type=jnp.float32)
    ).astype(jnp.bfloat16)
    update = layer_norm(
        jnp.dot(inner_rows, w_node_out, preferred_element_type=jnp.float32), gains[1]
    )
    return (node_rows.astype(jnp.float32) + update).astype(jnp.bfloat16)


def pool_sums(targets, weights, rows, segments):
    matches = targets[:, None] == jnp.arange(segments, dtype=jnp.int32)[None, :]
    weighted = jnp.where(matches, weights[:, None], 0.0)
    sums = lax.dot_general(
        weighted.astype(jnp.bfloat16),
        rows,
        (((0,), (0,)), ((), ())),
        preferred_element_type=jnp.float32,
    )
    totals = jnp.sum(weighted, axis=0)
    return (sums, totals)


def lift_rows(targets, table):
    matches = (targets[:, None] == jnp.arange(table.shape[0], dtype=jnp.int32)[None, :]).astype(
        jnp.bfloat16
    )
    return jnp.dot(matches, table, preferred_element_type=jnp.float32)


def body(
    fine_latent,
    fine_edges,
    fine_sender,
    fine_receiver,
    edge_count,
    fine_border,
    pool_rows,
    pool_target,
    pool_weight,
    fine_parent,
    fine_weight,
    coarse_edges,
    coarse_sender,
    coarse_receiver,
    coarse_border,
    coarse_parent,
    coarse_weight,
    top_edges,
    top_sender,
    top_receiver,
    edge_in,
    edge_out,
    node_in,
    node_out,
    norm_gain,
):
    fine_depth = fine_border.shape[2]
    outgoing = jnp.concatenate(
        [fine_latent[fine_border[0, 0]], fine_latent[fine_border[0, 1]]], axis=0
    )
    padded = with_halo(outgoing, (("dom", 0),), fine_depth)
    extended = jnp.concatenate([fine_latent, padded[:fine_depth], padded[3 * fine_depth :]], axis=0)
    live_mask = (jnp.arange(fine_sender.shape[0], dtype=jnp.int32) < edge_count[0]).astype(
        jnp.float32
    )
    fine_new = graph_step(
        fine_latent,
        extended[fine_sender],
        fine_receiver,
        fine_edges,
        live_mask,
        edge_in[0],
        edge_out[0],
        node_in[0],
        node_out[0],
        norm_gain[0],
    )
    coarse_rows = coarse_parent.shape[0]
    slot_depth = pool_rows.shape[2]
    outbound = jnp.concatenate([fine_new[pool_rows[0, 0]], fine_new[pool_rows[0, 1]]], axis=0)
    pool_padded = with_halo(outbound, (("dom", 0),), slot_depth)
    arrived = jnp.concatenate([pool_padded[:slot_depth], pool_padded[3 * slot_depth :]], axis=0)
    slot_count = 2 * slot_depth
    arrived_weight = pool_weight[0].reshape(slot_count).astype(jnp.float32)
    arrived_target = pool_target[0].reshape(slot_count)
    local_sums, local_totals = pool_sums(
        fine_parent, fine_weight.astype(jnp.float32), fine_new, coarse_rows
    )
    remote_sums, remote_totals = pool_sums(arrived_target, arrived_weight, arrived, coarse_rows)
    coarse_in = ((local_sums + remote_sums) / (local_totals + remote_totals)[:, None]).astype(
        jnp.bfloat16
    )
    coarse_depth = coarse_border.shape[2]
    coarse_outgoing = jnp.concatenate(
        [coarse_in[coarse_border[0, 0]], coarse_in[coarse_border[0, 1]]], axis=0
    )
    coarse_padded = with_halo(coarse_outgoing, (("dom", 0),), coarse_depth)
    coarse_ext = jnp.concatenate(
        [coarse_in, coarse_padded[:coarse_depth], coarse_padded[3 * coarse_depth :]], axis=0
    )
    coarse_mask = jnp.ones((coarse_sender.shape[0],), jnp.float32)
    coarse_new = graph_step(
        coarse_in,
        coarse_ext[coarse_sender],
        coarse_receiver,
        coarse_edges,
        coarse_mask,
        edge_in[1],
        edge_out[1],
        node_in[1],
        node_out[1],
        norm_gain[1],
    )
    block = coarse_rows // 8
    top_count = block * lax.axis_size("dom")
    top_weight = coarse_weight.astype(jnp.float32)
    top_sum, top_total = pool_sums(coarse_parent, top_weight, coarse_new, top_count)
    summed_rows, summed_weight = lax.psum((top_sum, top_total), "dom")
    top_in = (summed_rows / summed_weight[:, None]).astype(jnp.bfloat16)
    top_mask = jnp.ones((top_sender.shape[0],), jnp.float32)
    top_new = graph_step(
        top_in,
        top_in[top_sender],
        top_receiver,
        top_edges,
        top_mask,
        edge_in[2],
        edge_out[2],
        node_in[2],
        node_out[2],
        norm_gain[2],
    )
    coarse_out = (coarse_new.astype(jnp.float32) + lift_rows(coarse_parent, top_new)).astype(
        jnp.bfloat16
    )
    fine_out = (fine_new.astype(jnp.float32) + lift_rows(fine_parent, coarse_out)).astype(
        jnp.bfloat16
    )
    return (fine_out, coarse_out)


def solution(mesh):
    return jax.shard_map(
        body,
        mesh=mesh,
        in_specs=(
            P(("groups", "dom"), None),
            P(("groups", "dom"), None),
            P(("groups", "dom")),
            P(("groups", "dom")),
            P(("groups", "dom")),
            P(("groups", "dom"), None, None),
            P(("groups", "dom"), None, None),
            P(("groups", "dom"), None, None),
            P(("groups", "dom"), None, None),
            P(("groups", "dom")),
            P(("groups", "dom")),
            P(("groups", "dom"), None),
            P(("groups", "dom")),
            P(("groups", "dom")),
            P(("groups", "dom"), None, None),
            P(("groups", "dom")),
            P(("groups", "dom")),
            P("groups", None),
            P("groups"),
            P("groups"),
            P(),
            P(),
            P(),
            P(),
            P(),
        ),
        out_specs=(P(("groups", "dom"), None), P(("groups", "dom"), None)),
        check_vma=False,
    )
```

profile of v0, /device:TPU:0, one launch (start us, length us, event | category | flops | bytes accessed | tf_op | source)
XLA Modules:
  0.0 283.0 jit_solution(668826557036601947)
XLA Ops:
  8.1 4.2 %gather_fusion = bf16[1024,128]{1,0:T(8,128)(2,1)S(1)} fusion(bf16[4096,128]{1,0:T(8,128)(2,1)} %param.25, s32[1024]{0:T(1024)S(1)} %broadcast_clamp_fusion.1), kind=kCustom, calls=%fused_computation | custom fusion | bytes 528384 | tf_op jit(solution)/shard_map/gather | solution.py:136
  12.4 2.4 collective-permute-start
  14.8 3.2 %gather_fusion.1 = bf16[1024,128]{1,0:T(8,128)(2,1)S(1)} fusion(bf16[4096,128]{1,0:T(8,128)(2,1)S(1)} %copy-done, s32[1024]{0:T(1024)S(1)} %broadcast_clamp_fusion), kind=kCustom, calls=%fused_computation.1 | custom fusion | bytes 528384 | tf_op jit(solution)/shard_map/gather | solution.py:136
  18.1 1.4 collective-permute-start.1
  20.5 4.3 %convolution_convert_fusion = bf16[128,128,128]{2,1,0:T(8,128)(2,1)} fusion(bf16[128,32,128]{2,1,0:T(8,128)(2,1)S(1)} %bitcast.133, s32[128,128]{1,0:T(8,128)S(1)} %bitcast_subtract_fusion), kind=kOutput, calls=%fused_computation.37 | convolution fusion | flops 136839168 | bytes 5308416 | tf_op jit(solution)/shard_map/tew,twl->tel/dot_general | solution.py:58
  25.2 1.6 select_reduce_fusion
  27.1 1.3 copy.41
  29.3 57.4 %gather_fusion.2 = bf16[16384,128]{1,0:T(8,128)(2,1)} fusion(bf16[6144,128]{1,0:T(8,128)(2,1)S(1)} %pad_maximum_fusion, s32[16384]{0:T(1024)S(1)} %fusion.103), kind=kCustom, calls=%fused_computation.2 | custom fusion | bytes 8454144 | tf_op jit(solution)/shard_map/gather | solution.py:145
  86.7 11.6 %fusion.155 = (f32[16384]{0:T(1024)S(1)}, f32[16384,128]{1,0:T(8,128)}) fusion(bf16[3,128,128]{2,1,0:T(8,128)(2,1)} %param.46, bf16[16384,128]{1,0:T(8,128)(2,1)} %param.26, bf16[16384,128]{1,0:T(8,128)(2,1)} %bitcast.138, bf16[16384,128]{1,0:T(8,128)(2,1)} %gather_fusion.2, bf16[3,384,128]{2,1,0:T(8,128)(2,1)} %param.45), kind=kOutput, calls=%fused_computation.212 | convolution fusion | flops 2191507456 | bytes 21168128 | tf_op jit(solution)/shard_map/dot_general | solution.py:67
  98.3 7.5 %multiply_reduce_fusion = f32[16384]{0:T(1024)S(1)} fusion(f32[16384,128]{1,0:T(8,128)} %get-tuple-element.21, f32[16384]{0:T(1024)S(1)} %broadcast_multiply_fusion), kind=kLoop, calls=%fused_computation.21 | loop fusion | flops 6275072 | bytes 8519680 | tf_op jit(solution)/shard_map/reduce_sum | solution.py:29
  105.8 7.1 %multiply_multiply_fusion = f32[16384,128]{1,0:T(8,128)S(1)} fusion(f32[16384,128]{1,0:T(8,128)S(1)} %copy-done.1, f32[16384]{0:T(1024)S(1)} %fusion.116, f32[128]{0:T(128)S(1)} %get-tuple-element.16, f32[16384]{0:T(1024)S(1)} %add_rsqrt_fusion, f32[16384]{0:T(1024)S(1)} %broadcast_multiply_fusion), kind=kLoop, calls=%fused_computation.20 | loop fusion | flops 8388608 | bytes 16974336 | tf_op jit(solution)/shard_map/mul | solution.py:67
  112.9 5.2 %fusion.36 = bf16[128,32,128]{2,1,0:T(8,128)(2,1)} fusion(f32[128,128,128]{2,1,0:T(8,128)S(1)} %bitcast.134, s32[128,128]{1,0:T(8,128)S(1)} %bitcast_subtract_fusion), kind=kOutput, calls=%fused_computation.63 | convolution fusion | flops 806354944 | bytes 9502720 | tf_op jit(solution)/shard_map/tew,tel->twl/dot_general | solution.py:70
  118.1 2.5 fusion.160
  120.9 2.6 add_convert_fusion
  123.6 1.7 copy.42
  125.3 1.3 gather_fusion.3
  126.6 5.2 %collective-permute-start.2 = (bf16[512,128]{1,0:T(8,128)(2,1)S(1)}, bf16[512,128]{1,0:T(8,128)(2,1)S(1)}, u32[]{:S(2)}, u32[]{:S(2)}) collective-permute-start(bf16[512,128]{1,0:T(8,128)(2,1)S(1)} %gather_fusion.3), channel_id=1, source_target_pairs={{0,1},{1,2},{2,3},{3,4},{4,5},{5,6},{6,7},{7,8},{8,9},{9,10},{10,1... | collective-permute-start | bytes 393224 | tf_op jit(solution)/shard_map/ppermute | solution.py:17
  131.8 1.6 gather_fusion.4
  133.4 1.3 collective-permute-start.3
  134.7 2.4 fusion.13
  139.3 5.4 %collective-permute-start.4 = (bf16[128,128]{1,0:T(8,128)(2,1)S(1)}, bf16[128,128]{1,0:T(8,128)(2,1)S(1)}, u32[]{:S(2)}, u32[]{:S(2)}) collective-permute-start(bf16[128,128]{1,0:T(8,128)(2,1)S(1)} %gather_fusion.5), channel_id=1, source_target_pairs={{0,1},{1,2},{2,3},{3,4},{4,5},{5,6},{6,7},{7,8},{8,9},{9,10},{10,1... | collective-permute-start | bytes 98312 | tf_op jit(solution)/shard_map/ppermute | solution.py:17
  147.3 1.3 collective-permute-done.5
  148.6 6.2 %gather_fusion.7 = bf16[2048,128]{1,0:T(8,128)(2,1)S(1)} fusion(bf16[768,128]{1,0:T(8,128)(2,1)S(1)} %pad_maximum_fusion.1, s32[2048]{0:T(1024)S(1)} %fusion.129), kind=kCustom, calls=%fused_computation.7 | custom fusion | bytes 1056768 | tf_op jit(solution)/shard_map/gather | solution.py:181
  154.8 2.0 fusion.165
  160.6 1.4 fusion.54
  162.1 33.4 %psum.15 = f32[1024]{0:T(1024)S(1)} all-reduce(f32[1024]{0:T(1024)S(1)} %select_reduce_fusion.1), channel_id=1, replica_groups=mesh['groups'=2,'dom'=16] {'dom'}, use_global_device_ids=true, to_apply=%region_12.13 | all-reduce | flops 1024 | bytes 8192 | tf_op jit(solution)/shard_map/psum | solution.py:195
  195.6 61.5 %all-reduce.2.cloned.1.call-done = f32[1024,128]{1,0:T(8,128)} async-done(((f32[1024,128]{1,0:T(8,128)}), f32[1024,128]{1,0:T(8,128)}) %all-reduce.2.cloned.1.call-update) | async-done | bytes 524304 | tf_op jit(solution)/shard_map/psum | solution.py:195
  258.3 6.4 %gather_fusion.8 = bf16[2048,128]{1,0:T(8,128)(2,1)S(1)} fusion(bf16[1024,128]{1,0:T(8,128)(2,1)S(1)} %divide_convert_fusion, s32[2048]{0:T(1024)S(1)} %fusion.130), kind=kCustom, calls=%fused_computation.8 | custom fusion | bytes 1056768 | tf_op jit(solution)/shard_map/gather | solution.py:200
  265.2 2.0 fusion.175
  269.9 1.4 fusion.180
  272.7 2.2 fusion.12
  274.9 1.3 copy.47
  (114 shorter events, 16.9 us)
Async XLA Ops:
  7.2 7.6 %copy-start = (bf16[4096,128]{1,0:T(8,128)(2,1)S(1)}, bf16[4096,128]{1,0:T(8,128)(2,1)}, u32[]{:S(2)}) copy-start(bf16[4096,128]{1,0:T(8,128)(2,1)} %param.25) | copy-start | bytes 3145732
  7.2 12.3 %copy-start.3 = (s32[16384]{0:T(1024)S(1)}, s32[16384]{0:T(1024)}, u32[]{:S(2)}) copy-start(s32[16384]{0:T(1024)} %param.27) | copy-start | bytes 196612
  7.2 12.4 %copy-start.15 = (f32[3,2,128]{2,1,0:T(2,128)S(1)}, f32[3,2,128]{2,1,0:T(2,128)}, u32[]{:S(2)}) copy-start(f32[3,2,128]{2,1,0:T(2,128)} %param.49) | copy-start | bytes 9220
  7.2 12.9 %copy-start.12 = (s32[1,2,512]{2,1,0:T(2,128)S(1)}, s32[1,2,512]{2,1,0:T(2,128)}, u32[]{:S(2)}) copy-start(s32[1,2,512]{2,1,0:T(2,128)} %param.31) | copy-start | bytes 12292
  7.2 13.0 %copy-start.5 = (s32[4096]{0:T(1024)S(1)}, s32[4096]{0:T(1024)}, u32[]{:S(2)}) copy-start(s32[4096]{0:T(1024)} %param.35) | copy-start | bytes 49156
  7.2 13.0 %copy-start.13 = (s32[1,2,512]{2,1,0:T(2,128)S(1)}, s32[1,2,512]{2,1,0:T(2,128)}, u32[]{:S(2)}) copy-start(s32[1,2,512]{2,1,0:T(2,128)} %param.33) | copy-start | bytes 12292
  7.2 13.0 %copy-start.14 = (s32[1,2,512]{2,1,0:T(2,128)S(1)}, s32[1,2,512]{2,1,0:T(2,128)}, u32[]{:S(2)}) copy-start(s32[1,2,512]{2,1,0:T(2,128)} %param.32) | copy-start | bytes 12292
  7.2 13.0 %copy-start.19 = (s32[1,2,128]{2,1,0:T(2,128)S(1)}, s32[1,2,128]{2,1,0:T(2,128)}, u32[]{:S(2)}) copy-start(s32[1,2,128]{2,1,0:T(2,128)} %param.39) | copy-start | bytes 3076
  7.3 13.0 %copy-start.8 = (s32[2048]{0:T(1024)S(1)}, s32[2048]{0:T(1024)}, u32[]{:S(2)}) copy-start(s32[2048]{0:T(1024)} %param.37) | copy-start | bytes 24580
  7.3 13.1 %copy-start.16 = (s32[512]{0:T(512)S(1)}, s32[512]{0:T(512)}, u32[]{:S(2)}) copy-start(s32[512]{0:T(512)} %param.41) | copy-start | bytes 6148
  7.3 13.1 %copy-start.9 = (s32[2048]{0:T(1024)S(1)}, s32[2048]{0:T(1024)}, u32[]{:S(2)}) copy-start(s32[2048]{0:T(1024)} %param.43) | copy-start | bytes 24580
  7.3 13.1 %copy-start.4 = (s32[16384]{0:T(1024)S(1)}, s32[16384]{0:T(1024)}, u32[]{:S(2)}) copy-start(s32[16384]{0:T(1024)} %param.28) | copy-start | bytes 196612
  7.3 249.8 %all-reduce.2.cloned.1.call-start = ((), (), s32[]{:S(2)}) async-start(), calls=%async_computation | async-start | bytes 1048576 | tf_op jit(solution)/shard_map/psum | solution.py:195
  12.4 16.7 %collective-permute-start = (bf16[1024,128]{1,0:T(8,128)(2,1)S(1)}, bf16[1024,128]{1,0:T(8,128)(2,1)S(1)}, u32[]{:S(2)}, u32[]{:S(2)}) collective-permute-start(bf16[1024,128]{1,0:T(8,128)(2,1)S(1)} %gather_fusion), channel_id=1, source_target_pairs={{0,1},{1,2},{2,3},{3,4},{4,5},{5,6},{6,7},{7,8},{8,9},{9,10},{10,1... | collective-permute-start | bytes 786440 | tf_op jit(solution)/shard_map/ppermute | solution.py:17
  18.0 7.1 %copy-start.6 = (s32[4096]{0:T(1024)S(1)}, s32[4096]{0:T(1024)}, u32[]{:S(2)}) copy-start(s32[4096]{0:T(1024)} %param.34) | copy-start | bytes 49156
  18.0 8.7 %copy-start.10 = (s32[2048]{0:T(1024)S(1)}, s32[2048]{0:T(1024)}, u32[]{:S(2)}) copy-start(s32[2048]{0:T(1024)} %param.38) | copy-start | bytes 24580
  18.0 8.8 %copy-start.17 = (s32[512]{0:T(512)S(1)}, s32[512]{0:T(512)}, u32[]{:S(2)}) copy-start(s32[512]{0:T(512)} %param.40) | copy-start | bytes 6148
  18.1 11.1 %collective-permute-start.1 = (bf16[1024,128]{1,0:T(8,128)(2,1)S(1)}, bf16[1024,128]{1,0:T(8,128)(2,1)S(1)}, u32[]{:S(2)}, u32[]{:S(2)}) collective-permute-start(bf16[1024,128]{1,0:T(8,128)(2,1)S(1)} %gather_fusion.1), channel_id=1, source_target_pairs={{1,0},{2,1},{3,2},{4,3},{5,4},{6,5},{7,6},{8,7},{9,8},{10,9},{11,1... | collective-permute-start | bytes 786440 | tf_op jit(solution)/shard_map/ppermute | solution.py:19
  98.3 7.5 %copy-start.1 = (f32[16384,128]{1,0:T(8,128)S(1)}, f32[16384,128]{1,0:T(8,128)}, u32[]{:S(2)}) copy-start(f32[16384,128]{1,0:T(8,128)} %get-tuple-element.21) | copy-start | bytes 25165828
  123.6 11.1 %copy-start.2 = (bf16[4096,128]{0,1:T(8,128)(2,1)S(1)}, bf16[4096,128]{0,1:T(8,128)(2,1)}, u32[]{:S(2)}) copy-start(bf16[4096,128]{0,1:T(8,128)(2,1)} %add_convert_fusion) | copy-start | bytes 3145732
  126.6 10.5 %collective-permute-start.2 = (bf16[512,128]{1,0:T(8,128)(2,1)S(1)}, bf16[512,128]{1,0:T(8,128)(2,1)S(1)}, u32[]{:S(2)}, u32[]{:S(2)}) collective-permute-start(bf16[512,128]{1,0:T(8,128)(2,1)S(1)} %gather_fusion.3), channel_id=1, source_target_pairs={{0,1},{1,2},{2,3},{3,4},{4,5},{5,6},{6,7},{7,8},{8,9},{9,10},{10,1... | collective-permute-start | bytes 393224 | tf_op jit(solution)/shard_map/ppermute | solution.py:17
  133.4 4.5 %collective-permute-start.3 = (bf16[512,128]{1,0:T(8,128)(2,1)S(1)}, bf16[512,128]{1,0:T(8,128)(2,1)S(1)}, u32[]{:S(2)}, u32[]{:S(2)}) collective-permute-start(bf16[512,128]{1,0:T(8,128)(2,1)S(1)} %gather_fusion.4), channel_id=1, source_target_pairs={{1,0},{2,1},{3,2},{4,3},{5,4},{6,5},{7,6},{8,7},{9,8},{10,9},{11,1... | collective-permute-start | bytes 393224 | tf_op jit(solution)/shard_map/ppermute | solution.py:19
  139.3 7.9 %collective-permute-start.4 = (bf16[128,128]{1,0:T(8,128)(2,1)S(1)}, bf16[128,128]{1,0:T(8,128)(2,1)S(1)}, u32[]{:S(2)}, u32[]{:S(2)}) collective-permute-start(bf16[128,128]{1,0:T(8,128)(2,1)S(1)} %gather_fusion.5), channel_id=1, source_target_pairs={{0,1},{1,2},{2,3},{3,4},{4,5},{5,6},{6,7},{7,8},{8,9},{9,10},{10,1... | collective-permute-start | bytes 98312 | tf_op jit(solution)/shard_map/ppermute | solution.py:17
  145.5 3.1 %collective-permute-start.5 = (bf16[128,128]{1,0:T(8,128)(2,1)S(1)}, bf16[128,128]{1,0:T(8,128)(2,1)S(1)}, u32[]{:S(2)}, u32[]{:S(2)}) collective-permute-start(bf16[128,128]{1,0:T(8,128)(2,1)S(1)} %gather_fusion.6), channel_id=1, source_target_pairs={{1,0},{2,1},{3,2},{4,3},{5,4},{6,5},{7,6},{8,7},{9,8},{10,9},{11,1... | collective-permute-start | bytes 98312 | tf_op jit(solution)/shard_map/ppermute | solution.py:19
  158.1 37.4 %copy-start.11 = (s32[2048]{0:T(1024)S(1)}, s32[2048]{0:T(1024)}, u32[]{:S(2)}) copy-start(s32[2048]{0:T(1024)} %param.44) | copy-start | bytes 24580
  267.9 4.0 %copy-start.18 = (s32[512]{0:T(512)S(1)}, s32[512]{0:T(512)}, u32[]{:S(2)}) copy-start(s32[512]{0:T(512)} %param.40) | copy-start | bytes 6148
  267.9 4.0 %copy-start.20 = (f32[128]{0:T(128)S(1)}, f32[128]{0:T(128)}, u32[]{:S(2)}) copy-start(f32[128]{0:T(128)} %get-tuple-element.12) | copy-start | bytes 1540
  269.2 3.5 %copy-start.7 = (s32[4096]{0:T(1024)S(1)}, s32[4096]{0:T(1024)}, u32[]{:S(2)}) copy-start(s32[4096]{0:T(1024)} %param.34) | copy-start | bytes 49156
  272.7 3.5 %copy-start.21 = (bf16[512,128]{1,0:T(8,128)(2,1)}, bf16[512,128]{1,0:T(8,128)(2,1)S(1)}, u32[]{:S(2)}) copy-start(bf16[512,128]{1,0:T(8,128)(2,1)S(1)} %fusion.51) | copy-start | bytes 393220
Sparse Core Ops, SparseCore 0:
  162.2 94.8 all-reduce.1
where the time goes:
time: 284 us; the launch traced here: 283 us
  local copies, waits for them, and re-layouts  87.1 us (31%)
  waiting for transfers between devices  63.5 us (22%)
  matrix products  40.2 us (14%)
  blocking collectives  33.4 us (12%)
  other arithmetic  26.2 us (9%)
  starting transfers between devices  17 us (6%)
  between operations  15.5 us (5%)
    psum x1, waiting for transfers between devices, body(): summed_rows, summed_weight = lax.psum((top_sum, top_total), 'dom')  61.5 us
    gather x1, local copies, waits for them, and re-layouts, body(): extended[fine_sender]  57.4 us
    psum x1, blocking collectives, body(): summed_rows, summed_weight = lax.psum((top_sum, top_total), 'dom')  33.4 us
    dot_general x3, matrix products, graph_step(): jnp.dot(hidden, w_edge_out, preferred_element_type=jnp.float32)  15.6 us
    ppermute x3, starting transfers between devices, with_halo(): lax.ppermute(tail, axis, [(i, (i + 1) % count) for i in range(ends)])  13 us
    reduce_sum x6, other arithmetic, layer_norm(): spread = jnp.mean(centred * centred, axis=-1, keepdims=True)  9.57 us
    mul x1, other arithmetic, graph_step(): layer_norm(jnp.dot(hidden, w_edge_out, preferred_element_type=jnp.float32...  7.08 us
    dot_general x3, matrix products, graph_step(): jnp.einsum('tew,tel->twl', picks.astype(jnp.float32), message.reshape(til...  6.52 us
  transfers between devices with their start and end apart: 7, of which 3 were waited for; matrix products, arithmetic and copies ran while one was open for 6% of the time, Pallas kernels for 0%

commit v1 on v0

v1 whole, which is shorter than its diff:
```python
import functools

import jax
import jax.numpy as jnp
from jax import lax
from jax.experimental import pallas as pl
from jax.experimental.pallas import tpu as pltpu
from jax.sharding import PartitionSpec as P

epsilon = 1e-05
bf16 = jnp.bfloat16
f32 = jnp.float32
LANES = 128
GROUP = 4
VMEM_LIMIT = 52 * 2**20
whole_vmem = pl.BlockSpec(memory_space=pltpu.VMEM)
whole_smem = pl.BlockSpec(memory_space=pltpu.SMEM)
left_in_hbm = pl.BlockSpec(memory_space=pl.ANY)


def mm(a, b):
    return jnp.dot(a, b, preferred_element_type=f32)


def mm_first(a, b):
    return lax.dot_general(a, b, (((0,), (0,)), ((), ())), preferred_element_type=f32)


def gather_rows(index_ref, first, table_ref, into_ref, count, into_first=0):
    for j in range(count):
        into_ref[pl.ds(into_first + j, 1), :] = table_ref[pl.ds(index_ref[first + j], 1), :]


def match_rows(ids_row, count, weight_row=None):
    shape = (count, ids_row.shape[1])
    hit = lax.broadcasted_iota(jnp.int32, shape, 0) == ids_row
    if weight_row is None:
        return hit.astype(f32).astype(bf16)
    return jnp.where(hit, weight_row, 0.0).astype(bf16)


def side_by_side(rows):
    half = rows.shape[0] // 2
    return jnp.concatenate([rows[:half], rows[half:]], axis=1)


def normed_pairs(hidden, w_centred, spread_of):
    centred = mm(side_by_side(hidden), w_centred)
    spread = mm((centred * centred).astype(bf16), spread_of)
    return centred * lax.rsqrt(spread + epsilon)


def edge_sums(sender_part, receiver_part, edge_rows, picks, w_edge, w_out, spread_of):
    before = mm_first(picks, receiver_part) + mm(edge_rows, w_edge)
    hidden = jnp.maximum(before + sender_part, 0.0).astype(bf16)
    message = normed_pairs(hidden, w_out, spread_of).astype(bf16)
    half = edge_rows.shape[0] // 2
    return mm(picks[:, :half], message[:, :LANES]) + mm(picks[:, half:], message[:, LANES:])


def node_update(node_rows, summed, w_node, w_out, spread_of, gain):
    hidden = jnp.maximum(mm(jnp.concatenate([node_rows, summed], axis=1), w_node), 0.0)
    update = normed_pairs(hidden.astype(bf16), w_out, spread_of)
    update = jnp.concatenate([update[:, :LANES], update[:, LANES:]], axis=0)
    return (node_rows.astype(f32) + update * gain).astype(bf16)


def with_ones(rows):
    return jnp.concatenate([rows, jnp.ones(rows.shape, bf16)], axis=1)


def border_kernel(index_ref, x_ref, a_ref, b_ref, table, buffer):
    table[...] = x_ref[...].astype(f32)
    count = a_ref.shape[0]
    for side, out in enumerate((a_ref, b_ref)):
        gather_rows(index_ref, side * count, table, buffer, count)
        out[...] = buffer[...].astype(bf16)


def fill_tables(x_ref, place_ref, from_a, from_b, w_sr, table, receiver_part):
    count = x_ref.shape[0]
    border = from_a.shape[0]
    both = mm(x_ref[...], w_sr[...])
    table[:count, :] = both[:, :LANES]
    receiver_part[...] = both[:, LANES:].astype(bf16)
    w_s = w_sr[:, :LANES]
    at_a = pl.multiple_of(count + place_ref[0] * border, border)
    at_b = pl.multiple_of(count + (1 - place_ref[0]) * border, border)
    table[pl.ds(at_a, border), :] = mm(from_a[...], w_s)
    table[pl.ds(at_b, border), :] = mm(from_b[...], w_s) * place_ref[1].astype(f32)


def fine_kernel(
    place_ref, pool_index, sender_ref, edge_ref, x_ref, from_a, from_b, receiver_ref, parent_ref,
    weight_ref, w_sr, w_edge, w_out, w_node, w_node_out, spread_ref, gain_ref,
    new_ref, sums_ref, a_ref, b_ref,
    table, receiver_part, edges, gathered0, gathered1, aggregate, new32, buffer,
    index0, index1, index2, index3, edge_sem, index_sem,
):
    gathered = (gathered0, gathered1)
    indices = (index0, index1, index2, index3)
    block = gathered0.shape[0]
    groups, _, group_nodes = parent_ref.shape
    nodes = group_nodes // GROUP
    chunk = GROUP * block

    def edge_copy(g):
        at = pl.ds(pl.multiple_of(g * chunk, chunk), chunk)
        return pltpu.make_async_copy(edge_ref.at[at, :], edges.at[at, :], edge_sem.at[g])

    def index_copy(t, k):
        at = pl.ds(pl.multiple_of(t * block, block), block)
        return pltpu.make_async_copy(sender_ref.at[at], indices[k], index_sem.at[k])

    for k in range(GROUP):
        index_copy(k, k).start()
    for g in range(groups):
        edge_copy(g).start()
    fill_tables(x_ref, place_ref, from_a, from_b, w_sr, table, receiver_part)
    sums_ref[...] = jnp.zeros_like(sums_ref)
    index_copy(0, 0).wait()
    gather_rows(index0, 0, table, gathered0, block)

    def group_step(g, carry):
        edge_copy(g).wait()
        for k in range(GROUP):
            t = g * GROUP + k
            later = (k + 1) % GROUP
            index_copy(t + 1, later).wait()
            index_copy(t + GROUP, k).start()
            gather_rows(indices[later], 0, table, gathered[(k + 1) % 2], block)
            picks = match_rows(receiver_ref[t], nodes)
            summed = edge_sums(
                gathered[k % 2][...],
                receiver_part[pl.ds(pl.multiple_of(t * nodes, nodes), nodes), :],
                edges[pl.ds(pl.multiple_of(t * block, block), block), :],
                picks, w_edge[...], w_out[...], spread_ref[...],
            )
            aggregate[k * nodes : (k + 1) * nodes, :] = (summed * gain_ref[0:1, :]).astype(bf16)
        rows = pl.ds(pl.multiple_of(g * group_nodes, group_nodes), group_nodes)
        new_rows = node_update(
            x_ref[rows, :], aggregate[...], w_node[...], w_node_out[...], spread_ref[...],
            gain_ref[1:2, :],
        )
        new_ref[rows, :] = new_rows
        new32[rows, :] = new_rows.astype(f32)
        shares = match_rows(parent_ref[g], sums_ref.shape[0], weight_ref[g])
        sums_ref[...] += mm(shares, with_ones(new_rows))
        return carry

    lax.fori_loop(0, groups, group_step, 0)
    for k in range(1, GROUP):
        index_copy(groups * GROUP + k, k).wait()
    count = a_ref.shape[0]
    for side, out in enumerate((a_ref, b_ref)):
        gather_rows(pool_index, side * count, new32, buffer, count)
        out[...] = buffer[...].astype(bf16)


def pool_kernel(
    border_index, sums_ref, from_a, from_b, target_ref, weight_ref, coarse_ref, a_ref, b_ref, table, buffer
):
    count = sums_ref.shape[0]
    total = sums_ref[...]
    for side, rows in enumerate((from_a, from_b)):
        shares = match_rows(target_ref[side], count, weight_ref[side])
        total += mm(shares, with_ones(rows[...]))
    coarse = (total[:, :LANES] / total[:, LANES:]).astype(bf16)
    coarse_ref[...] = coarse
    table[...] = coarse.astype(f32)
    border = a_ref.shape[0]
    for side, out in enumerate((a_ref, b_ref)):
        gather_rows(border_index, side * border, table, buffer, border)
        out[...] = buffer[...].astype(bf16)


def coarse_kernel(
    place_ref, sender_ref, edge_ref, x_ref, from_a, from_b, receiver_ref, parent_ref, weight_ref,
    w_sr, w_edge, w_out, w_node, w_node_out, spread_ref, gain_ref,
    new_ref, own_ref, a_ref, b_ref,
    table, receiver_part, gathered, aggregate, shares_sum,
):
    blocks, _, block = receiver_ref.shape
    nodes = x_ref.shape[0] // blocks
    fill_tables(x_ref, place_ref, from_a, from_b, w_sr, table, receiver_part)
    for t in range(blocks):
        gather_rows(sender_ref, t * block, table, gathered, block, t * block)
    for t in range(blocks):
        picks = match_rows(receiver_ref[t], nodes)
        summed = edge_sums(
            gathered[t * block : (t + 1) * block, :],
            receiver_part[t * nodes : (t + 1) * nodes, :],
            edge_ref[t * block : (t + 1) * block, :],
            picks, w_edge[...], w_out[...], spread_ref[...],
        )
        aggregate[t * nodes : (t + 1) * nodes, :] = (summed * gain_ref[0:1, :]).astype(bf16)
    new_rows = node_update(
        x_ref[...], aggregate[...], w_node[...], w_node_out[...], spread_ref[...], gain_ref[1:2, :]
    )
    new_ref[...] = new_rows
    share = own_ref.shape[0]
    shares_sum[...] = mm(match_rows(parent_ref[...], 3 * share, weight_ref[...]), with_ones(new_rows))
    own_ref[...] = shares_sum[share : 2 * share, :]
    a_ref[...] = shares_sum[pl.ds(pl.multiple_of(2 * share * place_ref[0], share), share), :]
    b_ref[...] = shares_sum[pl.ds(pl.multiple_of(2 * share * (1 - place_ref[0]), share), share), :]


def top_kernel(
    place_ref, sender_ref, up_index, edge_ref, gathered_in, receiver_ref, parent_ref, coarse_ref,
    fine_ref, w_sr, w_edge, w_out, w_node, w_node_out, spread_ref, gain_ref,
    fine_out, coarse_out,
    table, top_rows, gathered, coarse32, lifted,
):
    share = receiver_ref.shape[1] // 6
    parts = gathered_in.shape[0] // share
    me = place_ref[0]
    nodes = 3 * share
    sender_part = mm(gathered_in[...], w_sr[:, :LANES])
    for q in range(parts):
        at = pl.multiple_of((q ^ me) * share, share)
        table[pl.ds(at, share), :] = sender_part[q * share : (q + 1) * share, :]
        top_rows[pl.ds(at, share), :] = gathered_in[q * share : (q + 1) * share, :]
    window = top_rows[pl.ds(pl.multiple_of(place_ref[1] * share, share), nodes), :]
    block = gathered.shape[0]
    gather_rows(sender_ref, 0, table, gathered, block)
    picks = match_rows(receiver_ref[...], nodes)
    summed = edge_sums(
        gathered[...], mm(window, w_sr[:, LANES:]).astype(bf16), edge_ref[...],
        picks, w_edge[...], w_out[...], spread_ref[...],
    )
    top_new = node_update(
        window, (summed * gain_ref[0:1, :]).astype(bf16), w_node[...], w_node_out[...],
        spread_ref[...], gain_ref[1:2, :],
    )
    up = mm_first(match_rows(parent_ref[...], nodes), top_new)
    coarse = (coarse_ref[...].astype(f32) + up).astype(bf16)
    coarse_out[...] = coarse
    coarse32[...] = coarse.astype(f32)
    step = lifted.shape[0]

    def lift(i, carry):
        gather_rows(up_index, i * step, coarse32, lifted, step)
        rows = pl.ds(pl.multiple_of(i * step, step), step)
        fine_out[rows, :] = (fine_ref[rows, :].astype(f32) + lifted[...]).astype(bf16)
        return carry

    lax.fori_loop(0, fine_ref.shape[0] // step, lift, 0)


def call(kernel, name, outs, specs, scratch, operands):
    return pl.pallas_call(
        kernel,
        name=name,
        out_shape=outs,
        in_specs=specs,
        out_specs=jax.tree.map(lambda _: whole_vmem, outs),
        scratch_shapes=scratch,
        compiler_params=pltpu.CompilerParams(vmem_limit_bytes=VMEM_LIMIT),
    )(*operands)


def rows_of(count, dtype=bf16, width=LANES):
    return jax.ShapeDtypeStruct((count, width), dtype)


def swap_with_neighbours(for_a, for_b):
    count = lax.axis_size("dom")
    pairs_a = [(i, i ^ 1) for i in range(count)]
    pairs_b = [(i, (i + 1) % count) for i in range(1, count, 2)]
    pairs_b += [(j, i) for i, j in pairs_b]
    return lax.ppermute(for_a, "dom", pairs_a), lax.ppermute(for_b, "dom", pairs_b)


def gather_all(rows):
    count = lax.axis_size("dom")
    steps = []
    stride = 1
    while stride < count:
        radix = 4 if stride * 4 <= count else 2
        steps.append((stride, radix))
        stride *= radix
    blocks = rows[None]
    for stride, radix in reversed(steps):
        taken = [blocks] + [
            lax.ppermute(blocks, "dom", [(i, i ^ (j * stride)) for i in range(count)])
            for j in range(1, radix)
        ]
        blocks = jnp.stack(taken, axis=1).reshape((-1,) + rows.shape)
    return blocks


def centred_pairs(weights):
    wide = weights.astype(f32)
    centred = (wide - jnp.mean(wide, axis=2, keepdims=True)).astype(bf16)
    blank = jnp.zeros_like(centred)
    return jnp.concatenate(
        [jnp.concatenate([centred, blank], axis=2), jnp.concatenate([blank, centred], axis=2)], axis=1
    )


def body(
    fine_latent, fine_edges, fine_sender, fine_receiver, edge_count, fine_border, pool_rows, pool_target,
    pool_weight, fine_parent, fine_weight, coarse_edges, coarse_sender, coarse_receiver, coarse_border,
    coarse_parent, coarse_weight, top_edges, top_sender, top_receiver, edge_in, edge_out, node_in, node_out,
    norm_gain,
):
    count = lax.axis_size("dom")
    me = lax.axis_index("dom").astype(jnp.int32)
    odd = me % 2
    inner = jnp.where((me == 0) | (me == count - 1), 0, 1).astype(jnp.int32)
    place = jnp.stack([1 - odd, inner])

    def by_partner(pair):
        return jnp.where(odd == 1, pair, pair[::-1])

    w_sr = jnp.concatenate([edge_in[:, :LANES], edge_in[:, LANES : 2 * LANES]], axis=2)
    w_edge = edge_in[:, 2 * LANES :]
    w_out = centred_pairs(edge_out)
    w_node_out = centred_pairs(node_out)
    lane = jnp.arange(2 * LANES, dtype=jnp.int32) // LANES
    spread_of = jnp.where(lane[:, None] == lane[None, :], 1.0 / LANES, 0.0).astype(bf16)

    def weights_of(level):
        return (
            w_sr[level], w_edge[level], w_out[level], node_in[level], w_node_out[level], spread_of,
            norm_gain[level],
        )

    fine_total = fine_latent.shape[0]
    edge_total = fine_sender.shape[0]
    coarse_total = coarse_parent.shape[0]
    border = fine_border.shape[2]
    slots = pool_rows.shape[2]

    with jax.named_scope("fine_border_rows"):
        for_a, for_b = call(
            border_kernel, "border_rows", [rows_of(border), rows_of(border)], [whole_smem, whole_vmem],
            [pltpu.VMEM((fine_total, LANES), f32), pltpu.VMEM((border, LANES), f32)],
            (by_partner(fine_border[0]).reshape(-1), fine_latent),
        )
        from_a, from_b = swap_with_neighbours(for_a, for_b)

    with jax.named_scope("fine_step"):
        nodes = LANES
        block = nodes * edge_total // fine_total
        blocks = edge_total // block
        groups = blocks // GROUP
        slot = jnp.arange(edge_total, dtype=jnp.int32)
        receiver = jnp.where(slot < edge_count[0], fine_receiver - slot // block * nodes, -1)
        sender = jnp.concatenate([fine_sender, jnp.zeros((GROUP * block,), jnp.int32)])
        fine_new, local_sums, for_a, for_b = call(
            fine_kernel, "fine_step",
            [rows_of(fine_total), rows_of(coarse_total, f32, 2 * LANES), rows_of(slots), rows_of(slots)],
            [whole_smem, whole_smem, left_in_hbm, left_in_hbm] + [whole_vmem] * 13,
            [
                pltpu.VMEM((fine_total + 2 * border, LANES), f32),
                pltpu.VMEM((fine_total, LANES), bf16),
                pltpu.VMEM((edge_total, LANES), bf16),
                pltpu.VMEM((block, LANES), f32),
                pltpu.VMEM((block, LANES), f32),
                pltpu.VMEM((GROUP * nodes, LANES), bf16),
                pltpu.VMEM((fine_total, LANES), f32),
                pltpu.VMEM((slots, LANES), f32),
            ]
            + [pltpu.SMEM((block,), jnp.int32)] * GROUP
            + [pltpu.SemaphoreType.DMA((groups,)), pltpu.SemaphoreType.DMA((GROUP,))],
            (
                place, by_partner(pool_rows[0]).reshape(-1), sender, fine_edges, fine_latent, from_a, from_b,
                receiver.reshape(blocks, 1, block), fine_parent.reshape(groups, 1, GROUP * nodes),
                fine_weight.astype(f32).reshape(groups, 1, GROUP * nodes),
            )
            + weights_of(0),
        )
        from_a, from_b = swap_with_neighbours(for_a, for_b)

    with jax.named_scope("coarse_input"):
        border1 = coarse_border.shape[2]
        coarse_in, for_a, for_b = call(
            pool_kernel, "coarse_input",
            [rows_of(coarse_total), rows_of(border1), rows_of(border1)],
            [whole_smem] + [whole_vmem] * 5,
            [pltpu.VMEM((coarse_total, LANES), f32), pltpu.VMEM((border1, LANES), f32)],
            (
                by_partner(coarse_border[0]).reshape(-1), local_sums, from_a, from_b,
                by_partner(pool_target[0])[:, None, :], by_partner(pool_weight[0]).astype(f32)[:, None, :],
            ),
        )
        from_a, from_b = swap_with_neighbours(for_a, for_b)

    with jax.named_scope("coarse_step"):
        edge_total1 = coarse_sender.shape[0]
        block1 = LANES * edge_total1 // coarse_total
        blocks1 = edge_total1 // block1
        share = coarse_total // 8
        slot1 = jnp.arange(edge_total1, dtype=jnp.int32)
        coarse_new, own, for_a, for_b = call(
            coarse_kernel, "coarse_step",
            [rows_of(coarse_total)] + [rows_of(share, f32, 2 * LANES)] * 3,
            [whole_smem, whole_smem] + [whole_vmem] * 14,
            [
                pltpu.VMEM((coarse_total + 2 * border1, LANES), f32),
                pltpu.VMEM((coarse_total, LANES), bf16),
                pltpu.VMEM((edge_total1, LANES), f32),
                pltpu.VMEM((coarse_total, LANES), bf16),
                pltpu.VMEM((3 * share, 2 * LANES), f32),
            ],
            (
                place, coarse_sender, coarse_edges, coarse_in, from_a, from_b,
                (coarse_receiver - slot1 // block1 * LANES).reshape(blocks1, 1, block1),
                (coarse_parent - (me - 1) * share)[None, :], coarse_weight.astype(f32)[None, :],
            )
            + weights_of(1),
        )
        from_a, from_b = swap_with_neighbours(for_a, for_b)
        shares = own + from_a + from_b
        top_in = (shares[:, :LANES] / shares[:, LANES:]).astype(bf16)

    with jax.named_scope("top_step"):
        everyone = gather_all(top_in).reshape(count * share, LANES)
        first = jnp.clip(me - 1, 0, count - 3)
        tile = 2 * share
        window = 3 * tile
        top_window = [
            lax.dynamic_slice_in_dim(a, first * tile, window, axis=0)
            for a in (top_edges, top_sender, top_receiver)
        ]
        step = 512
        fine_out, coarse_out = call(
            top_kernel, "top_step",
            [rows_of(fine_total), rows_of(coarse_total)],
            [whole_smem] * 3 + [whole_vmem] * 13,
            [
                pltpu.VMEM((count * share, LANES), f32),
                pltpu.VMEM((count * share, LANES), bf16),
                pltpu.VMEM((window, LANES), f32),
                pltpu.VMEM((coarse_total, LANES), f32),
                pltpu.VMEM((step, LANES), f32),
            ],
            (
                jnp.stack([me, first]), top_window[1], fine_parent, top_window[0], everyone,
                (top_window[2] - first * share)[None, :], (coarse_parent - first * share)[None, :], coarse_new,
                fine_new,
            )
            + weights_of(2),
        )
    return (fine_out, coarse_out)


def solution(mesh):
    row = ("groups", "dom")
    return jax.shard_map(
        body,
        mesh=mesh,
        in_specs=(
            P(row, None), P(row, None), P(row), P(row), P(row), P(row, None, None), P(row, None, None),
            P(row, None, None), P(row, None, None), P(row), P(row), P(row, None), P(row), P(row),
            P(row, None, None), P(row), P(row), P("groups", None), P("groups"), P("groups"), P(), P(), P(), P(),
            P(),
        ),
        out_specs=(P(row, None), P(row, None)),
        check_vma=False,
    )
```

time: 284 us -> 114 us (0.40)
  local copies, waits for them, and re-layouts: 87.1 us -> 13.8 us
  Pallas kernels: 0 us -> 52 us
  waiting for transfers between devices: 63.5 us -> 21.9 us
  matrix products: 40.2 us -> 0 us
  blocking collectives: 33.4 us -> 0 us
  other arithmetic: 26.2 us -> 8.76 us
  between operations: 15.5 us -> 1.67 us
    gather x9 -> x0, local copies, waits for them, and re-layouts: 81.8 us -> none  [the longest x1 57.4 us: body(): extended[fine_sender]]
    psum x1 -> x0, waiting for transfers between devices: 61.5 us -> none  [body(): summed_rows, summed_weight = lax.psum((top_sum, top_total), 'dom')]
    pallas_call x0 -> x5, Pallas kernels: none -> 52 us  [call(): pl.pallas_call(kernel, name=name, out_shape=outs, in_specs=specs, out_spe...]
    dot_general x17 -> x0, matrix products: 40.2 us -> none  [the longest x3 15.6 us: graph_step(): jnp.dot(hidden, w_edge_out, preferred_element_type=jnp.float32)]
    psum x1 -> x0, blocking collectives: 33.4 us -> none  [body(): summed_rows, summed_weight = lax.psum((top_sum, top_total), 'dom')]
    ppermute x6 -> x14, waiting for transfers between devices: 2.04 us -> 21.9 us  [the longest x4 15.1 us: swap_with_neighbours(): lax.ppermute(for_b, 'dom', pairs_b)]
    reduce_sum x9 -> x2, other arithmetic: 11.8 us -> 1.99 us  [centred_pairs(): centred = (wide - jnp.mean(wide, axis=2, keepdims=True)).astype(bf16)]
    mul x6 -> x0, other arithmetic: 8.98 us -> none  [the longest x1 7.08 us: graph_step(): layer_norm(jnp.dot(hidden, w_edge_out, preferred_element_type=jnp.float32...]
  transfers between devices with their start and end apart: 7 -> 14, of which waited for: 3 -> 9; matrix products, arithmetic and copies ran while one was open for 6% -> 15% of each run, Pallas kernels for 0% -> 0%
where the time goes in v1:
time: 114 us; the launch traced here: 113 us
  Pallas kernels  52 us (46%)
  waiting for transfers between devices  21.9 us (19%)
  starting transfers between devices  14.6 us (13%)
  local copies, waits for them, and re-layouts  13.8 us (12%)
  other arithmetic  8.76 us (8%)
  between operations  1.67 us (1%)
    pallas_call x5, Pallas kernels, call(): pl.pallas_call(kernel, name=name, out_shape=outs, in_specs=specs, out_spe...  52 us
    ppermute x4, waiting for transfers between devices, swap_with_neighbours(): lax.ppermute(for_b, 'dom', pairs_b)  15.1 us
    ppermute x4, starting transfers between devices, swap_with_neighbours(): lax.ppermute(for_b, 'dom', pairs_b)  7.49 us
    rev x5, local copies, waits for them, and re-layouts, by_partner(): return jnp.where(odd == 1, pair, pair[::-1])  7.21 us
    ppermute x6, starting transfers between devices, gather_all(): lax.ppermute(blocks, 'dom', [(i, i ^ j * stride) for i in range(count)])  6.36 us
    ppermute x6, waiting for transfers between devices, gather_all(): lax.ppermute(blocks, 'dom', [(i, i ^ j * stride) for i in range(count)])  5.38 us
    unnamed x26, local copies, waits for them, and re-layouts  2.32 us
  transfers between devices with their start and end apart: 14, of which 9 were waited for; matrix products, arithmetic and copies ran while one was open for 15% of the time, Pallas kernels for 0%

profile of v1, /device:TPU:0, one launch (start us, length us, event | category | flops | bytes accessed | tf_op | source)
XLA Modules:
  0.0 112.7 jit_solution(13057325743892286870)
XLA Ops:
  0.7 2.9 %rev.17 = s32[2,1024]{1,0:T(2,128)S(1)} reverse(s32[2,1024]{1,0:T(2,128)} %bitcast.99), dimensions={0} | reverse | bytes 16384 | tf_op jit(solution)/shard_map/fine_border_rows/rev | solution.py:314
  3.6 0.7 select_bitcast_fusion
  4.3 1.2 %copy-done.1 = bf16[4096,128]{1,0:T(8,128)(2,1)S(1)} copy-done((bf16[4096,128]{1,0:T(8,128)(2,1)S(1)}, bf16[4096,128]{1,0:T(8,128)(2,1)}, u32[]{:S(2)}) %copy-start.1) | copy-done | bytes 1048600
  5.5 1.9 %border_rows.1 = (bf16[1024,128]{1,0:T(8,128)(2,1)S(1)}, bf16[1024,128]{1,0:T(8,128)(2,1)S(1)}) custom-call(s32[2048]{0:T(1024)S(1)} %bitcast.91, bf16[4096,128]{1,0:T(8,128)(2,1)S(1)} %copy-done.1), custom_call_target="tpu_custom_call" | custom-call | tf_op jit(solution)/shard_map/fine_border_rows/border_rows/pallas_call | solution.py:251
  8.0 5.7 %collective-permute-start.1 = (bf16[1024,128]{1,0:T(8,128)(2,1)S(1)}, bf16[1024,128]{1,0:T(8,128)(2,1)S(1)}, u32[]{:S(2)}, u32[]{:S(2)}) collective-permute-start(bf16[1024,128]{1,0:T(8,128)(2,1)S(1)} %get-tuple-element.16), channel_id=1, source_target_pairs={{1,2},{3,4},{5,6},{7,8},{9,10},{11,12},{13,14},{15,0},{2,1},{4,3},... | collective-permute-start | bytes 786440 | tf_op jit(solution)/shard_map/fine_border_rows/ppermute | solution.py:271
  13.7 1.0 fusion.27
  14.6 0.8 slice_bitcast_fusion.9
  15.4 1.4 %rev.16 = s32[2,512]{1,0:T(2,128)S(1)} reverse(s32[2,512]{1,0:T(2,128)} %bitcast.103), dimensions={0} | reverse | bytes 8192 | tf_op jit(solution)/shard_map/fine_step/rev | solution.py:314
  17.6 1.0 convert_reduce_fusion.1
  18.6 1.0 fusion.6
  19.6 1.0 convert_reduce_fusion
  20.6 1.0 fusion.7
  21.7 0.9 slice_bitcast_fusion.6
  22.7 0.7 slice_bitcast_fusion.12
  24.1 1.4 %rev.19 = s32[2,512]{1,0:T(2,128)S(1)} reverse(s32[2,512]{1,0:T(2,128)} %bitcast.104), dimensions={0} | reverse | bytes 8192 | tf_op jit(solution)/shard_map/coarse_input/rev | solution.py:314
  26.2 1.4 %rev.18 = s32[2,512]{1,0:T(2,128)S(1)} reverse(s32[2,512]{1,0:T(2,128)} %bitcast.105), dimensions={0} | reverse | bytes 8192 | tf_op jit(solution)/shard_map/coarse_input/rev | solution.py:314
  28.3 0.7 fusion.23
  29.4 37.4 %fine_step.1 = (bf16[4096,128]{1,0:T(8,128)(2,1)}, f32[512,256]{1,0:T(8,128)}, bf16[512,128]{1,0:T(8,128)(2,1)S(1)}, bf16[512,128]{1,0:T(8,128)(2,1)S(1)}) custom-call(s32[2]{0:T(128)S(1)} %pad_add_fusion.1.place_ref, s32[1024]{0:T(1024)S(1)} %bitcast.92, s32[18432]{0:T(1024)S(1)} %concatenate.24.sender_ref, bf16[16384,128]{1,0:T(8,128)(2,1)} %edge_ref.2, ...), custom_call_target="tpu_custom_call" | custom-call | tf_op jit(solution)/shard_map/fine_step/fine_step/pallas_call | solution.py:251
  67.6 0.7 collective-permute-done.2.from_a
  68.3 5.8 %collective-permute-done.3.from_b = bf16[512,128]{1,0:T(8,128)(2,1)S(1)} collective-permute-done((bf16[512,128]{1,0:T(8,128)(2,1)S(1)}, bf16[512,128]{1,0:T(8,128)(2,1)S(1)}, u32[]{:S(2)}, u32[]{:S(2)}) %collective-permute-start.3) | collective-permute-done | bytes 131104 | tf_op jit(solution)/shard_map/fine_step/ppermute | solution.py:271
  74.1 1.0 copy-done.2
  75.2 1.2 %coarse_input.1 = (bf16[512,128]{1,0:T(8,128)(2,1)S(1)}, bf16[128,128]{1,0:T(8,128)(2,1)S(1)}, bf16[128,128]{1,0:T(8,128)(2,1)S(1)}) custom-call(s32[256]{0:T(256)S(1)} %select_bitcast_fusion.3.border_index, f32[512,256]{1,0:T(8,128)S(1)} %copy-done.2, bf16[512,128]{1,0:T(8,128)(2,1)S(1)} %collective-permute-done.2.from_a, ...), custom_call_target="tpu_custom_call" | custom-call | tf_op jit(solution)/shard_map/coarse_input/coarse_input/pallas_call | solution.py:251
  77.0 0.8 dynamic-slice_subtract_fusion
  77.8 0.8 dynamic_slice.9.sender_ref
  78.6 3.9 %collective-permute-done.5.from_b = bf16[128,128]{1,0:T(8,128)(2,1)S(1)} collective-permute-done((bf16[128,128]{1,0:T(8,128)(2,1)S(1)}, bf16[128,128]{1,0:T(8,128)(2,1)S(1)}, u32[]{:S(2)}, u32[]{:S(2)}) %collective-permute-start.5) | collective-permute-done | bytes 32800 | tf_op jit(solution)/shard_map/coarse_input/ppermute | solution.py:271
  82.5 4.0 %coarse_step.1 = (bf16[512,128]{1,0:T(8,128)(2,1)S(1)}, f32[64,256]{1,0:T(8,128)S(1)}, f32[64,256]{1,0:T(8,128)S(1)}, f32[64,256]{1,0:T(8,128)S(1)}) custom-call(s32[2]{0:T(128)S(1)} %pad_add_fusion.1.place_ref, s32[2048]{0:T(1024)S(1)} %copy-done.5, bf16[2048,128]{1,0:T(8,128)(2,1)S(1)} %copy-done.3, bf16[512,128]{1,0:T(8,128)(2,1)S(1)} %get-tuple-element.20.x_ref, ...), custom_call_target="tpu_custom_call" | custom-call | tf_op jit(solution)/shard_map/coarse_step/coarse_step/pallas_call | solution.py:251
  87.9 5.4 %collective-permute-done.7 = f32[64,256]{1,0:T(8,128)S(1)} collective-permute-done((f32[64,256]{1,0:T(8,128)S(1)}, f32[64,256]{1,0:T(8,128)S(1)}, u32[]{:S(2)}, u32[]{:S(2)}) %collective-permute-start.7) | collective-permute-done | bytes 65568 | tf_op jit(solution)/shard_map/coarse_step/ppermute | solution.py:271
  93.4 4.3 %collective-permute-start.10 = (bf16[1,64,128]{2,1,0:T(8,128)(2,1)S(1)}, bf16[1,64,128]{2,1,0:T(8,128)(2,1)S(1)}, u32[]{:S(2)}, u32[]{:S(2)}) collective-permute-start(bf16[1,64,128]{2,1,0:T(8,128)(2,1)S(1)} %fusion.29), channel_id=1, source_target_pairs={{0,12},{1,13},{2,14},{3,15},{4,8},{5,9},{6,10},{7,11},{8,4},{9,5},... | collective-permute-start | bytes 49160 | tf_op jit(solution)/shard_map/top_step/ppermute | solution.py:285
  98.1 1.6 %collective-permute-done.10 = bf16[1,64,128]{2,1,0:T(8,128)(2,1)S(1)} collective-permute-done((bf16[1,64,128]{2,1,0:T(8,128)(2,1)S(1)}, bf16[1,64,128]{2,1,0:T(8,128)(2,1)S(1)}, u32[]{:S(2)}, u32[]{:S(2)}) %collective-permute-start.10) | collective-permute-done | bytes 16416 | tf_op jit(solution)/shard_map/top_step/ppermute | solution.py:285
  99.8 1.8 %collective-permute-start.13 = (bf16[4,64,128]{2,1,0:T(8,128)(2,1)S(1)}, bf16[4,64,128]{2,1,0:T(8,128)(2,1)S(1)}, u32[]{:S(2)}, u32[]{:S(2)}) collective-permute-start(bf16[4,64,128]{2,1,0:T(8,128)(2,1)S(1)} %get-tuple-element.46), channel_id=1, source_target_pairs={{0,3},{1,2},{2,1},{3,0},{4,7},{5,6},{6,5},{7,4},{8,11},{9,10},{10,... | collective-permute-start | bytes 196616 | tf_op jit(solution)/shard_map/top_step/ppermute | solution.py:285
  101.7 3.0 %collective-permute-done.12 = bf16[4,64,128]{2,1,0:T(8,128)(2,1)S(1)} collective-permute-done((bf16[4,64,128]{2,1,0:T(8,128)(2,1)S(1)}, bf16[4,64,128]{2,1,0:T(8,128)(2,1)S(1)}, u32[]{:S(2)}, u32[]{:S(2)}) %collective-permute-start.12) | collective-permute-done | bytes 65568 | tf_op jit(solution)/shard_map/top_step/ppermute | solution.py:285
  105.2 7.4 %top_step.1 = (bf16[4096,128]{1,0:T(8,128)(2,1)}, bf16[512,128]{1,0:T(8,128)(2,1)}) custom-call(s32[2]{0:T(128)S(1)} %pad_add_fusion.place_ref, s32[384]{0:T(512)S(1)} %dynamic_slice.9.sender_ref, s32[4096]{0:T(1024)S(1)} %copy-done.4, bf16[384,128]{1,0:T(8,128)(2,1)S(1)} %constant_dynamic-slice_fusion.edge_ref, bf16[1024,128]{1,0:T(8,128)(2,1)S(1)} %bitcast.86, ...), custom_call_target="tpu_custom_call" | custom-call | tf_op jit(solution)/shard_map/top_step/top_step/pallas_call | solution.py:251
  (73 shorter events, 7.0 us)
Async XLA Ops:
  0.6 86.6 %copy-start = (bf16[2048,128]{1,0:T(8,128)(2,1)S(1)}, bf16[2048,128]{1,0:T(8,128)(2,1)}, u32[]{:S(2)}) copy-start(bf16[2048,128]{1,0:T(8,128)(2,1)} %param.42) | copy-start | bytes 1572868
  0.6 28.4 %copy-start.6 = (s32[16384]{0:T(1024)S(1)}, s32[16384]{0:T(1024)}, u32[]{:S(2)}) copy-start(s32[16384]{0:T(1024)} %param.28) | copy-start | bytes 196612
  0.7 28.5 %copy-start.10 = (s32[512]{0:T(512)S(1)}, s32[512]{0:T(512)}, u32[]{:S(2)}) copy-start(s32[512]{0:T(512)} %param.40) | copy-start | bytes 6148
  0.7 28.6 %copy-start.9 = (s32[1,2,128]{2,1,0:T(2,128)S(1)}, s32[1,2,128]{2,1,0:T(2,128)}, u32[]{:S(2)}) copy-start(s32[1,2,128]{2,1,0:T(2,128)} %param.39) | copy-start | bytes 3076
  0.7 28.7 %copy-start.4 = (s32[4096]{0:T(1024)S(1)}, s32[4096]{0:T(1024)}, u32[]{:S(2)}) copy-start(s32[4096]{0:T(1024)} %up_index.1) | copy-start | bytes 49156
  4.3 1.2 %copy-start.1 = (bf16[4096,128]{1,0:T(8,128)(2,1)S(1)}, bf16[4096,128]{1,0:T(8,128)(2,1)}, u32[]{:S(2)}) copy-start(bf16[4096,128]{1,0:T(8,128)(2,1)} %x_ref.3) | copy-start | bytes 3145732
  5.5 23.7 %copy-start.7 = (s32[16384]{0:T(1024)S(1)}, s32[16384]{0:T(1024)}, u32[]{:S(2)}) copy-start(s32[16384]{0:T(1024)} %param.27) | copy-start | bytes 196612
  5.5 23.7 %copy-start.8 = (s32[4096]{0:T(1024)S(1)}, s32[4096]{0:T(1024)}, u32[]{:S(2)}) copy-start(s32[4096]{0:T(1024)} %param.35) | copy-start | bytes 49156
  7.5 21.9 %collective-permute-start = (bf16[1024,128]{1,0:T(8,128)(2,1)S(1)}, bf16[1024,128]{1,0:T(8,128)(2,1)S(1)}, u32[]{:S(2)}, u32[]{:S(2)}) collective-permute-start(bf16[1024,128]{1,0:T(8,128)(2,1)S(1)} %get-tuple-element.15), channel_id=1, source_target_pairs={{0,1},{1,0},{2,3},{3,2},{4,5},{5,4},{6,7},{7,6},{8,9},{9,8},{10,11... | collective-permute-start | bytes 786440 | tf_op jit(solution)/shard_map/fine_border_rows/ppermute | solution.py:271
  8.0 21.4 %collective-permute-start.1 = (bf16[1024,128]{1,0:T(8,128)(2,1)S(1)}, bf16[1024,128]{1,0:T(8,128)(2,1)S(1)}, u32[]{:S(2)}, u32[]{:S(2)}) collective-permute-start(bf16[1024,128]{1,0:T(8,128)(2,1)S(1)} %get-tuple-element.16), channel_id=1, source_target_pairs={{1,2},{3,4},{5,6},{7,8},{9,10},{11,12},{13,14},{15,0},{2,1},{4,3},... | collective-permute-start | bytes 786440 | tf_op jit(solution)/shard_map/fine_border_rows/ppermute | solution.py:271
  29.3 48.5 %copy-start.11 = (s32[512]{0:T(512)S(1)}, s32[512]{0:T(512)}, u32[]{:S(2)}) copy-start(s32[512]{0:T(512)} %param.41) | copy-start | bytes 6148
  29.3 53.2 %copy-start.3 = (bf16[2048,128]{1,0:T(8,128)(2,1)S(1)}, bf16[2048,128]{1,0:T(8,128)(2,1)}, u32[]{:S(2)}) copy-start(bf16[2048,128]{1,0:T(8,128)(2,1)} %edge_ref.3) | copy-start | bytes 1572868
  29.3 53.2 %copy-start.5 = (s32[2048]{0:T(1024)S(1)}, s32[2048]{0:T(1024)}, u32[]{:S(2)}) copy-start(s32[2048]{0:T(1024)} %sender_ref.1) | copy-start | bytes 24580
  66.9 1.4 %collective-permute-start.2 = (bf16[512,128]{1,0:T(8,128)(2,1)S(1)}, bf16[512,128]{1,0:T(8,128)(2,1)S(1)}, u32[]{:S(2)}, u32[]{:S(2)}) collective-permute-start(bf16[512,128]{1,0:T(8,128)(2,1)S(1)} %get-tuple-element.18), channel_id=1, source_target_pairs={{0,1},{1,0},{2,3},{3,2},{4,5},{5,4},{6,7},{7,6},{8,9},{9,8},{10,11... | collective-permute-start | bytes 393224 | tf_op jit(solution)/shard_map/fine_step/ppermute | solution.py:271
  67.0 7.2 %collective-permute-start.3 = (bf16[512,128]{1,0:T(8,128)(2,1)S(1)}, bf16[512,128]{1,0:T(8,128)(2,1)S(1)}, u32[]{:S(2)}, u32[]{:S(2)}) collective-permute-start(bf16[512,128]{1,0:T(8,128)(2,1)S(1)} %get-tuple-element.19), channel_id=1, source_target_pairs={{1,2},{3,4},{5,6},{7,8},{9,10},{11,12},{13,14},{15,0},{2,1},{4,3},... | collective-permute-start | bytes 393224 | tf_op jit(solution)/shard_map/fine_step/ppermute | solution.py:271
  74.1 1.0 copy-start.2
  76.3 2.2 %collective-permute-start.4 = (bf16[128,128]{1,0:T(8,128)(2,1)S(1)}, bf16[128,128]{1,0:T(8,128)(2,1)S(1)}, u32[]{:S(2)}, u32[]{:S(2)}) collective-permute-start(bf16[128,128]{1,0:T(8,128)(2,1)S(1)} %get-tuple-element.21), channel_id=1, source_target_pairs={{0,1},{1,0},{2,3},{3,2},{4,5},{5,4},{6,7},{7,6},{8,9},{9,8},{10,11... | collective-permute-start | bytes 98312 | tf_op jit(solution)/shard_map/coarse_input/ppermute | solution.py:271
  76.4 6.1 %collective-permute-start.5 = (bf16[128,128]{1,0:T(8,128)(2,1)S(1)}, bf16[128,128]{1,0:T(8,128)(2,1)S(1)}, u32[]{:S(2)}, u32[]{:S(2)}) collective-permute-start(bf16[128,128]{1,0:T(8,128)(2,1)S(1)} %get-tuple-element.22), channel_id=1, source_target_pairs={{1,2},{3,4},{5,6},{7,8},{9,10},{11,12},{13,14},{15,0},{2,1},{4,3},... | collective-permute-start | bytes 98312 | tf_op jit(solution)/shard_map/coarse_input/ppermute | solution.py:271
  86.5 1.3 %collective-permute-start.6 = (f32[64,256]{1,0:T(8,128)S(1)}, f32[64,256]{1,0:T(8,128)S(1)}, u32[]{:S(2)}, u32[]{:S(2)}) collective-permute-start(f32[64,256]{1,0:T(8,128)S(1)} %get-tuple-element.24), channel_id=1, source_target_pairs={{0,1},{1,0},{2,3},{3,2},{4,5},{5,4},{6,7},{7,6},{8,9},{9,8},{10,11... | collective-permute-start | bytes 196616 | tf_op jit(solution)/shard_map/coarse_step/ppermute | solution.py:271
  86.6 6.6 %collective-permute-start.7 = (f32[64,256]{1,0:T(8,128)S(1)}, f32[64,256]{1,0:T(8,128)S(1)}, u32[]{:S(2)}, u32[]{:S(2)}) collective-permute-start(f32[64,256]{1,0:T(8,128)S(1)} %get-tuple-element.25), channel_id=1, source_target_pairs={{1,2},{3,4},{5,6},{7,8},{9,10},{11,12},{13,14},{15,0},{2,1},{4,3},... | collective-permute-start | bytes 196616 | tf_op jit(solution)/shard_map/coarse_step/ppermute | solution.py:271
  93.3 4.5 %collective-permute-start.8 = (bf16[1,64,128]{2,1,0:T(8,128)(2,1)S(1)}, bf16[1,64,128]{2,1,0:T(8,128)(2,1)S(1)}, u32[]{:S(2)}, u32[]{:S(2)}) collective-permute-start(bf16[1,64,128]{2,1,0:T(8,128)(2,1)S(1)} %fusion.29), channel_id=1, source_target_pairs={{0,4},{1,5},{2,6},{3,7},{4,0},{5,1},{6,2},{7,3},{8,12},{9,13},{10,... | collective-permute-start | bytes 49160 | tf_op jit(solution)/shard_map/top_step/ppermute | solution.py:285
  93.4 4.7 %collective-permute-start.9 = (bf16[1,64,128]{2,1,0:T(8,128)(2,1)S(1)}, bf16[1,64,128]{2,1,0:T(8,128)(2,1)S(1)}, u32[]{:S(2)}, u32[]{:S(2)}) collective-permute-start(bf16[1,64,128]{2,1,0:T(8,128)(2,1)S(1)} %fusion.29), channel_id=1, source_target_pairs={{0,8},{1,9},{2,10},{3,11},{4,12},{5,13},{6,14},{7,15},{8,0},{9,1},... | collective-permute-start | bytes 49160 | tf_op jit(solution)/shard_map/top_step/ppermute | solution.py:285
  93.4 6.2 %collective-permute-start.10 = (bf16[1,64,128]{2,1,0:T(8,128)(2,1)S(1)}, bf16[1,64,128]{2,1,0:T(8,128)(2,1)S(1)}, u32[]{:S(2)}, u32[]{:S(2)}) collective-permute-start(bf16[1,64,128]{2,1,0:T(8,128)(2,1)S(1)} %fusion.29), channel_id=1, source_target_pairs={{0,12},{1,13},{2,14},{3,15},{4,8},{5,9},{6,10},{7,11},{8,4},{9,5},... | collective-permute-start | bytes 49160 | tf_op jit(solution)/shard_map/top_step/ppermute | solution.py:285
  99.6 2.0 %collective-permute-start.11 = (bf16[4,64,128]{2,1,0:T(8,128)(2,1)S(1)}, bf16[4,64,128]{2,1,0:T(8,128)(2,1)S(1)}, u32[]{:S(2)}, u32[]{:S(2)}) collective-permute-start(bf16[4,64,128]{2,1,0:T(8,128)(2,1)S(1)} %get-tuple-element.46), channel_id=1, source_target_pairs={{0,1},{1,0},{2,3},{3,2},{4,5},{5,4},{6,7},{7,6},{8,9},{9,8},{10,11... | collective-permute-start | bytes 196616 | tf_op jit(solution)/shard_map/top_step/ppermute | solution.py:285
  99.7 5.0 %collective-permute-start.12 = (bf16[4,64,128]{2,1,0:T(8,128)(2,1)S(1)}, bf16[4,64,128]{2,1,0:T(8,128)(2,1)S(1)}, u32[]{:S(2)}, u32[]{:S(2)}) collective-permute-start(bf16[4,64,128]{2,1,0:T(8,128)(2,1)S(1)} %get-tuple-element.46), channel_id=1, source_target_pairs={{0,2},{1,3},{2,0},{3,1},{4,6},{5,7},{6,4},{7,5},{8,10},{9,11},{10,... | collective-permute-start | bytes 196616 | tf_op jit(solution)/shard_map/top_step/ppermute | solution.py:285
  99.8 5.4 %collective-permute-start.13 = (bf16[4,64,128]{2,1,0:T(8,128)(2,1)S(1)}, bf16[4,64,128]{2,1,0:T(8,128)(2,1)S(1)}, u32[]{:S(2)}, u32[]{:S(2)}) collective-permute-start(bf16[4,64,128]{2,1,0:T(8,128)(2,1)S(1)} %get-tuple-element.46), channel_id=1, source_target_pairs={{0,3},{1,2},{2,1},{3,0},{4,7},{5,6},{6,5},{7,4},{8,11},{9,10},{10,... | collective-permute-start | bytes 196616 | tf_op jit(solution)/shard_map/top_step/ppermute | solution.py:285

commit v2 on v1

v2 whole, which is shorter than its diff:
```python
import functools

import jax
import jax.numpy as jnp
from jax import lax
from jax.experimental import pallas as pl
from jax.experimental.pallas import tpu as pltpu
from jax.sharding import PartitionSpec as P

epsilon = 1e-05
bf16 = jnp.bfloat16
f32 = jnp.float32
LANES = 128
GROUP = 4
SPLIT = (64, 192, 256, 384)
VMEM_LIMIT = 52 * 2**20
whole_vmem = pl.BlockSpec(memory_space=pltpu.VMEM)
whole_smem = pl.BlockSpec(memory_space=pltpu.SMEM)
left_in_hbm = pl.BlockSpec(memory_space=pl.ANY)


def mm(a, b):
    return jnp.dot(a, b, preferred_element_type=f32)


def mm_first(a, b):
    return lax.dot_general(a, b, (((0,), (0,)), ((), ())), preferred_element_type=f32)


def gather_rows(index, table_ref, into_ref, count, into_first=0):
    for j in range(count):
        into_ref[pl.ds(into_first + j, 1), :] = table_ref[pl.ds(index(j), 1), :]


def match_rows(ids_row, count, weight_row=None):
    shape = (count, ids_row.shape[1])
    hit = lax.broadcasted_iota(jnp.int32, shape, 0) == ids_row
    if weight_row is None:
        return hit.astype(f32).astype(bf16)
    return jnp.where(hit, weight_row.astype(f32), 0.0).astype(bf16)


def aligned(at, size):
    return pl.ds(pl.multiple_of(at, size), size)


def side_by_side(rows):
    half = rows.shape[0] // 2
    return jnp.concatenate([rows[:half], rows[half:]], axis=1)


def normed_pairs(pairs, w_centred, spread_of):
    centred = mm(pairs, w_centred)
    spread = mm((centred * centred).astype(bf16), spread_of)
    return centred * lax.rsqrt(spread + epsilon)


def with_ones(rows):
    return jnp.concatenate([rows, jnp.ones(rows.shape, bf16)], axis=1)


def fill_weights(edge_out, node_out, w_out, w_node_out, spread_of):
    for weights, into in ((edge_out, w_out), (node_out, w_node_out)):
        wide = weights[...].astype(f32)
        centred = (wide - jnp.mean(wide, axis=1, keepdims=True)).astype(bf16)
        into[...] = jnp.zeros_like(into)
        into[:LANES, :LANES] = centred
        into[LANES:, LANES:] = centred
    shape = spread_of.shape
    same = (lax.broadcasted_iota(jnp.int32, shape, 0) < LANES) == (lax.broadcasted_iota(jnp.int32, shape, 1) < LANES)
    spread_of[...] = jnp.where(same, 1.0 / LANES, 0.0).astype(bf16)


weight_scratch = [pltpu.VMEM((2 * LANES, 2 * LANES), bf16)] * 3


weight_specs = [whole_vmem] * 5


def at_level(kernel, level, first):
    def with_level(*refs):
        one = [ref.at[level] for ref in refs[first : first + len(weight_specs)]]
        kernel(*refs[:first], *one, *refs[first + len(weight_specs) :])

    return with_level


def edge_first(picks, receiver_part, edge_rows, sender_part, w_edge):
    before = mm_first(picks, receiver_part) + mm(edge_rows, w_edge)
    return side_by_side(jnp.maximum(before + sender_part, 0.0).astype(bf16))


def edge_sums(picks, message, gain):
    half = picks.shape[1] // 2
    summed = mm(picks[:, :half], message[:, :LANES]) + mm(picks[:, half:], message[:, LANES:])
    return (summed * gain).astype(bf16)


def node_first(node_rows, summed, w_node):
    hidden = mm(jnp.concatenate([node_rows, summed], axis=1), w_node)
    return side_by_side(jnp.maximum(hidden, 0.0).astype(bf16))


def node_last(node_rows, update, gain):
    update = jnp.concatenate([update[:, :LANES], update[:, LANES:]], axis=0)
    return (node_rows.astype(f32) + update * gain).astype(bf16)


def border_kernel(place_ref, index_ref, x_ref, a_ref, b_ref, table, buffer):
    table[...] = x_ref[...].astype(f32)
    count = a_ref.shape[0]
    for side in range(2):
        gather_rows(lambda j: index_ref[0, side, j], table, buffer, count, side * count)
    a_ref[...] = buffer[aligned(count * place_ref[0], count), :].astype(bf16)
    b_ref[...] = buffer[aligned(count * (1 - place_ref[0]), count), :].astype(bf16)


def fill_tables(x_ref, place_ref, from_a, from_b, edge_in, table, receiver_part):
    count = x_ref.shape[0]
    border = from_a.shape[0]
    both = mm(x_ref[...], jnp.concatenate([edge_in[:LANES, :], edge_in[LANES : 2 * LANES, :]], axis=1))
    table[:count, :] = both[:, :LANES]
    receiver_part[...] = both[:, LANES:].astype(bf16)
    w_s = edge_in[:LANES, :]
    table[aligned(count + place_ref[0] * border, border), :] = mm(from_a[...], w_s)
    table[aligned(count + (1 - place_ref[0]) * border, border), :] = mm(from_b[...], w_s) * place_ref[1].astype(f32)


def fine_kernel(
    place_ref, pool_index, sender_ref, edge_ref, x_ref, from_a, from_b, receiver_ref, parent_ref,
    weight_ref, edge_in, edge_out, node_in, node_out, gain_ref,
    new_ref, sums_ref, a_ref, b_ref,
    table, receiver_part, edges, new32, buffer, aggregate, node_hidden,
    gathered0, gathered1, hidden0, hidden1, message0, message1,
    index0, index1, index2, index3, edge_sem, index_sem, w_out, w_node_out, spread_of,
):
    gathered, hidden, message = (gathered0, gathered1), (hidden0, hidden1), (message0, message1)
    indices = (index0, index1, index2, index3)
    block = gathered0.shape[0]
    groups, _, group_nodes = parent_ref.shape
    nodes = group_nodes // GROUP
    blocks = groups * GROUP
    chunk = GROUP * block
    gain, node_gain = gain_ref[0:1, :], gain_ref[1:2, :]

    def edge_copy(g):
        at = aligned(g * chunk, chunk)
        return pltpu.make_async_copy(edge_ref.at[at, :], edges.at[at, :], edge_sem.at[g])

    def index_copy(t, k):
        at = aligned(jnp.minimum(t, blocks - 1) * block, block)
        return pltpu.make_async_copy(sender_ref.at[at], indices[k], index_sem.at[k])

    def gather_block(k, into):
        gather_rows(lambda j: indices[k][j], table, into, block)

    for k in range(GROUP):
        index_copy(k, k).start()
    for g in range(groups):
        edge_copy(g).start()
    fill_weights(edge_out, node_out, w_out, w_node_out, spread_of)
    fill_tables(x_ref, place_ref, from_a, from_b, edge_in, table, receiver_part)
    sums_ref[...] = jnp.zeros_like(sums_ref)
    index_copy(0, 0).wait()
    gather_block(0, gathered0)

    def picks_of(t):
        t = jnp.maximum(t, 0)
        slot = lax.broadcasted_iota(jnp.int32, (1, block), 1) + t * block
        return match_rows(jnp.where(slot < place_ref[2], receiver_ref[t] - t * nodes, -1), nodes)

    def group_step(g, last):
        if not last:
            edge_copy(g).wait()
        for k in range(GROUP):
            t = g * GROUP + k
            here, before = k % 2, (k + 1) % 2
            if not last:
                later = (k + 1) % GROUP
                index_copy(t + 1, later).wait()
                index_copy(t + GROUP, k).start()
            keep = {}
            done = jnp.maximum(g - 1, 0)
            rows = aligned(done * group_nodes, group_nodes)

            def pick():
                if not last:
                    keep["picks"] = picks_of(t)
                if not last or k < 2:
                    keep["earlier"] = picks_of(t - 2)

            def multiply_first():
                if not last:
                    keep["before"] = mm_first(
                        keep["picks"], receiver_part[aligned(t * nodes, nodes), :]
                    ) + mm(edges[aligned(t * block, block), :], edge_in[2 * LANES :, :])
                if not last or k < 1:
                    keep["centred"] = mm(hidden[before][...], w_out[...])
                if k == 2:
                    node_hidden[...] = node_first(x_ref[rows, :], aggregate[...], node_in[...])
                if k == 3:
                    keep["node_centred"] = mm(node_hidden[...], w_node_out[...])

            def rectify():
                if not last:
                    rows = jnp.maximum(keep["before"] + gathered[here][...], 0.0)
                    hidden[here][...] = side_by_side(rows.astype(bf16))
                if not last or k < 1:
                    keep["squares"] = (keep["centred"] * keep["centred"]).astype(bf16)
                if k == 3:
                    keep["node_squares"] = (keep["node_centred"] * keep["node_centred"]).astype(bf16)

            def multiply_last():
                if not last or k < 1:
                    keep["spread"] = mm(keep["squares"], spread_of[...])
                if not last or k < 2:
                    into = (k - 2) % GROUP * nodes
                    aggregate[into : into + nodes, :] = edge_sums(keep["earlier"], message[here][...], gain)
                if k == 3:
                    keep["node_spread"] = mm(keep["node_squares"], spread_of[...])

            def scale():
                if not last or k < 1:
                    message[before][...] = (keep["centred"] * lax.rsqrt(keep["spread"] + epsilon)).astype(bf16)
                if k == 3:
                    update = keep["node_centred"] * lax.rsqrt(keep["node_spread"] + epsilon)
                    new_rows = node_last(x_ref[rows, :], update, node_gain)
                    new_ref[rows, :] = new_rows
                    new32[rows, :] = new_rows.astype(f32)
                    shares = match_rows(parent_ref[done], sums_ref.shape[0], weight_ref[done])
                    sums = sums_ref[...] + mm(shares, with_ones(new_rows))
                    sums_ref[...] = sums if last else jnp.where(g > 0, sums, 0.0)

            cuts = (0, *SPLIT, block)
            for i, step in enumerate((pick, multiply_first, rectify, multiply_last, scale)):
                step()
                if not last:
                    gather_rows(
                        lambda j: indices[later][cuts[i] + j], table, gathered[before],
                        cuts[i + 1] - cuts[i], cuts[i],
                    )
    def loop_step(g, carry):
        group_step(g, False)
        return carry

    lax.fori_loop(0, groups, loop_step, 0)
    group_step(groups, True)
    for k in range(1, GROUP):
        index_copy(blocks + k, k).wait()
    count = a_ref.shape[0]
    for side in range(2):
        gather_rows(lambda j: pool_index[0, side, j], new32, buffer, count, side * count)
    a_ref[...] = buffer[aligned(count * place_ref[0], count), :].astype(bf16)
    b_ref[...] = buffer[aligned(count * (1 - place_ref[0]), count), :].astype(bf16)


def pool_kernel(
    place_ref, border_index, sums_ref, from_a, from_b, target_ref, weight_ref,
    coarse_ref, a_ref, b_ref, table, buffer,
):
    count = sums_ref.shape[0]
    total = sums_ref[...]
    for side, rows in ((place_ref[0], from_a), (1 - place_ref[0], from_b)):
        shares = match_rows(target_ref[side], count, weight_ref[side])
        total += mm(shares, with_ones(rows[...]))
    coarse = (total[:, :LANES] / total[:, LANES:]).astype(bf16)
    coarse_ref[...] = coarse
    table[...] = coarse.astype(f32)
    border = a_ref.shape[0]
    for side in range(2):
        gather_rows(lambda j: border_index[0, side, j], table, buffer, border, side * border)
    a_ref[...] = buffer[aligned(border * place_ref[0], border), :].astype(bf16)
    b_ref[...] = buffer[aligned(border * (1 - place_ref[0]), border), :].astype(bf16)


def coarse_kernel(
    place_ref, sender_ref, edge_ref, x_ref, from_a, from_b, receiver_ref, parent_ref, weight_ref,
    edge_in, edge_out, node_in, node_out, gain_ref,
    new_ref, own_ref, a_ref, b_ref,
    table, receiver_part, gathered, aggregate, shares_sum, w_out, w_node_out, spread_of,
):
    blocks, _, block = receiver_ref.shape
    nodes = x_ref.shape[0] // blocks
    fill_weights(edge_out, node_out, w_out, w_node_out, spread_of)
    fill_tables(x_ref, place_ref, from_a, from_b, edge_in, table, receiver_part)
    gather_rows(lambda j: sender_ref[j], table, gathered, blocks * block)
    for t in range(blocks):
        at = slice(t * block, (t + 1) * block)
        own = slice(t * nodes, (t + 1) * nodes)
        picks = match_rows(receiver_ref[t] - t * nodes, nodes)
        pairs = edge_first(
            picks, receiver_part[own, :], edge_ref[at, :], gathered[at, :], edge_in[2 * LANES :, :]
        )
        message = normed_pairs(pairs, w_out[...], spread_of[...]).astype(bf16)
        aggregate[own, :] = edge_sums(picks, message, gain_ref[0:1, :])
    pairs = node_first(x_ref[...], aggregate[...], node_in[...])
    new_rows = node_last(x_ref[...], normed_pairs(pairs, w_node_out[...], spread_of[...]), gain_ref[1:2, :])
    new_ref[...] = new_rows
    share = own_ref.shape[0]
    shares = match_rows(parent_ref[...] - (place_ref[3] - 1) * share, 3 * share, weight_ref[...])
    shares_sum[...] = mm(shares, with_ones(new_rows))
    own_ref[...] = shares_sum[share : 2 * share, :]
    a_ref[...] = shares_sum[aligned(2 * share * place_ref[0], share), :]
    b_ref[...] = shares_sum[aligned(2 * share * (1 - place_ref[0]), share), :]


def lift_kernel(parent_ref, picks_ref):
    groups, _, size = parent_ref.shape
    for g in range(groups):
        picks_ref[g * size : (g + 1) * size, :] = match_rows(parent_ref[g], picks_ref.shape[1]).T


def top_kernel(
    place_ref, sender_ref, picks_ref, edge_ref, gathered_in, receiver_ref, parent_ref, coarse_ref,
    fine_ref, edge_in, edge_out, node_in, node_out, gain_ref,
    fine_out, coarse_out,
    picks, table, top_rows, gathered, picks_sem, w_out, w_node_out, spread_of,
):
    chunk = coarse_ref.shape[0]
    chunks = fine_ref.shape[0] // chunk

    def picks_copy(i):
        at = slice(i * chunk, (i + 1) * chunk)
        return pltpu.make_async_copy(picks_ref.at[at, :], picks.at[at, :], picks_sem.at[i])

    for i in range(chunks):
        picks_copy(i).start()
    tile = receiver_ref.shape[2]
    share = tile // 2
    nodes = 3 * share
    block = 3 * tile
    parts = gathered_in.shape[0] // share
    me, first = place_ref[3], place_ref[4]
    fill_weights(edge_out, node_out, w_out, w_node_out, spread_of)
    sender_part = mm(gathered_in[...], edge_in[:LANES, :])
    for q in range(parts):
        at = aligned((q ^ me) * share, share)
        table[at, :] = sender_part[q * share : (q + 1) * share, :]
        top_rows[at, :] = gathered_in[q * share : (q + 1) * share, :]
    window = top_rows[pl.ds(pl.multiple_of(first * share, share), nodes), :]
    gather_rows(lambda j: sender_ref[first * tile + j], table, gathered, block)
    ids = jnp.concatenate([receiver_ref[first + i] for i in range(3)], axis=1) - first * share
    matches = match_rows(ids, nodes)
    pairs = edge_first(
        matches, mm(window, edge_in[LANES : 2 * LANES, :]).astype(bf16),
        edge_ref[pl.ds(pl.multiple_of(first * tile, tile), block), :], gathered[...], edge_in[2 * LANES :, :],
    )
    message = normed_pairs(pairs, w_out[...], spread_of[...]).astype(bf16)
    pairs = node_first(window, edge_sums(matches, message, gain_ref[0:1, :]), node_in[...])
    top_new = node_last(window, normed_pairs(pairs, w_node_out[...], spread_of[...]), gain_ref[1:2, :])
    up = mm_first(match_rows(parent_ref[...] - first * share, nodes), top_new)
    coarse = (coarse_ref[...].astype(f32) + up).astype(bf16)
    coarse_out[...] = coarse
    for i in range(chunks):
        picks_copy(i).wait()
        at = slice(i * chunk, (i + 1) * chunk)
        fine_out[at, :] = (fine_ref[at, :].astype(f32) + mm(picks[at, :], coarse)).astype(bf16)


def call(kernel, name, outs, specs, scratch, operands, flops=0, moved=0):
    return pl.pallas_call(
        kernel,
        name=name,
        out_shape=outs,
        in_specs=specs,
        out_specs=jax.tree.map(lambda _: whole_vmem, outs),
        scratch_shapes=scratch,
        cost_estimate=pl.CostEstimate(flops=flops, bytes_accessed=moved, transcendentals=0),
        compiler_params=pltpu.CompilerParams(vmem_limit_bytes=VMEM_LIMIT),
    )(*operands)


def rows_of(count, dtype=bf16, width=LANES):
    return jax.ShapeDtypeStruct((count, width), dtype)


def swap_with_neighbours(for_a, for_b):
    count = lax.axis_size("dom")
    pairs_a = [(i, i ^ 1) for i in range(count)]
    pairs_b = [(i, (i + 1) % count) for i in range(1, count, 2)]
    pairs_b += [(j, i) for i, j in pairs_b]
    return lax.ppermute(for_a, "dom", pairs_a), lax.ppermute(for_b, "dom", pairs_b)


def gather_all(rows):
    count = lax.axis_size("dom")
    steps = []
    stride = 1
    while stride < count:
        radix = 4 if stride * 4 <= count else 2
        steps.append((stride, radix))
        stride *= radix
    blocks = rows[None]
    for stride, radix in reversed(steps):
        taken = [blocks] + [
            lax.ppermute(blocks, "dom", [(i, i ^ (j * stride)) for i in range(count)])
            for j in range(1, radix)
        ]
        blocks = jnp.stack(taken, axis=1).reshape((-1,) + rows.shape)
    return blocks


def body(
    fine_latent, fine_edges, fine_sender, fine_receiver, edge_count, fine_border, pool_rows, pool_target,
    pool_weight, fine_parent, fine_weight, coarse_edges, coarse_sender, coarse_receiver, coarse_border,
    coarse_parent, coarse_weight, top_edges, top_sender, top_receiver, edge_in, edge_out, node_in, node_out,
    norm_gain,
):
    count = lax.axis_size("dom")
    me = lax.axis_index("dom").astype(jnp.int32)
    inner = jnp.where((me == 0) | (me == count - 1), 0, 1).astype(jnp.int32)
    place = jnp.stack([1 - me % 2, inner, edge_count[0], me, jnp.clip(me - 1, 0, count - 3)])
    weights = (edge_in, edge_out, node_in, node_out, norm_gain)

    fine_total = fine_latent.shape[0]
    edge_total = fine_sender.shape[0]
    coarse_total = coarse_parent.shape[0]
    border = fine_border.shape[2]
    slots = pool_rows.shape[2]
    nodes = LANES
    block = nodes * edge_total // fine_total
    blocks = edge_total // block
    groups = blocks // GROUP

    with jax.named_scope("fine_border_rows"):
        for_a, for_b = call(
            border_kernel, "border_rows", [rows_of(border), rows_of(border)],
            [whole_smem, whole_smem, whole_vmem],
            [pltpu.VMEM((fine_total, LANES), f32), pltpu.VMEM((2 * border, LANES), f32)],
            (place, fine_border, fine_latent),
        )
        from_a, from_b = swap_with_neighbours(for_a, for_b)
        lift_picks = call(
            lift_kernel, "lift_picks", rows_of(fine_total, bf16, coarse_total), [whole_vmem], [],
            (fine_parent.reshape(fine_total // coarse_total, 1, coarse_total),),
            flops=10**9, moved=fine_total * coarse_total * 2,
        )

    with jax.named_scope("fine_step"):
        fine_new, local_sums, for_a, for_b = call(
            at_level(fine_kernel, 0, 10), "fine_step",
            [rows_of(fine_total), rows_of(coarse_total, f32, 2 * LANES), rows_of(slots), rows_of(slots)],
            [whole_smem, whole_smem, left_in_hbm, left_in_hbm] + [whole_vmem] * 6 + weight_specs,
            [
                pltpu.VMEM((fine_total + 2 * border, LANES), f32),
                pltpu.VMEM((fine_total, LANES), bf16),
                pltpu.VMEM((edge_total, LANES), bf16),
                pltpu.VMEM((fine_total, LANES), f32),
                pltpu.VMEM((2 * slots, LANES), f32),
                pltpu.VMEM((GROUP * nodes, LANES), bf16),
                pltpu.VMEM((GROUP * nodes // 2, 2 * LANES), bf16),
            ]
            + [pltpu.VMEM((block, LANES), f32)] * 2
            + [pltpu.VMEM((block // 2, 2 * LANES), bf16)] * 4
            + [pltpu.SMEM((block,), jnp.int32)] * GROUP
            + [pltpu.SemaphoreType.DMA((groups,)), pltpu.SemaphoreType.DMA((GROUP,))]
            + weight_scratch,
            (
                place, pool_rows, fine_sender, fine_edges, fine_latent, from_a, from_b,
                fine_receiver.reshape(blocks, 1, block), fine_parent.reshape(groups, 1, GROUP * nodes),
                fine_weight.reshape(groups, 1, GROUP * nodes),
            )
            + weights,
        )
        from_a, from_b = swap_with_neighbours(for_a, for_b)

    with jax.named_scope("coarse_input"):
        border1 = coarse_border.shape[2]
        coarse_in, for_a, for_b = call(
            pool_kernel, "coarse_input",
            [rows_of(coarse_total), rows_of(border1), rows_of(border1)],
            [whole_smem] * 2 + [whole_vmem] * 5,
            [pltpu.VMEM((coarse_total, LANES), f32), pltpu.VMEM((2 * border1, LANES), f32)],
            (
                place, coarse_border, local_sums, from_a, from_b,
                pool_target.reshape(2, 1, slots), pool_weight.reshape(2, 1, slots),
            ),
        )
        from_a, from_b = swap_with_neighbours(for_a, for_b)

    with jax.named_scope("coarse_step"):
        edge_total1 = coarse_sender.shape[0]
        block1 = LANES * edge_total1 // coarse_total
        blocks1 = edge_total1 // block1
        share = coarse_total // 8
        coarse_new, own, for_a, for_b = call(
            at_level(coarse_kernel, 1, 9), "coarse_step",
            [rows_of(coarse_total)] + [rows_of(share, f32, 2 * LANES)] * 3,
            [whole_smem, whole_smem] + [whole_vmem] * 7 + weight_specs,
            [
                pltpu.VMEM((coarse_total + 2 * border1, LANES), f32),
                pltpu.VMEM((coarse_total, LANES), bf16),
                pltpu.VMEM((edge_total1, LANES), f32),
                pltpu.VMEM((coarse_total, LANES), bf16),
                pltpu.VMEM((3 * share, 2 * LANES), f32),
            ]
            + weight_scratch,
            (
                place, coarse_sender, coarse_edges, coarse_in, from_a, from_b,
                coarse_receiver.reshape(blocks1, 1, block1), coarse_parent[None, :], coarse_weight[None, :],
            )
            + weights,
        )
        from_a, from_b = swap_with_neighbours(for_a, for_b)
        shares = own + from_a + from_b
        top_in = (shares[:, :LANES] / shares[:, LANES:]).astype(bf16)

    with jax.named_scope("top_step"):
        everyone = gather_all(top_in).reshape(count * share, LANES)
        tile = 2 * share
        window = 3 * tile
        fine_out, coarse_out = call(
            at_level(top_kernel, 2, 9), "top_step",
            [rows_of(fine_total), rows_of(coarse_total)],
            [whole_smem] * 2 + [left_in_hbm] + [whole_vmem] * 6 + weight_specs,
            [
                pltpu.VMEM((fine_total, coarse_total), bf16),
                pltpu.VMEM((count * share, LANES), f32),
                pltpu.VMEM((count * share, LANES), bf16),
                pltpu.VMEM((window, LANES), f32),
                pltpu.SemaphoreType.DMA((fine_total // coarse_total,)),
            ]
            + weight_scratch,
            (
                place, top_sender, lift_picks, top_edges, everyone,
                top_receiver.reshape(top_receiver.shape[0] // tile, 1, tile), coarse_parent[None, :], coarse_new,
                fine_new,
            )
            + weights,
        )
    return (fine_out, coarse_out)


def solution(mesh):
    row = ("groups", "dom")
    return jax.shard_map(
        body,
        mesh=mesh,
        in_specs=(
            P(row, None), P(row, None), P(row), P(row), P(row), P(row, None, None), P(row, None, None),
            P(row, None, None), P(row, None, None), P(row), P(row), P(row, None), P(row), P(row),
            P(row, None, None), P(row), P(row), P("groups", None), P("groups"), P("groups"), P(), P(), P(), P(),
            P(),
        ),
        out_specs=(P(row, None), P(row, None)),
        check_vma=False,
    )
```

time: 114 us -> 94.5 us (0.83)
  starting transfers between devices: 14.6 us -> 26.6 us
  Pallas kernels: 52 us -> 40.9 us
  waiting for transfers between devices: 21.9 us -> 13 us
  other arithmetic: 8.76 us -> 0.09 us
  local copies, waits for them, and re-layouts: 13.8 us -> 11.3 us
    ppermute x4, starting transfers between devices: 7.49 us -> 19.1 us  [swap_with_neighbours(): lax.ppermute(for_b, 'dom', pairs_b)]
    pallas_call x5 -> x6, Pallas kernels: 52 us -> 40.9 us  [call(): pl.pallas_call(kernel, name=name, out_shape=outs, in_specs=specs, out_spe...]
    unnamed x26 -> x60, local copies, waits for them, and re-layouts: 2.32 us -> 11.2 us
    rev x5 -> x0, local copies, waits for them, and re-layouts: 7.21 us -> none  [by_partner(): return jnp.where(odd == 1, pair, pair[::-1])]
    ppermute x4, waiting for transfers between devices: 15.1 us -> 10.3 us  [swap_with_neighbours(): lax.ppermute(for_b, 'dom', pairs_b)]
    convert_element_type x6 -> x0, other arithmetic: 2.82 us -> none  [the longest x2 2.02 us: centred_pairs(): centred = (wide - jnp.mean(wide, axis=2, keepdims=True)).astype(bf16)]
    ppermute x6, waiting for transfers between devices: 5.38 us -> 2.65 us  [gather_all(): lax.ppermute(blocks, 'dom', [(i, i ^ j * stride) for i in range(count)])]
    squeeze x4 -> x0, local copies, waits for them, and re-layouts: 2.49 us -> none  [the longest x1 0.92 us: weights_of(): node_in[level]]
  transfers between devices with their start and end apart: 14 -> 14, of which waited for: 9 -> 7; matrix products, arithmetic and copies ran while one was open for 15% -> 0% of each run, Pallas kernels for 0% -> 3%
where the time goes in v2:
time: 94.5 us; the launch traced here: 93.7 us
  Pallas kernels  40.9 us (43%)
  starting transfers between devices  26.6 us (28%)
  waiting for transfers between devices  13 us (14%)
  local copies, waits for them, and re-layouts  11.3 us (12%)
  between operations  1.78 us (2%)
    pallas_call x6, Pallas kernels, call(): pl.pallas_call(kernel, name=name, out_shape=outs, in_specs=specs, out_spe...  40.9 us
    ppermute x4, starting transfers between devices, swap_with_neighbours(): lax.ppermute(for_b, 'dom', pairs_b)  19.1 us
    unnamed x60, local copies, waits for them, and re-layouts  11.2 us
    ppermute x4, waiting for transfers between devices, swap_with_neighbours(): lax.ppermute(for_b, 'dom', pairs_b)  10.3 us
    ppermute x6, starting transfers between devices, gather_all(): lax.ppermute(blocks, 'dom', [(i, i ^ j * stride) for i in range(count)])  6.76 us
    ppermute x6, waiting for transfers between devices, gather_all(): lax.ppermute(blocks, 'dom', [(i, i ^ j * stride) for i in range(count)])  2.65 us
  transfers between devices with their start and end apart: 14, of which 7 were waited for; matrix products, arithmetic and copies ran while one was open for 0% of the time, Pallas kernels for 3%

profile of v2, /device:TPU:0, one launch (start us, length us, event | category | flops | bytes accessed | tf_op | source)
XLA Modules:
  0.0 93.7 jit_solution(11770650185645149890)
XLA Ops:
  1.4 1.2 %copy-done = bf16[4096,128]{1,0:T(8,128)(2,1)S(1)} copy-done((bf16[4096,128]{1,0:T(8,128)(2,1)S(1)}, bf16[4096,128]{1,0:T(8,128)(2,1)}, u32[]{:S(2)}) %copy-start) | copy-done | bytes 1048600
  2.6 0.7 copy-done.19
  3.4 1.9 %border_rows.1 = (bf16[1024,128]{1,0:T(8,128)(2,1)S(1)}, bf16[1024,128]{1,0:T(8,128)(2,1)S(1)}) custom-call(s32[5]{0:T(128)S(1)} %stack.43.place_ref.refs_0_, s32[1,2,1024]{2,1,0:T(2,128)S(1)} %copy-done.19, bf16[4096,128]{1,0:T(8,128)(2,1)S(1)} %copy-done), custom_call_target="tpu_custom_call" | custom-call | tf_op jit(solution)/shard_map/fine_border_rows/border_rows/pallas_call | solution.py:361
  5.3 0.5 collective-permute-start
  5.9 5.7 %collective-permute-start.1 = (bf16[1024,128]{1,0:T(8,128)(2,1)S(1)}, bf16[1024,128]{1,0:T(8,128)(2,1)S(1)}, u32[]{:S(2)}, u32[]{:S(2)}) collective-permute-start(bf16[1024,128]{1,0:T(8,128)(2,1)S(1)} %get-tuple-element.16), channel_id=1, source_target_pairs={{1,2},{3,4},{5,6},{7,8},{9,10},{11,12},{13,14},{15,0},{2,1},{4,3},... | collective-permute-start | bytes 786440 | tf_op jit(solution)/shard_map/fine_border_rows/ppermute | solution.py:382
  11.5 4.1 %collective-permute-done.1.refs_6_ = bf16[1024,128]{1,0:T(8,128)(2,1)S(1)} collective-permute-done((bf16[1024,128]{1,0:T(8,128)(2,1)S(1)}, bf16[1024,128]{1,0:T(8,128)(2,1)S(1)}, u32[]{:S(2)}, u32[]{:S(2)}) %collective-permute-start.1) | collective-permute-done | bytes 262176 | tf_op jit(solution)/shard_map/fine_border_rows/ppermute | solution.py:382
  15.6 1.0 %copy-done.1 = bf16[3,384,128]{2,1,0:T(8,128)(2,1)S(1)} copy-done((bf16[3,384,128]{2,1,0:T(8,128)(2,1)S(1)}, bf16[3,384,128]{2,1,0:T(8,128)(2,1)}, u32[]{:S(2)}) %copy-start.1) | copy-done | bytes 294936
  16.6 0.9 copy-done.3
  17.5 0.9 copy-done.5
  18.4 0.9 copy-done.7
  19.3 0.8 copy-done.12
  20.1 0.8 copy-done.13
  21.0 0.7 copy-done.14
  21.7 0.7 copy-done.16
  22.4 0.7 copy-done.18
  23.1 0.7 copy-done.25
  23.8 24.3 %fine_step.1 = (bf16[4096,128]{1,0:T(8,128)(2,1)}, f32[512,256]{1,0:T(8,128)}, bf16[512,128]{1,0:T(8,128)(2,1)S(1)}, bf16[512,128]{1,0:T(8,128)(2,1)S(1)}) custom-call(s32[5]{0:T(128)S(1)} %stack.43.place_ref.refs_0_, s32[1,2,512]{2,1,0:T(2,128)S(1)} %copy-done.25, s32[16384]{0:T(1024)S(1)} %copy-done.12, bf16[16384,128]{1,0:T(8,128)(2,1)} %refs_3_.2, ...), custom_call_target="tpu_custom_call" | custom-call | tf_op jit(solution)/shard_map/fine_step/fine_step/pallas_call | solution.py:361
  48.3 4.5 %collective-permute-start.3 = (bf16[512,128]{1,0:T(8,128)(2,1)S(1)}, bf16[512,128]{1,0:T(8,128)(2,1)S(1)}, u32[]{:S(2)}, u32[]{:S(2)}) collective-permute-start(bf16[512,128]{1,0:T(8,128)(2,1)S(1)} %get-tuple-element.19), channel_id=1, source_target_pairs={{1,2},{3,4},{5,6},{7,8},{9,10},{11,12},{13,14},{15,0},{2,1},{4,3},... | collective-permute-start | bytes 393224 | tf_op jit(solution)/shard_map/fine_step/ppermute | solution.py:382
  52.8 2.6 %collective-permute-done.3.from_b = bf16[512,128]{1,0:T(8,128)(2,1)S(1)} collective-permute-done((bf16[512,128]{1,0:T(8,128)(2,1)S(1)}, bf16[512,128]{1,0:T(8,128)(2,1)S(1)}, u32[]{:S(2)}, u32[]{:S(2)}) %collective-permute-start.3) | collective-permute-done | bytes 131104 | tf_op jit(solution)/shard_map/fine_step/ppermute | solution.py:382
  55.4 1.0 %copy-done.10 = f32[512,256]{1,0:T(8,128)S(1)} copy-done((f32[512,256]{1,0:T(8,128)S(1)}, f32[512,256]{1,0:T(8,128)}, u32[]{:S(2)}) %copy-start.10) | copy-done | bytes 524312
  56.5 1.1 %coarse_input.1 = (bf16[512,128]{1,0:T(8,128)(2,1)S(1)}, bf16[128,128]{1,0:T(8,128)(2,1)S(1)}, bf16[128,128]{1,0:T(8,128)(2,1)S(1)}) custom-call(s32[5]{0:T(128)S(1)} %stack.43.place_ref.refs_0_, s32[1,2,128]{2,1,0:T(2,128)S(1)} %copy-done.27, f32[512,256]{1,0:T(8,128)S(1)} %copy-done.10, bf16[512,128]{1,0:T(8,128)(2,1)S(1)} %collective-permute-done.2.from_a, ...), custom_call_target="tpu_custom_call" | custom-call | tf_op jit(solution)/shard_map/coarse_input/coarse_input/pallas_call | solution.py:361
  57.7 4.5 %collective-permute-start.5 = (bf16[128,128]{1,0:T(8,128)(2,1)S(1)}, bf16[128,128]{1,0:T(8,128)(2,1)S(1)}, u32[]{:S(2)}, u32[]{:S(2)}) collective-permute-start(bf16[128,128]{1,0:T(8,128)(2,1)S(1)} %get-tuple-element.22), channel_id=1, source_target_pairs={{1,2},{3,4},{5,6},{7,8},{9,10},{11,12},{13,14},{15,0},{2,1},{4,3},... | collective-permute-start | bytes 98312 | tf_op jit(solution)/shard_map/coarse_input/ppermute | solution.py:382
  62.2 1.6 %collective-permute-done.5.refs_5_ = bf16[128,128]{1,0:T(8,128)(2,1)S(1)} collective-permute-done((bf16[128,128]{1,0:T(8,128)(2,1)S(1)}, bf16[128,128]{1,0:T(8,128)(2,1)S(1)}, u32[]{:S(2)}, u32[]{:S(2)}) %collective-permute-start.5) | collective-permute-done | bytes 32800 | tf_op jit(solution)/shard_map/coarse_input/ppermute | solution.py:382
  63.9 4.0 %coarse_step.1 = (bf16[512,128]{1,0:T(8,128)(2,1)S(1)}, f32[64,256]{1,0:T(8,128)S(1)}, f32[64,256]{1,0:T(8,128)S(1)}, f32[64,256]{1,0:T(8,128)S(1)}) custom-call(s32[5]{0:T(128)S(1)} %stack.43.place_ref.refs_0_, s32[2048]{0:T(1024)S(1)} %copy-done.20, bf16[2048,128]{1,0:T(8,128)(2,1)S(1)} %copy-done.9, bf16[512,128]{1,0:T(8,128)(2,1)S(1)} %get-tuple-element.20.refs_3_, ...), custom_call_target="tpu_custom_call" | custom-call | tf_op jit(solution)/shard_map/coarse_step/coarse_step/pallas_call | solution.py:361
  68.0 4.5 %collective-permute-start.7 = (f32[64,256]{1,0:T(8,128)S(1)}, f32[64,256]{1,0:T(8,128)S(1)}, u32[]{:S(2)}, u32[]{:S(2)}) collective-permute-start(f32[64,256]{1,0:T(8,128)S(1)} %get-tuple-element.25), channel_id=1, source_target_pairs={{1,2},{3,4},{5,6},{7,8},{9,10},{11,12},{13,14},{15,0},{2,1},{4,3},... | collective-permute-start | bytes 196616 | tf_op jit(solution)/shard_map/coarse_step/ppermute | solution.py:382
  72.5 2.0 %collective-permute-done.7 = f32[64,256]{1,0:T(8,128)S(1)} collective-permute-done((f32[64,256]{1,0:T(8,128)S(1)}, f32[64,256]{1,0:T(8,128)S(1)}, u32[]{:S(2)}, u32[]{:S(2)}) %collective-permute-start.7) | collective-permute-done | bytes 65568 | tf_op jit(solution)/shard_map/coarse_step/ppermute | solution.py:382
  74.7 4.3 %collective-permute-start.8 = (bf16[1,64,128]{2,1,0:T(8,128)(2,1)S(1)}, bf16[1,64,128]{2,1,0:T(8,128)(2,1)S(1)}, u32[]{:S(2)}, u32[]{:S(2)}) collective-permute-start(bf16[1,64,128]{2,1,0:T(8,128)(2,1)S(1)} %fusion.4), channel_id=1, source_target_pairs={{0,4},{1,5},{2,6},{3,7},{4,0},{5,1},{6,2},{7,3},{8,12},{9,13},{10,... | collective-permute-start | bytes 49160 | tf_op jit(solution)/shard_map/top_step/ppermute | solution.py:396
  79.0 1.3 %collective-permute-done.10 = bf16[1,64,128]{2,1,0:T(8,128)(2,1)S(1)} collective-permute-done((bf16[1,64,128]{2,1,0:T(8,128)(2,1)S(1)}, bf16[1,64,128]{2,1,0:T(8,128)(2,1)S(1)}, u32[]{:S(2)}, u32[]{:S(2)}) %collective-permute-start.10) | collective-permute-done | bytes 16416 | tf_op jit(solution)/shard_map/top_step/ppermute | solution.py:396
  80.7 2.1 %collective-permute-start.13 = (bf16[4,64,128]{2,1,0:T(8,128)(2,1)S(1)}, bf16[4,64,128]{2,1,0:T(8,128)(2,1)S(1)}, u32[]{:S(2)}, u32[]{:S(2)}) collective-permute-start(bf16[4,64,128]{2,1,0:T(8,128)(2,1)S(1)} %get-tuple-element.29), channel_id=1, source_target_pairs={{0,3},{1,2},{2,1},{3,0},{4,7},{5,6},{6,5},{7,4},{8,11},{9,10},{10,... | collective-permute-start | bytes 196616 | tf_op jit(solution)/shard_map/top_step/ppermute | solution.py:396
  83.0 3.1 %lift_picks.1.refs_2_ = bf16[4096,512]{1,0:T(8,128)(2,1)} custom-call(s32[8,1,512]{2,1,0:T(1,128)S(1)} %bitcast.29), custom_call_target="tpu_custom_call" | custom-call | flops 1000000000 | bytes 4194304 | tf_op jit(solution)/shard_map/fine_border_rows/lift_picks/pallas_call | solution.py:361
  86.1 0.9 %collective-permute-done.12 = bf16[4,64,128]{2,1,0:T(8,128)(2,1)S(1)} collective-permute-done((bf16[4,64,128]{2,1,0:T(8,128)(2,1)S(1)}, bf16[4,64,128]{2,1,0:T(8,128)(2,1)S(1)}, u32[]{:S(2)}, u32[]{:S(2)}) %collective-permute-start.12) | collective-permute-done | bytes 65568 | tf_op jit(solution)/shard_map/top_step/ppermute | solution.py:396
  87.2 6.4 %top_step.1 = (bf16[4096,128]{1,0:T(8,128)(2,1)}, bf16[512,128]{1,0:T(8,128)(2,1)}) custom-call(s32[5]{0:T(128)S(1)} %stack.43.place_ref.refs_0_, s32[2048]{0:T(1024)S(1)} %copy-done.22, bf16[4096,512]{1,0:T(8,128)(2,1)} %lift_picks.1.refs_2_, bf16[2048,128]{1,0:T(8,128)(2,1)S(1)} %copy-done.11, bf16[1024,128]{1,0:T(8,128)(2,1)S(1)} %bitcast.26, ...), custom_call_target="tpu_custom_call" | custom-call | tf_op jit(solution)/shard_map/top_step/top_step/pallas_call | solution.py:361
  (71 shorter events, 1.3 us)
Async XLA Ops:
  0.6 52.1 %copy-start.28 = (s32[1,2,512]{2,1,0:T(2,128)S(1)}, s32[1,2,512]{2,1,0:T(2,128)}, u32[]{:S(2)}) copy-start(s32[1,2,512]{2,1,0:T(2,128)} %param.32) | copy-start | bytes 12292
  0.6 52.1 %copy-start.29 = (s32[1,2,512]{2,1,0:T(2,128)S(1)}, s32[1,2,512]{2,1,0:T(2,128)}, u32[]{:S(2)}) copy-start(s32[1,2,512]{2,1,0:T(2,128)} %param.33) | copy-start | bytes 12292
  0.7 54.8 %copy-start.27 = (s32[1,2,128]{2,1,0:T(2,128)S(1)}, s32[1,2,128]{2,1,0:T(2,128)}, u32[]{:S(2)}) copy-start(s32[1,2,128]{2,1,0:T(2,128)} %border_index.1) | copy-start | bytes 3076
  1.4 1.2 %copy-start = (bf16[4096,128]{1,0:T(8,128)(2,1)S(1)}, bf16[4096,128]{1,0:T(8,128)(2,1)}, u32[]{:S(2)}) copy-start(bf16[4096,128]{1,0:T(8,128)(2,1)} %refs_4_.1) | copy-start | bytes 3145732
  3.3 60.5 %copy-start.2 = (bf16[3,384,128]{2,1,0:T(8,128)(2,1)S(1)}, bf16[3,384,128]{2,1,0:T(8,128)(2,1)}, u32[]{:S(2)}) copy-start(bf16[3,384,128]{2,1,0:T(8,128)(2,1)} %refs_9_.3) | copy-start | bytes 884740
  3.3 60.5 %copy-start.4 = (bf16[3,256,128]{2,1,0:T(8,128)(2,1)S(1)}, bf16[3,256,128]{2,1,0:T(8,128)(2,1)}, u32[]{:S(2)}) copy-start(bf16[3,256,128]{2,1,0:T(8,128)(2,1)} %refs_11_.5) | copy-start | bytes 589828
  3.3 60.5 %copy-start.6 = (bf16[3,128,128]{2,1,0:T(8,128)(2,1)S(1)}, bf16[3,128,128]{2,1,0:T(8,128)(2,1)}, u32[]{:S(2)}) copy-start(bf16[3,128,128]{2,1,0:T(8,128)(2,1)} %refs_10_.5) | copy-start | bytes 294916
  3.3 60.5 %copy-start.8 = (bf16[3,128,128]{2,1,0:T(8,128)(2,1)S(1)}, bf16[3,128,128]{2,1,0:T(8,128)(2,1)}, u32[]{:S(2)}) copy-start(bf16[3,128,128]{2,1,0:T(8,128)(2,1)} %refs_12_.5) | copy-start | bytes 294916
  3.4 60.5 %copy-start.20 = (s32[2048]{0:T(1024)S(1)}, s32[2048]{0:T(1024)}, u32[]{:S(2)}) copy-start(s32[2048]{0:T(1024)} %refs_1_.4) | copy-start | bytes 24580
  3.4 60.5 %copy-start.21 = (s32[2048]{0:T(1024)S(1)}, s32[2048]{0:T(1024)}, u32[]{:S(2)}) copy-start(s32[2048]{0:T(1024)} %param.38) | copy-start | bytes 24580
  3.4 60.5 %copy-start.24 = (s32[512]{0:T(512)S(1)}, s32[512]{0:T(512)}, u32[]{:S(2)}) copy-start(s32[512]{0:T(512)} %param.40) | copy-start | bytes 6148
  3.4 60.5 %copy-start.26 = (s32[512]{0:T(512)S(1)}, s32[512]{0:T(512)}, u32[]{:S(2)}) copy-start(s32[512]{0:T(512)} %param.41) | copy-start | bytes 6148
  5.3 6.2 %collective-permute-start = (bf16[1024,128]{1,0:T(8,128)(2,1)S(1)}, bf16[1024,128]{1,0:T(8,128)(2,1)S(1)}, u32[]{:S(2)}, u32[]{:S(2)}) collective-permute-start(bf16[1024,128]{1,0:T(8,128)(2,1)S(1)} %get-tuple-element.15), channel_id=1, source_target_pairs={{0,1},{1,0},{2,3},{3,2},{4,5},{5,4},{6,7},{7,6},{8,9},{9,8},{10,11... | collective-permute-start | bytes 786440 | tf_op jit(solution)/shard_map/fine_border_rows/ppermute | solution.py:382
  5.9 9.8 %collective-permute-start.1 = (bf16[1024,128]{1,0:T(8,128)(2,1)S(1)}, bf16[1024,128]{1,0:T(8,128)(2,1)S(1)}, u32[]{:S(2)}, u32[]{:S(2)}) collective-permute-start(bf16[1024,128]{1,0:T(8,128)(2,1)S(1)} %get-tuple-element.16), channel_id=1, source_target_pairs={{1,2},{3,4},{5,6},{7,8},{9,10},{11,12},{13,14},{15,0},{2,1},{4,3},... | collective-permute-start | bytes 786440 | tf_op jit(solution)/shard_map/fine_border_rows/ppermute | solution.py:382
  23.8 40.1 %copy-start.9 = (bf16[2048,128]{1,0:T(8,128)(2,1)S(1)}, bf16[2048,128]{1,0:T(8,128)(2,1)}, u32[]{:S(2)}) copy-start(bf16[2048,128]{1,0:T(8,128)(2,1)} %refs_2_.3) | copy-start | bytes 1572868
  23.8 59.2 %copy-start.15 = (s32[4096]{0:T(1024)S(1)}, s32[4096]{0:T(1024)}, u32[]{:S(2)}) copy-start(s32[4096]{0:T(1024)} %param.34) | copy-start | bytes 49156
  23.8 63.4 %copy-start.11 = (bf16[2048,128]{1,0:T(8,128)(2,1)S(1)}, bf16[2048,128]{1,0:T(8,128)(2,1)}, u32[]{:S(2)}) copy-start(bf16[2048,128]{1,0:T(8,128)(2,1)} %refs_3_.3) | copy-start | bytes 1572868
  48.1 39.0 %copy-start.17 = (f32[3,2,128]{2,1,0:T(2,128)S(1)}, f32[3,2,128]{2,1,0:T(2,128)}, u32[]{:S(2)}) copy-start(f32[3,2,128]{2,1,0:T(2,128)} %refs_13_.5) | copy-start | bytes 9220
  48.2 39.0 %copy-start.22 = (s32[2048]{0:T(1024)S(1)}, s32[2048]{0:T(1024)}, u32[]{:S(2)}) copy-start(s32[2048]{0:T(1024)} %refs_1_.5) | copy-start | bytes 24580
  48.2 39.0 %copy-start.23 = (s32[2048]{0:T(1024)S(1)}, s32[2048]{0:T(1024)}, u32[]{:S(2)}) copy-start(s32[2048]{0:T(1024)} %param.44) | copy-start | bytes 24580
  48.2 4.6 %collective-permute-start.2 = (bf16[512,128]{1,0:T(8,128)(2,1)S(1)}, bf16[512,128]{1,0:T(8,128)(2,1)S(1)}, u32[]{:S(2)}, u32[]{:S(2)}) collective-permute-start(bf16[512,128]{1,0:T(8,128)(2,1)S(1)} %get-tuple-element.18), channel_id=1, source_target_pairs={{0,1},{1,0},{2,3},{3,2},{4,5},{5,4},{6,7},{7,6},{8,9},{9,8},{10,11... | collective-permute-start | bytes 393224 | tf_op jit(solution)/shard_map/fine_step/ppermute | solution.py:382
  48.3 7.2 %collective-permute-start.3 = (bf16[512,128]{1,0:T(8,128)(2,1)S(1)}, bf16[512,128]{1,0:T(8,128)(2,1)S(1)}, u32[]{:S(2)}, u32[]{:S(2)}) collective-permute-start(bf16[512,128]{1,0:T(8,128)(2,1)S(1)} %get-tuple-element.19), channel_id=1, source_target_pairs={{1,2},{3,4},{5,6},{7,8},{9,10},{11,12},{13,14},{15,0},{2,1},{4,3},... | collective-permute-start | bytes 393224 | tf_op jit(solution)/shard_map/fine_step/ppermute | solution.py:382
  57.6 4.6 %collective-permute-start.4 = (bf16[128,128]{1,0:T(8,128)(2,1)S(1)}, bf16[128,128]{1,0:T(8,128)(2,1)S(1)}, u32[]{:S(2)}, u32[]{:S(2)}) collective-permute-start(bf16[128,128]{1,0:T(8,128)(2,1)S(1)} %get-tuple-element.21), channel_id=1, source_target_pairs={{0,1},{1,0},{2,3},{3,2},{4,5},{5,4},{6,7},{7,6},{8,9},{9,8},{10,11... | collective-permute-start | bytes 98312 | tf_op jit(solution)/shard_map/coarse_input/ppermute | solution.py:382
  57.7 6.1 %collective-permute-start.5 = (bf16[128,128]{1,0:T(8,128)(2,1)S(1)}, bf16[128,128]{1,0:T(8,128)(2,1)S(1)}, u32[]{:S(2)}, u32[]{:S(2)}) collective-permute-start(bf16[128,128]{1,0:T(8,128)(2,1)S(1)} %get-tuple-element.22), channel_id=1, source_target_pairs={{1,2},{3,4},{5,6},{7,8},{9,10},{11,12},{13,14},{15,0},{2,1},{4,3},... | collective-permute-start | bytes 98312 | tf_op jit(solution)/shard_map/coarse_input/ppermute | solution.py:382
  67.9 4.6 %collective-permute-start.6 = (f32[64,256]{1,0:T(8,128)S(1)}, f32[64,256]{1,0:T(8,128)S(1)}, u32[]{:S(2)}, u32[]{:S(2)}) collective-permute-start(f32[64,256]{1,0:T(8,128)S(1)} %get-tuple-element.24), channel_id=1, source_target_pairs={{0,1},{1,0},{2,3},{3,2},{4,5},{5,4},{6,7},{7,6},{8,9},{9,8},{10,11... | collective-permute-start | bytes 196616 | tf_op jit(solution)/shard_map/coarse_step/ppermute | solution.py:382
  68.0 6.5 %collective-permute-start.7 = (f32[64,256]{1,0:T(8,128)S(1)}, f32[64,256]{1,0:T(8,128)S(1)}, u32[]{:S(2)}, u32[]{:S(2)}) collective-permute-start(f32[64,256]{1,0:T(8,128)S(1)} %get-tuple-element.25), channel_id=1, source_target_pairs={{1,2},{3,4},{5,6},{7,8},{9,10},{11,12},{13,14},{15,0},{2,1},{4,3},... | collective-permute-start | bytes 196616 | tf_op jit(solution)/shard_map/coarse_step/ppermute | solution.py:382
  74.5 5.8 %collective-permute-start.10 = (bf16[1,64,128]{2,1,0:T(8,128)(2,1)S(1)}, bf16[1,64,128]{2,1,0:T(8,128)(2,1)S(1)}, u32[]{:S(2)}, u32[]{:S(2)}) collective-permute-start(bf16[1,64,128]{2,1,0:T(8,128)(2,1)S(1)} %fusion.4), channel_id=1, source_target_pairs={{0,12},{1,13},{2,14},{3,15},{4,8},{5,9},{6,10},{7,11},{8,4},{9,5},... | collective-permute-start | bytes 49160 | tf_op jit(solution)/shard_map/top_step/ppermute | solution.py:396
  74.6 5.7 %collective-permute-start.9 = (bf16[1,64,128]{2,1,0:T(8,128)(2,1)S(1)}, bf16[1,64,128]{2,1,0:T(8,128)(2,1)S(1)}, u32[]{:S(2)}, u32[]{:S(2)}) collective-permute-start(bf16[1,64,128]{2,1,0:T(8,128)(2,1)S(1)} %fusion.4), channel_id=1, source_target_pairs={{0,8},{1,9},{2,10},{3,11},{4,12},{5,13},{6,14},{7,15},{8,0},{9,1},... | collective-permute-start | bytes 49160 | tf_op jit(solution)/shard_map/top_step/ppermute | solution.py:396
  74.7 6.0 %collective-permute-start.8 = (bf16[1,64,128]{2,1,0:T(8,128)(2,1)S(1)}, bf16[1,64,128]{2,1,0:T(8,128)(2,1)S(1)}, u32[]{:S(2)}, u32[]{:S(2)}) collective-permute-start(bf16[1,64,128]{2,1,0:T(8,128)(2,1)S(1)} %fusion.4), channel_id=1, source_target_pairs={{0,4},{1,5},{2,6},{3,7},{4,0},{5,1},{6,2},{7,3},{8,12},{9,13},{10,... | collective-permute-start | bytes 49160 | tf_op jit(solution)/shard_map/top_step/ppermute | solution.py:396
  80.7 5.4 %collective-permute-start.13 = (bf16[4,64,128]{2,1,0:T(8,128)(2,1)S(1)}, bf16[4,64,128]{2,1,0:T(8,128)(2,1)S(1)}, u32[]{:S(2)}, u32[]{:S(2)}) collective-permute-start(bf16[4,64,128]{2,1,0:T(8,128)(2,1)S(1)} %get-tuple-element.29), channel_id=1, source_target_pairs={{0,3},{1,2},{2,1},{3,0},{4,7},{5,6},{6,5},{7,4},{8,11},{9,10},{10,... | collective-permute-start | bytes 196616 | tf_op jit(solution)/shard_map/top_step/ppermute | solution.py:396
  82.8 4.3 %collective-permute-start.12 = (bf16[4,64,128]{2,1,0:T(8,128)(2,1)S(1)}, bf16[4,64,128]{2,1,0:T(8,128)(2,1)S(1)}, u32[]{:S(2)}, u32[]{:S(2)}) collective-permute-start(bf16[4,64,128]{2,1,0:T(8,128)(2,1)S(1)} %get-tuple-element.29), channel_id=1, source_target_pairs={{0,2},{1,3},{2,0},{3,1},{4,6},{5,7},{6,4},{7,5},{8,10},{9,11},{10,... | collective-permute-start | bytes 196616 | tf_op jit(solution)/shard_map/top_step/ppermute | solution.py:396
  82.8 4.3 %collective-permute-start.11 = (bf16[4,64,128]{2,1,0:T(8,128)(2,1)S(1)}, bf16[4,64,128]{2,1,0:T(8,128)(2,1)S(1)}, u32[]{:S(2)}, u32[]{:S(2)}) collective-permute-start(bf16[4,64,128]{2,1,0:T(8,128)(2,1)S(1)} %get-tuple-element.29), channel_id=1, source_target_pairs={{0,1},{1,0},{2,3},{3,2},{4,5},{5,4},{6,7},{7,6},{8,9},{9,8},{10,11... | collective-permute-start | bytes 196616 | tf_op jit(solution)/shard_map/top_step/ppermute | solution.py:396
  (12 other events, 9.9 us)

commit v3 on v2

--- a/solution.py
+++ b/solution.py
@@ -13,10 +13,8 @@
 LANES = 128
 GROUP = 4
 SPLIT = (64, 192, 256, 384)
-VMEM_LIMIT = 52 * 2**20
-whole_vmem = pl.BlockSpec(memory_space=pltpu.VMEM)
-whole_smem = pl.BlockSpec(memory_space=pltpu.SMEM)
-left_in_hbm = pl.BlockSpec(memory_space=pl.ANY)
+VMEM_LIMIT = 20 * 2**20
+whole_vmem, whole_smem, left_in_hbm = "vmem", "smem", "any"
 
 
 def mm(a, b):
@@ -71,18 +69,10 @@
     spread_of[...] = jnp.where(same, 1.0 / LANES, 0.0).astype(bf16)
 
 
-weight_scratch = [pltpu.VMEM((2 * LANES, 2 * LANES), bf16)] * 3
-
-
-weight_specs = [whole_vmem] * 5
-
-
-def at_level(kernel, level, first):
-    def with_level(*refs):
-        one = [ref.at[level] for ref in refs[first : first + len(weight_specs)]]
-        kernel(*refs[:first], *one, *refs[first + len(weight_specs) :])
-
-    return with_level
+weight_scratch = [pltpu.VMEM((2 * LANES, 2 * LANES), bf16)] * 4
+
+
+weight_specs = ["level"] * 5
 
 
 def edge_first(picks, receiver_part, edge_rows, sender_part, w_edge):
@@ -115,24 +105,35 @@
     b_ref[...] = buffer[aligned(count * (1 - place_ref[0]), count), :].astype(bf16)
 
 
-def fill_tables(x_ref, place_ref, from_a, from_b, edge_in, table, receiver_part):
-    count = x_ref.shape[0]
-    border = from_a.shape[0]
-    both = mm(x_ref[...], jnp.concatenate([edge_in[:LANES, :], edge_in[LANES : 2 * LANES, :]], axis=1))
+def fill_table(x_ref, place_ref, from_a, from_b, edge_in, table, receiver_part, w_pairs):
+    w_s = edge_in[:LANES, :]
+    w_pairs[...] = jnp.zeros_like(w_pairs)
+    w_pairs[:LANES, :LANES] = w_s
+    w_pairs[LANES:, LANES:] = w_s
+
+    count, border = x_ref.shape[0], from_a.shape[0]
+    half = border // 2
+    both = mm(x_ref[...], jnp.concatenate([w_s, edge_in[LANES : 2 * LANES, :]], axis=1))
     table[:count, :] = both[:, :LANES]
     receiver_part[...] = both[:, LANES:].astype(bf16)
-    w_s = edge_in[:LANES, :]
-    table[aligned(count + place_ref[0] * border, border), :] = mm(from_a[...], w_s)
-    table[aligned(count + (1 - place_ref[0]) * border, border), :] = mm(from_b[...], w_s) * place_ref[1].astype(f32)
+    for rows, first, scale in (
+        (from_a, count + place_ref[0] * border, None),
+        (from_b, count + (1 - place_ref[0]) * border, place_ref[1].astype(f32)),
+    ):
+        both = mm(side_by_side(rows[...]), w_pairs[...])
+        if scale is not None:
+            both = both * scale
+        table[aligned(first, half), :] = both[:, :LANES]
+        table[aligned(first + half, half), :] = both[:, LANES:]
 
 
 def fine_kernel(
     place_ref, pool_index, sender_ref, edge_ref, x_ref, from_a, from_b, receiver_ref, parent_ref,
     weight_ref, edge_in, edge_out, node_in, node_out, gain_ref,
     new_ref, sums_ref, a_ref, b_ref,
-    table, receiver_part, edges, new32, buffer, aggregate, node_hidden,
+    table, receiver_part, new32, buffer, aggregate, node_hidden,
     gathered0, gathered1, hidden0, hidden1, message0, message1,
-    index0, index1, index2, index3, edge_sem, index_sem, w_out, w_node_out, spread_of,
+    index0, index1, index2, index3, index_sem, w_out, w_node_out, spread_of, w_pairs,
 ):
     gathered, hidden, message = (gathered0, gathered1), (hidden0, hidden1), (message0, message1)
     indices = (index0, index1, index2, index3)
@@ -140,12 +141,7 @@
     groups, _, group_nodes = parent_ref.shape
     nodes = group_nodes // GROUP
     blocks = groups * GROUP
-    chunk = GROUP * block
     gain, node_gain = gain_ref[0:1, :], gain_ref[1:2, :]
-
-    def edge_copy(g):
-        at = aligned(g * chunk, chunk)
-        return pltpu.make_async_copy(edge_ref.at[at, :], edges.at[at, :], edge_sem.at[g])
 
     def index_copy(t, k):
         at = aligned(jnp.minimum(t, blocks - 1) * block, block)
@@ -156,10 +152,8 @@
 
     for k in range(GROUP):
         index_copy(k, k).start()
-    for g in range(groups):
-        edge_copy(g).start()
     fill_weights(edge_out, node_out, w_out, w_node_out, spread_of)
-    fill_tables(x_ref, place_ref, from_a, from_b, edge_in, table, receiver_part)
+    fill_table(x_ref, place_ref, from_a, from_b, edge_in, table, receiver_part, w_pairs)
     sums_ref[...] = jnp.zeros_like(sums_ref)
     index_copy(0, 0).wait()
     gather_block(0, gathered0)
@@ -170,8 +164,6 @@
         return match_rows(jnp.where(slot < place_ref[2], receiver_ref[t] - t * nodes, -1), nodes)
 
     def group_step(g, last):
-        if not last:
-            edge_copy(g).wait()
         for k in range(GROUP):
             t = g * GROUP + k
             here, before = k % 2, (k + 1) % 2
@@ -193,7 +185,7 @@
                 if not last:
                     keep["before"] = mm_first(
                         keep["picks"], receiver_part[aligned(t * nodes, nodes), :]
-                    ) + mm(edges[aligned(t * block, block), :], edge_in[2 * LANES :, :])
+                    ) + mm(edge_ref[aligned(t * block, block), :], edge_in[2 * LANES :, :])
                 if not last or k < 1:
                     keep["centred"] = mm(hidden[before][...], w_out[...])
                 if k == 2:
@@ -277,12 +269,12 @@
     place_ref, sender_ref, edge_ref, x_ref, from_a, from_b, receiver_ref, parent_ref, weight_ref,
     edge_in, edge_out, node_in, node_out, gain_ref,
     new_ref, own_ref, a_ref, b_ref,
-    table, receiver_part, gathered, aggregate, shares_sum, w_out, w_node_out, spread_of,
+    table, receiver_part, gathered, aggregate, shares_sum, w_out, w_node_out, spread_of, w_pairs,
 ):
     blocks, _, block = receiver_ref.shape
     nodes = x_ref.shape[0] // blocks
     fill_weights(edge_out, node_out, w_out, w_node_out, spread_of)
-    fill_tables(x_ref, place_ref, from_a, from_b, edge_in, table, receiver_part)
+    fill_table(x_ref, place_ref, from_a, from_b, edge_in, table, receiver_part, w_pairs)
     gather_rows(lambda j: sender_ref[j], table, gathered, blocks * block)
     for t in range(blocks):
         at = slice(t * block, (t + 1) * block)
@@ -314,17 +306,10 @@
     place_ref, sender_ref, picks_ref, edge_ref, gathered_in, receiver_ref, parent_ref, coarse_ref,
     fine_ref, edge_in, edge_out, node_in, node_out, gain_ref,
     fine_out, coarse_out,
-    picks, table, top_rows, gathered, picks_sem, w_out, w_node_out, spread_of,
+    table, top_rows, gathered, w_out, w_node_out, spread_of, w_pairs,
 ):
     chunk = coarse_ref.shape[0]
     chunks = fine_ref.shape[0] // chunk
-
-    def picks_copy(i):
-        at = slice(i * chunk, (i + 1) * chunk)
-        return pltpu.make_async_copy(picks_ref.at[at, :], picks.at[at, :], picks_sem.at[i])
-
-    for i in range(chunks):
-        picks_copy(i).start()
     tile = receiver_ref.shape[2]
     share = tile // 2
     nodes = 3 * share
@@ -352,20 +337,25 @@
     coarse = (coarse_ref[...].astype(f32) + up).astype(bf16)
     coarse_out[...] = coarse
     for i in range(chunks):
-        picks_copy(i).wait()
         at = slice(i * chunk, (i + 1) * chunk)
-        fine_out[at, :] = (fine_ref[at, :].astype(f32) + mm(picks[at, :], coarse)).astype(bf16)
-
-
-def call(kernel, name, outs, specs, scratch, operands, flops=0, moved=0):
+        fine_out[at, :] = (fine_ref[at, :].astype(f32) + mm(picks_ref[at, :], coarse)).astype(bf16)
+
+
+def call(kernel, name, outs, kinds, scratch, operands, level=None, us=1.0):
+    def with_level(*refs):
+        kernel(*[
+            ref.at[level] if i < len(kinds) and kinds[i] == "level" else ref for i, ref in enumerate(refs)
+        ])
+
+    spaces = {whole_smem: pltpu.SMEM, left_in_hbm: pl.ANY}
     return pl.pallas_call(
-        kernel,
+        with_level,
         name=name,
         out_shape=outs,
-        in_specs=specs,
-        out_specs=jax.tree.map(lambda _: whole_vmem, outs),
+        in_specs=[pl.BlockSpec(memory_space=spaces.get(kind, pltpu.VMEM)) for kind in kinds],
+        out_specs=jax.tree.map(lambda _: pl.BlockSpec(memory_space=pltpu.VMEM), outs),
         scratch_shapes=scratch,
-        cost_estimate=pl.CostEstimate(flops=flops, bytes_accessed=moved, transcendentals=0),
+        cost_estimate=pl.CostEstimate(flops=int(us * 10**9), bytes_accessed=0, transcendentals=0),
         compiler_params=pltpu.CompilerParams(vmem_limit_bytes=VMEM_LIMIT),
     )(*operands)
 
@@ -428,23 +418,23 @@
             [whole_smem, whole_smem, whole_vmem],
             [pltpu.VMEM((fine_total, LANES), f32), pltpu.VMEM((2 * border, LANES), f32)],
             (place, fine_border, fine_latent),
+            us=3.0,
         )
         from_a, from_b = swap_with_neighbours(for_a, for_b)
         lift_picks = call(
             lift_kernel, "lift_picks", rows_of(fine_total, bf16, coarse_total), [whole_vmem], [],
             (fine_parent.reshape(fine_total // coarse_total, 1, coarse_total),),
-            flops=10**9, moved=fine_total * coarse_total * 2,
+            us=3.0,
         )
 
     with jax.named_scope("fine_step"):
         fine_new, local_sums, for_a, for_b = call(
-            at_level(fine_kernel, 0, 10), "fine_step",
+            fine_kernel, "fine_step",
             [rows_of(fine_total), rows_of(coarse_total, f32, 2 * LANES), rows_of(slots), rows_of(slots)],
-            [whole_smem, whole_smem, left_in_hbm, left_in_hbm] + [whole_vmem] * 6 + weight_specs,
+            [whole_smem, whole_smem, left_in_hbm] + [whole_vmem] * 7 + weight_specs,
             [
                 pltpu.VMEM((fine_total + 2 * border, LANES), f32),
                 pltpu.VMEM((fine_total, LANES), bf16),
-                pltpu.VMEM((edge_total, LANES), bf16),
                 pltpu.VMEM((fine_total, LANES), f32),
                 pltpu.VMEM((2 * slots, LANES), f32),
                 pltpu.VMEM((GROUP * nodes, LANES), bf16),
@@ -453,7 +443,7 @@
             + [pltpu.VMEM((block, LANES), f32)] * 2
             + [pltpu.VMEM((block // 2, 2 * LANES), bf16)] * 4
             + [pltpu.SMEM((block,), jnp.int32)] * GROUP
-            + [pltpu.SemaphoreType.DMA((groups,)), pltpu.SemaphoreType.DMA((GROUP,))]
+            + [pltpu.SemaphoreType.DMA((GROUP,))]
             + weight_scratch,
             (
                 place, pool_rows, fine_sender, fine_edges, fine_latent, from_a, from_b,
@@ -461,6 +451,8 @@
                 fine_weight.reshape(groups, 1, GROUP * nodes),
             )
             + weights,
+            level=0,
+            us=24.0,
         )
         from_a, from_b = swap_with_neighbours(for_a, for_b)
 
@@ -469,7 +461,7 @@
         coarse_in, for_a, for_b = call(
             pool_kernel, "coarse_input",
             [rows_of(coarse_total), rows_of(border1), rows_of(border1)],
-            [whole_smem] * 2 + [whole_vmem] * 5,
+            [whole_smem, whole_smem] + [whole_vmem] * 5,
             [pltpu.VMEM((coarse_total, LANES), f32), pltpu.VMEM((2 * border1, LANES), f32)],
             (
                 place, coarse_border, local_sums, from_a, from_b,
@@ -484,7 +476,7 @@
         blocks1 = edge_total1 // block1
         share = coarse_total // 8
         coarse_new, own, for_a, for_b = call(
-            at_level(coarse_kernel, 1, 9), "coarse_step",
+            coarse_kernel, "coarse_step",
             [rows_of(coarse_total)] + [rows_of(share, f32, 2 * LANES)] * 3,
             [whole_smem, whole_smem] + [whole_vmem] * 7 + weight_specs,
             [
@@ -500,6 +492,8 @@
                 coarse_receiver.reshape(blocks1, 1, block1), coarse_parent[None, :], coarse_weight[None, :],
             )
             + weights,
+            level=1,
+            us=4.0,
         )
         from_a, from_b = swap_with_neighbours(for_a, for_b)
         shares = own + from_a + from_b
@@ -510,15 +504,13 @@
         tile = 2 * share
         window = 3 * tile
         fine_out, coarse_out = call(
-            at_level(top_kernel, 2, 9), "top_step",
+            top_kernel, "top_step",
             [rows_of(fine_total), rows_of(coarse_total)],
-            [whole_smem] * 2 + [left_in_hbm] + [whole_vmem] * 6 + weight_specs,
+            [whole_smem, whole_smem] + [whole_vmem] * 7 + weight_specs,
             [
-                pltpu.VMEM((fine_total, coarse_total), bf16),
                 pltpu.VMEM((count * share, LANES), f32),
                 pltpu.VMEM((count * share, LANES), bf16),
                 pltpu.VMEM((window, LANES), f32),
-                pltpu.SemaphoreType.DMA((fine_total // coarse_total,)),
             ]
             + weight_scratch,
             (
@@ -527,6 +519,8 @@
                 fine_new,
             )
             + weights,
+            level=2,
+            us=5.0,
         )
     return (fine_out, coarse_out)
 

time: 94.5 us -> 80.7 us (0.85)
  local copies, waits for them, and re-layouts: 11.3 us -> 2.17 us
  Pallas kernels: 40.9 us -> 35 us
  waiting for transfers between devices: 13 us -> 15 us
    unnamed x60 -> x50, local copies, waits for them, and re-layouts: 11.2 us -> 2.06 us
    pallas_call x6, Pallas kernels: 40.9 us -> 35 us  [call(): pl.pallas_call(with_level, name=name, out_shape=outs, in_specs=[pl.BlockS...]
    ppermute x6, waiting for transfers between devices: 2.65 us -> 4.62 us  [gather_all(): lax.ppermute(blocks, 'dom', [(i, i ^ j * stride) for i in range(count)])]
  transfers between devices with their start and end apart: 14 -> 14, of which waited for: 7 -> 8; matrix products, arithmetic and copies ran while one was open for 0% -> 0% of each run, Pallas kernels for 3% -> 1%
where the time goes in v3:
time: 80.7 us; the launch traced here: 80.5 us
  Pallas kernels  35 us (43%)
  starting transfers between devices  26.6 us (33%)
  waiting for transfers between devices  15 us (19%)
  local copies, waits for them, and re-layouts  2.17 us (3%)
  between operations  1.71 us (2%)
    pallas_call x6, Pallas kernels, call(): pl.pallas_call(with_level, name=name, out_shape=outs, in_specs=[pl.BlockS...  35 us
    ppermute x4, starting transfers between devices, swap_with_neighbours(): lax.ppermute(for_b, 'dom', pairs_b)  19.1 us
    ppermute x4, waiting for transfers between devices, swap_with_neighbours(): lax.ppermute(for_b, 'dom', pairs_b)  10.3 us
    ppermute x6, starting transfers between devices, gather_all(): lax.ppermute(blocks, 'dom', [(i, i ^ j * stride) for i in range(count)])  6.75 us
    ppermute x6, waiting for transfers between devices, gather_all(): lax.ppermute(blocks, 'dom', [(i, i ^ j * stride) for i in range(count)])  4.62 us
    unnamed x50, local copies, waits for them, and re-layouts  2.06 us
  transfers between devices with their start and end apart: 14, of which 8 were waited for; matrix products, arithmetic and copies ran while one was open for 0% of the time, Pallas kernels for 1%

profile of v3, /device:TPU:0, one launch (start us, length us, event | category | flops | bytes accessed | tf_op | source)
XLA Modules:
  0.0 80.5 jit_solution(17552656559112968658)
XLA Ops:
  1.3 0.1 stack.43.refs_0_
  1.4 1.2 %copy-done.1 = bf16[4096,128]{1,0:T(8,128)(2,1)S(1)} copy-done((bf16[4096,128]{1,0:T(8,128)(2,1)S(1)}, bf16[4096,128]{1,0:T(8,128)(2,1)}, u32[]{:S(2)}) %copy-start.1) | copy-done | bytes 1048600
  2.6 0.7 copy-done.13
  3.3 0.0 copy-start.9
  3.4 0.0 copy-start.10
  3.4 1.9 %border_rows.1 = (bf16[1024,128]{1,0:T(8,128)(2,1)S(1)}, bf16[1024,128]{1,0:T(8,128)(2,1)S(1)}) custom-call(s32[5]{0:T(128)S(1)} %stack.43.refs_0_, s32[1,2,1024]{2,1,0:T(2,128)S(1)} %copy-done.13, bf16[4096,128]{1,0:T(8,128)(2,1)S(1)} %copy-done.1), custom_call_target="tpu_custom_call" | custom-call | flops 3000000000 | tf_op jit(solution)/shard_map/fine_border_rows/border_rows/pallas_call | solution.py:351
  5.4 0.5 collective-permute-start
  5.9 5.7 %collective-permute-start.1 = (bf16[1024,128]{1,0:T(8,128)(2,1)S(1)}, bf16[1024,128]{1,0:T(8,128)(2,1)S(1)}, u32[]{:S(2)}, u32[]{:S(2)}) collective-permute-start(bf16[1024,128]{1,0:T(8,128)(2,1)S(1)} %get-tuple-element.16), channel_id=1, source_target_pairs={{1,2},{3,4},{5,6},{7,8},{9,10},{11,12},{13,14},{15,0},{2,1},{4,3},... | collective-permute-start | bytes 786440 | tf_op jit(solution)/shard_map/fine_border_rows/ppermute | solution.py:372
  11.5 4.1 %collective-permute-done.1.refs_6_ = bf16[1024,128]{1,0:T(8,128)(2,1)S(1)} collective-permute-done((bf16[1024,128]{1,0:T(8,128)(2,1)S(1)}, bf16[1024,128]{1,0:T(8,128)(2,1)S(1)}, u32[]{:S(2)}, u32[]{:S(2)}) %collective-permute-start.1) | collective-permute-done | bytes 262176 | tf_op jit(solution)/shard_map/fine_border_rows/ppermute | solution.py:372
  15.8 22.2 %fine_step.1 = (bf16[4096,128]{1,0:T(8,128)(2,1)S(1)}, f32[512,256]{1,0:T(8,128)S(1)}, bf16[512,128]{1,0:T(8,128)(2,1)S(1)}, bf16[512,128]{1,0:T(8,128)(2,1)S(1)}) custom-call(s32[5]{0:T(128)S(1)} %stack.43.refs_0_, s32[1,2,512]{2,1,0:T(2,128)S(1)} %copy-done.18, s32[16384]{0:T(1024)S(1)} %copy-done.9, bf16[16384,128]{1,0:T(8,128)(2,1)S(1)} %copy-done, ...), custom_call_target="tpu_custom_call" | custom-call | flops 24000000000 | tf_op jit(solution)/shard_map/fine_step/fine_step/pallas_call | solution.py:351
  38.0 0.1 collective-permute-start.2
  38.1 4.5 %collective-permute-start.3 = (bf16[512,128]{1,0:T(8,128)(2,1)S(1)}, bf16[512,128]{1,0:T(8,128)(2,1)S(1)}, u32[]{:S(2)}, u32[]{:S(2)}) collective-permute-start(bf16[512,128]{1,0:T(8,128)(2,1)S(1)} %get-tuple-element.19), channel_id=1, source_target_pairs={{1,2},{3,4},{5,6},{7,8},{9,10},{11,12},{13,14},{15,0},{2,1},{4,3},... | collective-permute-start | bytes 393224 | tf_op jit(solution)/shard_map/fine_step/ppermute | solution.py:372
  42.6 2.6 %collective-permute-done.3.refs_4_ = bf16[512,128]{1,0:T(8,128)(2,1)S(1)} collective-permute-done((bf16[512,128]{1,0:T(8,128)(2,1)S(1)}, bf16[512,128]{1,0:T(8,128)(2,1)S(1)}, u32[]{:S(2)}, u32[]{:S(2)}) %collective-permute-start.3) | collective-permute-done | bytes 131104 | tf_op jit(solution)/shard_map/fine_step/ppermute | solution.py:372
  45.3 1.1 %coarse_input.1 = (bf16[512,128]{1,0:T(8,128)(2,1)S(1)}, bf16[128,128]{1,0:T(8,128)(2,1)S(1)}, bf16[128,128]{1,0:T(8,128)(2,1)S(1)}) custom-call(s32[5]{0:T(128)S(1)} %stack.43.refs_0_, s32[1,2,128]{2,1,0:T(2,128)S(1)} %copy-done.22, f32[512,256]{1,0:T(8,128)S(1)} %get-tuple-element.17.refs_2_, bf16[512,128]{1,0:T(8,128)(2,1)S(1)} %collective-permute-done.2.refs_3_, ...), custom_call_target="tpu_custom_call" | custom-call | flops 1000000000 | tf_op jit(solution)/shard_map/coarse_input/coarse_input/pallas_call | solution.py:351
  46.4 0.1 collective-permute-start.4
  46.5 4.5 %collective-permute-start.5 = (bf16[128,128]{1,0:T(8,128)(2,1)S(1)}, bf16[128,128]{1,0:T(8,128)(2,1)S(1)}, u32[]{:S(2)}, u32[]{:S(2)}) collective-permute-start(bf16[128,128]{1,0:T(8,128)(2,1)S(1)} %get-tuple-element.22), channel_id=1, source_target_pairs={{1,2},{3,4},{5,6},{7,8},{9,10},{11,12},{13,14},{15,0},{2,1},{4,3},... | collective-permute-start | bytes 98312 | tf_op jit(solution)/shard_map/coarse_input/ppermute | solution.py:372
  51.0 1.6 %collective-permute-done.5.refs_5_ = bf16[128,128]{1,0:T(8,128)(2,1)S(1)} collective-permute-done((bf16[128,128]{1,0:T(8,128)(2,1)S(1)}, bf16[128,128]{1,0:T(8,128)(2,1)S(1)}, u32[]{:S(2)}, u32[]{:S(2)}) %collective-permute-start.5) | collective-permute-done | bytes 32800 | tf_op jit(solution)/shard_map/coarse_input/ppermute | solution.py:372
  52.6 4.0 %coarse_step.1 = (bf16[512,128]{1,0:T(8,128)(2,1)S(1)}, f32[64,256]{1,0:T(8,128)S(1)}, f32[64,256]{1,0:T(8,128)S(1)}, f32[64,256]{1,0:T(8,128)S(1)}) custom-call(s32[5]{0:T(128)S(1)} %stack.43.refs_0_, s32[2048]{0:T(1024)S(1)} %copy-done.14, bf16[2048,128]{1,0:T(8,128)(2,1)S(1)} %copy-done.3, bf16[512,128]{1,0:T(8,128)(2,1)S(1)} %get-tuple-element.20.refs_3_, ...), custom_call_target="tpu_custom_call" | custom-call | flops 4000000000 | tf_op jit(solution)/shard_map/coarse_step/coarse_step/pallas_call | solution.py:351
  56.7 0.1 collective-permute-start.6
  56.7 4.5 %collective-permute-start.7 = (f32[64,256]{1,0:T(8,128)S(1)}, f32[64,256]{1,0:T(8,128)S(1)}, u32[]{:S(2)}, u32[]{:S(2)}) collective-permute-start(f32[64,256]{1,0:T(8,128)S(1)} %get-tuple-element.25), channel_id=1, source_target_pairs={{1,2},{3,4},{5,6},{7,8},{9,10},{11,12},{13,14},{15,0},{2,1},{4,3},... | collective-permute-start | bytes 196616 | tf_op jit(solution)/shard_map/coarse_step/ppermute | solution.py:372
  61.2 2.0 %collective-permute-done.7 = f32[64,256]{1,0:T(8,128)S(1)} collective-permute-done((f32[64,256]{1,0:T(8,128)S(1)}, f32[64,256]{1,0:T(8,128)S(1)}, u32[]{:S(2)}, u32[]{:S(2)}) %collective-permute-start.7) | collective-permute-done | bytes 65568 | tf_op jit(solution)/shard_map/coarse_step/ppermute | solution.py:372
  63.3 0.1 collective-permute-start.10
  63.3 0.1 collective-permute-start.9
  63.4 4.3 %collective-permute-start.8 = (bf16[1,64,128]{2,1,0:T(8,128)(2,1)S(1)}, bf16[1,64,128]{2,1,0:T(8,128)(2,1)S(1)}, u32[]{:S(2)}, u32[]{:S(2)}) collective-permute-start(bf16[1,64,128]{2,1,0:T(8,128)(2,1)S(1)} %fusion.4), channel_id=1, source_target_pairs={{0,4},{1,5},{2,6},{3,7},{4,0},{5,1},{6,2},{7,3},{8,12},{9,13},{10,... | collective-permute-start | bytes 49160 | tf_op jit(solution)/shard_map/top_step/ppermute | solution.py:386
  67.7 1.3 %collective-permute-done.10 = bf16[1,64,128]{2,1,0:T(8,128)(2,1)S(1)} collective-permute-done((bf16[1,64,128]{2,1,0:T(8,128)(2,1)S(1)}, bf16[1,64,128]{2,1,0:T(8,128)(2,1)S(1)}, u32[]{:S(2)}, u32[]{:S(2)}) %collective-permute-start.10) | collective-permute-done | bytes 16416 | tf_op jit(solution)/shard_map/top_step/ppermute | solution.py:386
  69.0 0.4 collective-permute-done.8
  69.5 2.1 %collective-permute-start.13 = (bf16[4,64,128]{2,1,0:T(8,128)(2,1)S(1)}, bf16[4,64,128]{2,1,0:T(8,128)(2,1)S(1)}, u32[]{:S(2)}, u32[]{:S(2)}) collective-permute-start(bf16[4,64,128]{2,1,0:T(8,128)(2,1)S(1)} %get-tuple-element.29), channel_id=1, source_target_pairs={{0,3},{1,2},{2,1},{3,0},{4,7},{5,6},{6,5},{7,4},{8,11},{9,10},{10,... | collective-permute-start | bytes 196616 | tf_op jit(solution)/shard_map/top_step/ppermute | solution.py:386
  71.6 0.2 collective-permute-start.11
  71.8 1.1 %lift_picks.1.refs_2_ = bf16[4096,512]{1,0:T(8,128)(2,1)S(1)} custom-call(s32[8,1,512]{2,1,0:T(1,128)S(1)} %bitcast.30), custom_call_target="tpu_custom_call" | custom-call | flops 3000000000 | tf_op jit(solution)/shard_map/fine_border_rows/lift_picks/pallas_call | solution.py:351
  72.9 0.6 collective-permute-done.13
  73.6 2.3 %collective-permute-done.12 = bf16[4,64,128]{2,1,0:T(8,128)(2,1)S(1)} collective-permute-done((bf16[4,64,128]{2,1,0:T(8,128)(2,1)S(1)}, bf16[4,64,128]{2,1,0:T(8,128)(2,1)S(1)}, u32[]{:S(2)}, u32[]{:S(2)}) %collective-permute-start.12) | collective-permute-done | bytes 65568 | tf_op jit(solution)/shard_map/top_step/ppermute | solution.py:386
  76.0 4.6 %top_step.1 = (bf16[4096,128]{1,0:T(8,128)(2,1)}, bf16[512,128]{1,0:T(8,128)(2,1)}) custom-call(s32[5]{0:T(128)S(1)} %stack.43.refs_0_, s32[2048]{0:T(1024)S(1)} %copy-done.16, bf16[4096,512]{1,0:T(8,128)(2,1)S(1)} %lift_picks.1.refs_2_, bf16[2048,128]{1,0:T(8,128)(2,1)S(1)} %copy-done.4, bf16[1024,128]{1,0:T(8,128)(2,1)S(1)} %bitcast.26, ...), custom_call_target="tpu_custom_call" | custom-call | flops 5000000000 | tf_op jit(solution)/shard_map/top_step/top_step/pallas_call | solution.py:351
  (61 shorter events, 0.3 us)
Async XLA Ops:
  3.3 12.3 %copy-start = (bf16[16384,128]{1,0:T(8,128)(2,1)S(1)}, bf16[16384,128]{1,0:T(8,128)(2,1)}, u32[]{:S(2)}) copy-start(bf16[16384,128]{1,0:T(8,128)(2,1)} %refs_3_.2) | copy-start | bytes 12582916
  3.3 12.3 %copy-start.2 = (bf16[4096,128]{1,0:T(8,128)(2,1)S(1)}, bf16[4096,128]{1,0:T(8,128)(2,1)}, u32[]{:S(2)}) copy-start(bf16[4096,128]{1,0:T(8,128)(2,1)} %refs_4_.1) | copy-start | bytes 3145732
  3.3 12.3 %copy-start.5 = (bf16[3,384,128]{2,1,0:T(8,128)(2,1)S(1)}, bf16[3,384,128]{2,1,0:T(8,128)(2,1)}, u32[]{:S(2)}) copy-start(bf16[3,384,128]{2,1,0:T(8,128)(2,1)} %refs_9_.3) | copy-start | bytes 884740
  3.3 12.3 %copy-start.6 = (bf16[3,256,128]{2,1,0:T(8,128)(2,1)S(1)}, bf16[3,256,128]{2,1,0:T(8,128)(2,1)}, u32[]{:S(2)}) copy-start(bf16[3,256,128]{2,1,0:T(8,128)(2,1)} %refs_11_.5) | copy-start | bytes 589828
  3.3 12.3 %copy-start.7 = (bf16[3,128,128]{2,1,0:T(8,128)(2,1)S(1)}, bf16[3,128,128]{2,1,0:T(8,128)(2,1)}, u32[]{:S(2)}) copy-start(bf16[3,128,128]{2,1,0:T(8,128)(2,1)} %refs_10_.5) | copy-start | bytes 294916
  3.3 12.3 %copy-start.8 = (bf16[3,128,128]{2,1,0:T(8,128)(2,1)S(1)}, bf16[3,128,128]{2,1,0:T(8,128)(2,1)}, u32[]{:S(2)}) copy-start(bf16[3,128,128]{2,1,0:T(8,128)(2,1)} %refs_12_.5) | copy-start | bytes 294916
  3.3 12.3 %copy-start.9 = (s32[16384]{0:T(1024)S(1)}, s32[16384]{0:T(1024)}, u32[]{:S(2)}) copy-start(s32[16384]{0:T(1024)} %refs_2_.4) | copy-start | bytes 196612
  3.4 12.3 %copy-start.10 = (s32[16384]{0:T(1024)S(1)}, s32[16384]{0:T(1024)}, u32[]{:S(2)}) copy-start(s32[16384]{0:T(1024)} %param.28) | copy-start | bytes 196612
  3.4 12.3 %copy-start.11 = (s32[4096]{0:T(1024)S(1)}, s32[4096]{0:T(1024)}, u32[]{:S(2)}) copy-start(s32[4096]{0:T(1024)} %param.35) | copy-start | bytes 49156
  3.4 12.3 %copy-start.12 = (s32[4096]{0:T(1024)S(1)}, s32[4096]{0:T(1024)}, u32[]{:S(2)}) copy-start(s32[4096]{0:T(1024)} %param.34) | copy-start | bytes 49156
  5.4 6.2 %collective-permute-start = (bf16[1024,128]{1,0:T(8,128)(2,1)S(1)}, bf16[1024,128]{1,0:T(8,128)(2,1)S(1)}, u32[]{:S(2)}, u32[]{:S(2)}) collective-permute-start(bf16[1024,128]{1,0:T(8,128)(2,1)S(1)} %get-tuple-element.15), channel_id=1, source_target_pairs={{0,1},{1,0},{2,3},{3,2},{4,5},{5,4},{6,7},{7,6},{8,9},{9,8},{10,11... | collective-permute-start | bytes 786440 | tf_op jit(solution)/shard_map/fine_border_rows/ppermute | solution.py:372
  5.9 9.8 %collective-permute-start.1 = (bf16[1024,128]{1,0:T(8,128)(2,1)S(1)}, bf16[1024,128]{1,0:T(8,128)(2,1)S(1)}, u32[]{:S(2)}, u32[]{:S(2)}) collective-permute-start(bf16[1024,128]{1,0:T(8,128)(2,1)S(1)} %get-tuple-element.16), channel_id=1, source_target_pairs={{1,2},{3,4},{5,6},{7,8},{9,10},{11,12},{13,14},{15,0},{2,1},{4,3},... | collective-permute-start | bytes 786440 | tf_op jit(solution)/shard_map/fine_border_rows/ppermute | solution.py:372
  15.7 26.9 %copy-start.23 = (s32[1,2,512]{2,1,0:T(2,128)S(1)}, s32[1,2,512]{2,1,0:T(2,128)}, u32[]{:S(2)}) copy-start(s32[1,2,512]{2,1,0:T(2,128)} %param.32) | copy-start | bytes 12292
  15.7 26.9 %copy-start.24 = (s32[1,2,512]{2,1,0:T(2,128)S(1)}, s32[1,2,512]{2,1,0:T(2,128)}, u32[]{:S(2)}) copy-start(s32[1,2,512]{2,1,0:T(2,128)} %param.33) | copy-start | bytes 12292
  15.8 29.5 %copy-start.22 = (s32[1,2,128]{2,1,0:T(2,128)S(1)}, s32[1,2,128]{2,1,0:T(2,128)}, u32[]{:S(2)}) copy-start(s32[1,2,128]{2,1,0:T(2,128)} %refs_1_.7) | copy-start | bytes 3076
  15.8 36.8 %copy-start.3 = (bf16[2048,128]{1,0:T(8,128)(2,1)S(1)}, bf16[2048,128]{1,0:T(8,128)(2,1)}, u32[]{:S(2)}) copy-start(bf16[2048,128]{1,0:T(8,128)(2,1)} %refs_2_.5) | copy-start | bytes 1572868
  15.8 36.8 %copy-start.14 = (s32[2048]{0:T(1024)S(1)}, s32[2048]{0:T(1024)}, u32[]{:S(2)}) copy-start(s32[2048]{0:T(1024)} %refs_1_.8) | copy-start | bytes 24580
  15.8 36.8 %copy-start.15 = (s32[2048]{0:T(1024)S(1)}, s32[2048]{0:T(1024)}, u32[]{:S(2)}) copy-start(s32[2048]{0:T(1024)} %param.38) | copy-start | bytes 24580
  15.8 36.8 %copy-start.20 = (s32[512]{0:T(512)S(1)}, s32[512]{0:T(512)}, u32[]{:S(2)}) copy-start(s32[512]{0:T(512)} %param.41) | copy-start | bytes 6148
  15.8 36.8 %copy-start.21 = (s32[512]{0:T(512)S(1)}, s32[512]{0:T(512)}, u32[]{:S(2)}) copy-start(s32[512]{0:T(512)} %param.40) | copy-start | bytes 6148
  38.0 4.6 %collective-permute-start.2 = (bf16[512,128]{1,0:T(8,128)(2,1)S(1)}, bf16[512,128]{1,0:T(8,128)(2,1)S(1)}, u32[]{:S(2)}, u32[]{:S(2)}) collective-permute-start(bf16[512,128]{1,0:T(8,128)(2,1)S(1)} %get-tuple-element.18), channel_id=1, source_target_pairs={{0,1},{1,0},{2,3},{3,2},{4,5},{5,4},{6,7},{7,6},{8,9},{9,8},{10,11... | collective-permute-start | bytes 393224 | tf_op jit(solution)/shard_map/fine_step/ppermute | solution.py:372
  38.1 7.2 %collective-permute-start.3 = (bf16[512,128]{1,0:T(8,128)(2,1)S(1)}, bf16[512,128]{1,0:T(8,128)(2,1)S(1)}, u32[]{:S(2)}, u32[]{:S(2)}) collective-permute-start(bf16[512,128]{1,0:T(8,128)(2,1)S(1)} %get-tuple-element.19), channel_id=1, source_target_pairs={{1,2},{3,4},{5,6},{7,8},{9,10},{11,12},{13,14},{15,0},{2,1},{4,3},... | collective-permute-start | bytes 393224 | tf_op jit(solution)/shard_map/fine_step/ppermute | solution.py:372
  46.4 4.6 %collective-permute-start.4 = (bf16[128,128]{1,0:T(8,128)(2,1)S(1)}, bf16[128,128]{1,0:T(8,128)(2,1)S(1)}, u32[]{:S(2)}, u32[]{:S(2)}) collective-permute-start(bf16[128,128]{1,0:T(8,128)(2,1)S(1)} %get-tuple-element.21), channel_id=1, source_target_pairs={{0,1},{1,0},{2,3},{3,2},{4,5},{5,4},{6,7},{7,6},{8,9},{9,8},{10,11... | collective-permute-start | bytes 98312 | tf_op jit(solution)/shard_map/coarse_input/ppermute | solution.py:372
  46.5 6.1 %collective-permute-start.5 = (bf16[128,128]{1,0:T(8,128)(2,1)S(1)}, bf16[128,128]{1,0:T(8,128)(2,1)S(1)}, u32[]{:S(2)}, u32[]{:S(2)}) collective-permute-start(bf16[128,128]{1,0:T(8,128)(2,1)S(1)} %get-tuple-element.22), channel_id=1, source_target_pairs={{1,2},{3,4},{5,6},{7,8},{9,10},{11,12},{13,14},{15,0},{2,1},{4,3},... | collective-permute-start | bytes 98312 | tf_op jit(solution)/shard_map/coarse_input/ppermute | solution.py:372
  56.7 4.6 %collective-permute-start.6 = (f32[64,256]{1,0:T(8,128)S(1)}, f32[64,256]{1,0:T(8,128)S(1)}, u32[]{:S(2)}, u32[]{:S(2)}) collective-permute-start(f32[64,256]{1,0:T(8,128)S(1)} %get-tuple-element.24), channel_id=1, source_target_pairs={{0,1},{1,0},{2,3},{3,2},{4,5},{5,4},{6,7},{7,6},{8,9},{9,8},{10,11... | collective-permute-start | bytes 196616 | tf_op jit(solution)/shard_map/coarse_step/ppermute | solution.py:372
  56.7 6.5 %collective-permute-start.7 = (f32[64,256]{1,0:T(8,128)S(1)}, f32[64,256]{1,0:T(8,128)S(1)}, u32[]{:S(2)}, u32[]{:S(2)}) collective-permute-start(f32[64,256]{1,0:T(8,128)S(1)} %get-tuple-element.25), channel_id=1, source_target_pairs={{1,2},{3,4},{5,6},{7,8},{9,10},{11,12},{13,14},{15,0},{2,1},{4,3},... | collective-permute-start | bytes 196616 | tf_op jit(solution)/shard_map/coarse_step/ppermute | solution.py:372
  63.3 5.7 %collective-permute-start.10 = (bf16[1,64,128]{2,1,0:T(8,128)(2,1)S(1)}, bf16[1,64,128]{2,1,0:T(8,128)(2,1)S(1)}, u32[]{:S(2)}, u32[]{:S(2)}) collective-permute-start(bf16[1,64,128]{2,1,0:T(8,128)(2,1)S(1)} %fusion.4), channel_id=1, source_target_pairs={{0,12},{1,13},{2,14},{3,15},{4,8},{5,9},{6,10},{7,11},{8,4},{9,5},... | collective-permute-start | bytes 49160 | tf_op jit(solution)/shard_map/top_step/ppermute | solution.py:386
  63.3 5.7 %collective-permute-start.9 = (bf16[1,64,128]{2,1,0:T(8,128)(2,1)S(1)}, bf16[1,64,128]{2,1,0:T(8,128)(2,1)S(1)}, u32[]{:S(2)}, u32[]{:S(2)}) collective-permute-start(bf16[1,64,128]{2,1,0:T(8,128)(2,1)S(1)} %fusion.4), channel_id=1, source_target_pairs={{0,8},{1,9},{2,10},{3,11},{4,12},{5,13},{6,14},{7,15},{8,0},{9,1},... | collective-permute-start | bytes 49160 | tf_op jit(solution)/shard_map/top_step/ppermute | solution.py:386
  63.4 6.0 %collective-permute-start.8 = (bf16[1,64,128]{2,1,0:T(8,128)(2,1)S(1)}, bf16[1,64,128]{2,1,0:T(8,128)(2,1)S(1)}, u32[]{:S(2)}, u32[]{:S(2)}) collective-permute-start(bf16[1,64,128]{2,1,0:T(8,128)(2,1)S(1)} %fusion.4), channel_id=1, source_target_pairs={{0,4},{1,5},{2,6},{3,7},{4,0},{5,1},{6,2},{7,3},{8,12},{9,13},{10,... | collective-permute-start | bytes 49160 | tf_op jit(solution)/shard_map/top_step/ppermute | solution.py:386
  69.5 4.1 %collective-permute-start.13 = (bf16[4,64,128]{2,1,0:T(8,128)(2,1)S(1)}, bf16[4,64,128]{2,1,0:T(8,128)(2,1)S(1)}, u32[]{:S(2)}, u32[]{:S(2)}) collective-permute-start(bf16[4,64,128]{2,1,0:T(8,128)(2,1)S(1)} %get-tuple-element.29), channel_id=1, source_target_pairs={{0,3},{1,2},{2,1},{3,0},{4,7},{5,6},{6,5},{7,4},{8,11},{9,10},{10,... | collective-permute-start | bytes 196616 | tf_op jit(solution)/shard_map/top_step/ppermute | solution.py:386
  71.6 4.3 %collective-permute-start.12 = (bf16[4,64,128]{2,1,0:T(8,128)(2,1)S(1)}, bf16[4,64,128]{2,1,0:T(8,128)(2,1)S(1)}, u32[]{:S(2)}, u32[]{:S(2)}) collective-permute-start(bf16[4,64,128]{2,1,0:T(8,128)(2,1)S(1)} %get-tuple-element.29), channel_id=1, source_target_pairs={{0,2},{1,3},{2,0},{3,1},{4,6},{5,7},{6,4},{7,5},{8,10},{9,11},{10,... | collective-permute-start | bytes 196616 | tf_op jit(solution)/shard_map/top_step/ppermute | solution.py:386
  71.6 4.3 %collective-permute-start.11 = (bf16[4,64,128]{2,1,0:T(8,128)(2,1)S(1)}, bf16[4,64,128]{2,1,0:T(8,128)(2,1)S(1)}, u32[]{:S(2)}, u32[]{:S(2)}) collective-permute-start(bf16[4,64,128]{2,1,0:T(8,128)(2,1)S(1)} %get-tuple-element.29), channel_id=1, source_target_pairs={{0,1},{1,0},{2,3},{3,2},{4,5},{5,4},{6,7},{7,6},{8,9},{9,8},{10,11... | collective-permute-start | bytes 196616 | tf_op jit(solution)/shard_map/top_step/ppermute | solution.py:386
  (7 other events, 46.0 us)

commit v4 on v3

--- a/solution.py
+++ b/solution.py
@@ -128,9 +128,9 @@
 
 
 def fine_kernel(
-    place_ref, pool_index, sender_ref, edge_ref, x_ref, from_a, from_b, receiver_ref, parent_ref,
-    weight_ref, edge_in, edge_out, node_in, node_out, gain_ref,
-    new_ref, sums_ref, a_ref, b_ref,
+    place_ref, pool_index, sender_ref, edge_ref, x_ref, from_a, from_b, receiver_ref,
+    edge_in, edge_out, node_in, node_out, gain_ref,
+    new_ref, a_ref, b_ref,
     table, receiver_part, new32, buffer, aggregate, node_hidden,
     gathered0, gathered1, hidden0, hidden1, message0, message1,
     index0, index1, index2, index3, index_sem, w_out, w_node_out, spread_of, w_pairs,
@@ -138,9 +138,10 @@
     gathered, hidden, message = (gathered0, gathered1), (hidden0, hidden1), (message0, message1)
     indices = (index0, index1, index2, index3)
     block = gathered0.shape[0]
-    groups, _, group_nodes = parent_ref.shape
-    nodes = group_nodes // GROUP
-    blocks = groups * GROUP
+    blocks = receiver_ref.shape[0]
+    groups = blocks // GROUP
+    nodes = x_ref.shape[0] // blocks
+    group_nodes = GROUP * nodes
     gain, node_gain = gain_ref[0:1, :], gain_ref[1:2, :]
 
     def index_copy(t, k):
@@ -154,7 +155,6 @@
         index_copy(k, k).start()
     fill_weights(edge_out, node_out, w_out, w_node_out, spread_of)
     fill_table(x_ref, place_ref, from_a, from_b, edge_in, table, receiver_part, w_pairs)
-    sums_ref[...] = jnp.zeros_like(sums_ref)
     index_copy(0, 0).wait()
     gather_block(0, gathered0)
 
@@ -219,9 +219,6 @@
                     new_rows = node_last(x_ref[rows, :], update, node_gain)
                     new_ref[rows, :] = new_rows
                     new32[rows, :] = new_rows.astype(f32)
-                    shares = match_rows(parent_ref[done], sums_ref.shape[0], weight_ref[done])
-                    sums = sums_ref[...] + mm(shares, with_ones(new_rows))
-                    sums_ref[...] = sums if last else jnp.where(g > 0, sums, 0.0)
 
             cuts = (0, *SPLIT, block)
             for i, step in enumerate((pick, multiply_first, rectify, multiply_last, scale)):
@@ -244,6 +241,15 @@
         gather_rows(lambda j: pool_index[0, side, j], new32, buffer, count, side * count)
     a_ref[...] = buffer[aligned(count * place_ref[0], count), :].astype(bf16)
     b_ref[...] = buffer[aligned(count * (1 - place_ref[0]), count), :].astype(bf16)
+
+
+def local_pool_kernel(new_ref, parent_ref, weight_ref, sums_ref):
+    groups, _, size = parent_ref.shape
+    total = 0.0
+    for g in range(groups):
+        shares = match_rows(parent_ref[g], sums_ref.shape[0], weight_ref[g])
+        total += mm(shares, with_ones(new_ref[g * size : (g + 1) * size, :]))
+    sums_ref[...] = total
 
 
 def pool_kernel(
@@ -275,25 +281,57 @@
     nodes = x_ref.shape[0] // blocks
     fill_weights(edge_out, node_out, w_out, w_node_out, spread_of)
     fill_table(x_ref, place_ref, from_a, from_b, edge_in, table, receiver_part, w_pairs)
-    gather_rows(lambda j: sender_ref[j], table, gathered, blocks * block)
-    for t in range(blocks):
-        at = slice(t * block, (t + 1) * block)
+    keep = {}
+
+    def gather_part(t, part):
+        if t < blocks:
+            begin = t * block + part * block // 4
+            gather_rows(lambda j: sender_ref[begin + j], table, gathered, block // 4, begin)
+
+    def first(t):
+        own, at = slice(t * nodes, (t + 1) * nodes), slice(t * block, (t + 1) * block)
+        keep["picks", t] = match_rows(receiver_ref[t] - t * nodes, nodes)
+        keep["pairs", t] = edge_first(
+            keep["picks", t], receiver_part[own, :], edge_ref[at, :], gathered[at, :], edge_in[2 * LANES :, :]
+        )
+
+    def second(t):
+        keep["centred", t] = mm(keep["pairs", t], w_out[...])
+
+    def third(t):
+        centred = keep["centred", t]
+        spread = mm((centred * centred).astype(bf16), spread_of[...])
+        keep["message", t] = (centred * lax.rsqrt(spread + epsilon)).astype(bf16)
+
+    def sum_edges(t):
         own = slice(t * nodes, (t + 1) * nodes)
-        picks = match_rows(receiver_ref[t] - t * nodes, nodes)
-        pairs = edge_first(
-            picks, receiver_part[own, :], edge_ref[at, :], gathered[at, :], edge_in[2 * LANES :, :]
-        )
-        message = normed_pairs(pairs, w_out[...], spread_of[...]).astype(bf16)
-        aggregate[own, :] = edge_sums(picks, message, gain_ref[0:1, :])
+        aggregate[own, :] = edge_sums(keep["picks", t], keep["message", t], gain_ref[0:1, :])
+
+    for part in range(4):
+        gather_part(0, part)
+    for tick in range(blocks + 3):
+        for part, (stage, lag) in enumerate(((first, 0), (second, 1), (third, 2), (sum_edges, 3))):
+            if 0 <= tick - lag < blocks:
+                stage(tick - lag)
+            gather_part(tick + 1, part)
     pairs = node_first(x_ref[...], aggregate[...], node_in[...])
     new_rows = node_last(x_ref[...], normed_pairs(pairs, w_node_out[...], spread_of[...]), gain_ref[1:2, :])
     new_ref[...] = new_rows
-    share = own_ref.shape[0]
+    share = x_ref.shape[0] // 8
+    size = own_ref.shape[0]
     shares = match_rows(parent_ref[...] - (place_ref[3] - 1) * share, 3 * share, weight_ref[...])
-    shares_sum[...] = mm(shares, with_ones(new_rows))
-    own_ref[...] = shares_sum[share : 2 * share, :]
-    a_ref[...] = shares_sum[aligned(2 * share * place_ref[0], share), :]
-    b_ref[...] = shares_sum[aligned(2 * share * (1 - place_ref[0]), share), :]
+    sums = mm(shares, new_rows)
+    rest = jnp.zeros((LANES - share, shares.shape[1]), bf16)
+    for i in range(3):
+        at = slice(i * share, (i + 1) * share)
+        shares_sum[i * size : i * size + share, :] = sums[at]
+        shares_sum[i * size + share : (i + 1) * size, :] = lax.dot_general(
+            jnp.ones((size - share, shares.shape[1]), bf16), jnp.concatenate([shares[at], rest], axis=0),
+            (((1,), (1,)), ((), ())), preferred_element_type=f32,
+        )
+    own_ref[...] = shares_sum[size : 2 * size, :]
+    a_ref[...] = shares_sum[aligned(2 * size * place_ref[0], size), :]
+    b_ref[...] = shares_sum[aligned(2 * size * (1 - place_ref[0]), size), :]
 
 
 def lift_kernel(parent_ref, picks_ref):
@@ -428,10 +466,10 @@
         )
 
     with jax.named_scope("fine_step"):
-        fine_new, local_sums, for_a, for_b = call(
+        fine_new, for_a, for_b = call(
             fine_kernel, "fine_step",
-            [rows_of(fine_total), rows_of(coarse_total, f32, 2 * LANES), rows_of(slots), rows_of(slots)],
-            [whole_smem, whole_smem, left_in_hbm] + [whole_vmem] * 7 + weight_specs,
+            [rows_of(fine_total), rows_of(slots), rows_of(slots)],
+            [whole_smem, whole_smem, left_in_hbm] + [whole_vmem] * 5 + weight_specs,
             [
                 pltpu.VMEM((fine_total + 2 * border, LANES), f32),
                 pltpu.VMEM((fine_total, LANES), bf16),
@@ -447,14 +485,19 @@
             + weight_scratch,
             (
                 place, pool_rows, fine_sender, fine_edges, fine_latent, from_a, from_b,
-                fine_receiver.reshape(blocks, 1, block), fine_parent.reshape(groups, 1, GROUP * nodes),
-                fine_weight.reshape(groups, 1, GROUP * nodes),
+                fine_receiver.reshape(blocks, 1, block),
             )
             + weights,
             level=0,
             us=24.0,
         )
         from_a, from_b = swap_with_neighbours(for_a, for_b)
+        by_group = (groups, 1, GROUP * nodes)
+        local_sums = call(
+            local_pool_kernel, "local_pool_step", rows_of(coarse_total, f32, 2 * LANES), [whole_vmem] * 3, [],
+            (fine_new, fine_parent.reshape(by_group), fine_weight.reshape(by_group)),
+            us=2.0,
+        )
 
     with jax.named_scope("coarse_input"):
         border1 = coarse_border.shape[2]
@@ -477,14 +520,14 @@
         share = coarse_total // 8
         coarse_new, own, for_a, for_b = call(
             coarse_kernel, "coarse_step",
-            [rows_of(coarse_total)] + [rows_of(share, f32, 2 * LANES)] * 3,
+            [rows_of(coarse_total)] + [rows_of(share + 8, f32)] * 3,
             [whole_smem, whole_smem] + [whole_vmem] * 7 + weight_specs,
             [
                 pltpu.VMEM((coarse_total + 2 * border1, LANES), f32),
                 pltpu.VMEM((coarse_total, LANES), bf16),
                 pltpu.VMEM((edge_total1, LANES), f32),
                 pltpu.VMEM((coarse_total, LANES), bf16),
-                pltpu.VMEM((3 * share, 2 * LANES), f32),
+                pltpu.VMEM((3 * (share + 8), LANES), f32),
             ]
             + weight_scratch,
             (
@@ -497,7 +540,7 @@
         )
         from_a, from_b = swap_with_neighbours(for_a, for_b)
         shares = own + from_a + from_b
-        top_in = (shares[:, :LANES] / shares[:, LANES:]).astype(bf16)
+        top_in = (shares[:share] / shares[share, :share][:, None]).astype(bf16)
 
     with jax.named_scope("top_step"):
         everyone = gather_all(top_in).reshape(count * share, LANES)

time: 80.7 us -> 77.8 us (0.964)
  waiting for transfers between devices: 15 us -> 13.3 us
  Pallas kernels: 35 us -> 33.7 us
    ppermute x4, waiting for transfers between devices: 10.3 us -> 8.75 us  [swap_with_neighbours(): lax.ppermute(for_b, 'dom', pairs_b)]
    pallas_call x6 -> x7, Pallas kernels: 35 us -> 33.7 us  [call(): pl.pallas_call(with_level, name=name, out_shape=outs, in_specs=[pl.BlockS...]
  transfers between devices with their start and end apart: 14 -> 14, of which waited for: 8 -> 8; matrix products, arithmetic and copies ran while one was open for 0% -> 0% of each run, Pallas kernels for 1% -> 3%
where the time goes in v4:
time: 77.8 us; the launch traced here: 77.6 us
  Pallas kernels  33.7 us (43%)
  starting transfers between devices  26.5 us (34%)
  waiting for transfers between devices  13.3 us (17%)
  local copies, waits for them, and re-layouts  2.17 us (3%)
  between operations  1.71 us (2%)
    pallas_call x7, Pallas kernels, call(): pl.pallas_call(with_level, name=name, out_shape=outs, in_specs=[pl.BlockS...  33.7 us
    ppermute x4, starting transfers between devices, swap_with_neighbours(): lax.ppermute(for_b, 'dom', pairs_b)  19.1 us
    ppermute x4, waiting for transfers between devices, swap_with_neighbours(): lax.ppermute(for_b, 'dom', pairs_b)  8.75 us
    ppermute x6, starting transfers between devices, gather_all(): lax.ppermute(blocks, 'dom', [(i, i ^ j * stride) for i in range(count)])  6.74 us
    ppermute x6, waiting for transfers between devices, gather_all(): lax.ppermute(blocks, 'dom', [(i, i ^ j * stride) for i in range(count)])  4.54 us
    unnamed x50, local copies, waits for them, and re-layouts  2.05 us
  transfers between devices with their start and end apart: 14, of which 8 were waited for; matrix products, arithmetic and copies ran while one was open for 0% of the time, Pallas kernels for 3%

profile of v4, /device:TPU:0, one launch (start us, length us, event | category | flops | bytes accessed | tf_op | source)
XLA Modules:
  0.0 77.6 jit_solution(2550931879841919784)
XLA Ops:
  1.3 0.1 stack.43.refs_0_
  1.4 1.2 %copy-done.1 = bf16[4096,128]{1,0:T(8,128)(2,1)S(1)} copy-done((bf16[4096,128]{1,0:T(8,128)(2,1)S(1)}, bf16[4096,128]{1,0:T(8,128)(2,1)}, u32[]{:S(2)}) %copy-start.1) | copy-done | bytes 1048600
  2.6 0.7 copy-done.13
  3.4 1.9 %border_rows.1 = (bf16[1024,128]{1,0:T(8,128)(2,1)S(1)}, bf16[1024,128]{1,0:T(8,128)(2,1)S(1)}) custom-call(s32[5]{0:T(128)S(1)} %stack.43.refs_0_, s32[1,2,1024]{2,1,0:T(2,128)S(1)} %copy-done.13, bf16[4096,128]{1,0:T(8,128)(2,1)S(1)} %copy-done.1), custom_call_target="tpu_custom_call" | custom-call | flops 3000000000 | tf_op jit(solution)/shard_map/fine_border_rows/border_rows/pallas_call | solution.py:389
  5.4 0.5 collective-permute-start
  5.9 5.7 %collective-permute-start.1 = (bf16[1024,128]{1,0:T(8,128)(2,1)S(1)}, bf16[1024,128]{1,0:T(8,128)(2,1)S(1)}, u32[]{:S(2)}, u32[]{:S(2)}) collective-permute-start(bf16[1024,128]{1,0:T(8,128)(2,1)S(1)} %get-tuple-element.15), channel_id=1, source_target_pairs={{1,2},{3,4},{5,6},{7,8},{9,10},{11,12},{13,14},{15,0},{2,1},{4,3},... | collective-permute-start | bytes 786440 | tf_op jit(solution)/shard_map/fine_border_rows/ppermute | solution.py:410
  11.6 4.1 %collective-permute-done.1.refs_6_ = bf16[1024,128]{1,0:T(8,128)(2,1)S(1)} collective-permute-done((bf16[1024,128]{1,0:T(8,128)(2,1)S(1)}, bf16[1024,128]{1,0:T(8,128)(2,1)S(1)}, u32[]{:S(2)}, u32[]{:S(2)}) %collective-permute-start.1) | collective-permute-done | bytes 262176 | tf_op jit(solution)/shard_map/fine_border_rows/ppermute | solution.py:410
  15.7 20.0 %fine_step.1 = (bf16[4096,128]{1,0:T(8,128)(2,1)S(1)}, bf16[512,128]{1,0:T(8,128)(2,1)S(1)}, bf16[512,128]{1,0:T(8,128)(2,1)S(1)}) custom-call(s32[5]{0:T(128)S(1)} %stack.43.refs_0_, s32[1,2,512]{2,1,0:T(2,128)S(1)} %copy-done.18, s32[16384]{0:T(1024)S(1)} %copy-done.9, bf16[16384,128]{1,0:T(8,128)(2,1)S(1)} %copy-done, bf16[4096,128]{1,0:T(8,128)(2,1)S(1)} %copy-done.2, ...), custom_call_target="tpu_custom_call" | custom-call | flops 24000000000 | tf_op jit(solution)/shard_map/fine_step/fine_step/pallas_call | solution.py:389
  35.8 0.1 collective-permute-start.2
  35.9 4.5 %collective-permute-start.3 = (bf16[512,128]{1,0:T(8,128)(2,1)S(1)}, bf16[512,128]{1,0:T(8,128)(2,1)S(1)}, u32[]{:S(2)}, u32[]{:S(2)}) collective-permute-start(bf16[512,128]{1,0:T(8,128)(2,1)S(1)} %get-tuple-element.18), channel_id=1, source_target_pairs={{1,2},{3,4},{5,6},{7,8},{9,10},{11,12},{13,14},{15,0},{2,1},{4,3},... | collective-permute-start | bytes 393224 | tf_op jit(solution)/shard_map/fine_step/ppermute | solution.py:410
  40.4 1.2 %local_pool_step.1.refs_2_ = f32[512,256]{1,0:T(8,128)S(1)} custom-call(bf16[4096,128]{1,0:T(8,128)(2,1)S(1)} %get-tuple-element.16.refs_0_.refs_8_, s32[8,1,512]{2,1,0:T(1,128)S(1)} %bitcast.31, s32[8,1,512]{2,1,0:T(1,128)S(1)} %bitcast.30), custom_call_target="tpu_custom_call" | custom-call | flops 2000000000 | tf_op jit(solution)/shard_map/fine_step/local_pool_step/pallas_call | solution.py:389
  41.6 1.4 %collective-permute-done.3.refs_4_ = bf16[512,128]{1,0:T(8,128)(2,1)S(1)} collective-permute-done((bf16[512,128]{1,0:T(8,128)(2,1)S(1)}, bf16[512,128]{1,0:T(8,128)(2,1)S(1)}, u32[]{:S(2)}, u32[]{:S(2)}) %collective-permute-start.3) | collective-permute-done | bytes 131104 | tf_op jit(solution)/shard_map/fine_step/ppermute | solution.py:410
  43.0 1.1 %coarse_input.1 = (bf16[512,128]{1,0:T(8,128)(2,1)S(1)}, bf16[128,128]{1,0:T(8,128)(2,1)S(1)}, bf16[128,128]{1,0:T(8,128)(2,1)S(1)}) custom-call(s32[5]{0:T(128)S(1)} %stack.43.refs_0_, s32[1,2,128]{2,1,0:T(2,128)S(1)} %copy-done.22, f32[512,256]{1,0:T(8,128)S(1)} %local_pool_step.1.refs_2_, bf16[512,128]{1,0:T(8,128)(2,1)S(1)} %collective-permute-done.2.refs_3_, ...), custom_call_target="tpu_custom_call" | custom-call | flops 1000000000 | tf_op jit(solution)/shard_map/coarse_input/coarse_input/pallas_call | solution.py:389
  44.2 0.1 collective-permute-start.4
  44.2 4.5 %collective-permute-start.5 = (bf16[128,128]{1,0:T(8,128)(2,1)S(1)}, bf16[128,128]{1,0:T(8,128)(2,1)S(1)}, u32[]{:S(2)}, u32[]{:S(2)}) collective-permute-start(bf16[128,128]{1,0:T(8,128)(2,1)S(1)} %get-tuple-element.21), channel_id=1, source_target_pairs={{1,2},{3,4},{5,6},{7,8},{9,10},{11,12},{13,14},{15,0},{2,1},{4,3},... | collective-permute-start | bytes 98312 | tf_op jit(solution)/shard_map/coarse_input/ppermute | solution.py:410
  48.7 1.6 %collective-permute-done.5.refs_5_ = bf16[128,128]{1,0:T(8,128)(2,1)S(1)} collective-permute-done((bf16[128,128]{1,0:T(8,128)(2,1)S(1)}, bf16[128,128]{1,0:T(8,128)(2,1)S(1)}, u32[]{:S(2)}, u32[]{:S(2)}) %collective-permute-start.5) | collective-permute-done | bytes 32800 | tf_op jit(solution)/shard_map/coarse_input/ppermute | solution.py:410
  50.4 3.6 %coarse_step.1 = (bf16[512,128]{1,0:T(8,128)(2,1)S(1)}, f32[72,128]{1,0:T(8,128)S(1)}, f32[72,128]{1,0:T(8,128)S(1)}, f32[72,128]{1,0:T(8,128)S(1)}) custom-call(s32[5]{0:T(128)S(1)} %stack.43.refs_0_, s32[2048]{0:T(1024)S(1)} %copy-done.14, bf16[2048,128]{1,0:T(8,128)(2,1)S(1)} %copy-done.3, bf16[512,128]{1,0:T(8,128)(2,1)S(1)} %get-tuple-element.19.refs_3_, ...), custom_call_target="tpu_custom_call" | custom-call | flops 4000000000 | tf_op jit(solution)/shard_map/coarse_step/coarse_step/pallas_call | solution.py:389
  54.0 4.5 %collective-permute-start.7 = (f32[72,128]{1,0:T(8,128)S(1)}, f32[72,128]{1,0:T(8,128)S(1)}, u32[]{:S(2)}, u32[]{:S(2)}) collective-permute-start(f32[72,128]{1,0:T(8,128)S(1)} %get-tuple-element.24), channel_id=1, source_target_pairs={{1,2},{3,4},{5,6},{7,8},{9,10},{11,12},{13,14},{15,0},{2,1},{4,3},... | collective-permute-start | bytes 110600 | tf_op jit(solution)/shard_map/coarse_step/ppermute | solution.py:410
  58.5 1.7 %collective-permute-done.7 = f32[72,128]{1,0:T(8,128)S(1)} collective-permute-done((f32[72,128]{1,0:T(8,128)S(1)}, f32[72,128]{1,0:T(8,128)S(1)}, u32[]{:S(2)}, u32[]{:S(2)}) %collective-permute-start.7) | collective-permute-done | bytes 36896 | tf_op jit(solution)/shard_map/coarse_step/ppermute | solution.py:410
  60.2 0.1 fusion.4
  60.3 0.1 collective-permute-start.10
  60.4 0.1 collective-permute-start.9
  60.5 4.3 %collective-permute-start.8 = (bf16[1,64,128]{2,1,0:T(8,128)(2,1)S(1)}, bf16[1,64,128]{2,1,0:T(8,128)(2,1)S(1)}, u32[]{:S(2)}, u32[]{:S(2)}) collective-permute-start(bf16[1,64,128]{2,1,0:T(8,128)(2,1)S(1)} %fusion.4), channel_id=1, source_target_pairs={{0,4},{1,5},{2,6},{3,7},{4,0},{5,1},{6,2},{7,3},{8,12},{9,13},{10,... | collective-permute-start | bytes 49160 | tf_op jit(solution)/shard_map/top_step/ppermute | solution.py:424
  64.8 0.1 fusion.3
  64.9 1.2 %collective-permute-done.10 = bf16[1,64,128]{2,1,0:T(8,128)(2,1)S(1)} collective-permute-done((bf16[1,64,128]{2,1,0:T(8,128)(2,1)S(1)}, bf16[1,64,128]{2,1,0:T(8,128)(2,1)S(1)}, u32[]{:S(2)}, u32[]{:S(2)}) %collective-permute-start.10) | collective-permute-done | bytes 16416 | tf_op jit(solution)/shard_map/top_step/ppermute | solution.py:424
  66.1 0.4 collective-permute-done.8
  66.6 2.1 %collective-permute-start.13 = (bf16[4,64,128]{2,1,0:T(8,128)(2,1)S(1)}, bf16[4,64,128]{2,1,0:T(8,128)(2,1)S(1)}, u32[]{:S(2)}, u32[]{:S(2)}) collective-permute-start(bf16[4,64,128]{2,1,0:T(8,128)(2,1)S(1)} %get-tuple-element.27), channel_id=1, source_target_pairs={{0,3},{1,2},{2,1},{3,0},{4,7},{5,6},{6,5},{7,4},{8,11},{9,10},{10,... | collective-permute-start | bytes 196616 | tf_op jit(solution)/shard_map/top_step/ppermute | solution.py:424
  68.7 0.2 collective-permute-start.11
  68.9 1.1 %lift_picks.1.refs_2_ = bf16[4096,512]{1,0:T(8,128)(2,1)S(1)} custom-call(s32[8,1,512]{2,1,0:T(1,128)S(1)} %bitcast.32), custom_call_target="tpu_custom_call" | custom-call | flops 3000000000 | tf_op jit(solution)/shard_map/fine_border_rows/lift_picks/pallas_call | solution.py:389
  70.0 0.6 collective-permute-done.13
  70.7 2.3 %collective-permute-done.12 = bf16[4,64,128]{2,1,0:T(8,128)(2,1)S(1)} collective-permute-done((bf16[4,64,128]{2,1,0:T(8,128)(2,1)S(1)}, bf16[4,64,128]{2,1,0:T(8,128)(2,1)S(1)}, u32[]{:S(2)}, u32[]{:S(2)}) %collective-permute-start.12) | collective-permute-done | bytes 65568 | tf_op jit(solution)/shard_map/top_step/ppermute | solution.py:424
  73.0 4.6 %top_step.1 = (bf16[4096,128]{1,0:T(8,128)(2,1)}, bf16[512,128]{1,0:T(8,128)(2,1)}) custom-call(s32[5]{0:T(128)S(1)} %stack.43.refs_0_, s32[2048]{0:T(1024)S(1)} %copy-done.16, bf16[4096,512]{1,0:T(8,128)(2,1)S(1)} %lift_picks.1.refs_2_, bf16[2048,128]{1,0:T(8,128)(2,1)S(1)} %copy-done.4, bf16[1024,128]{1,0:T(8,128)(2,1)S(1)} %bitcast.28, ...), custom_call_target="tpu_custom_call" | custom-call | flops 5000000000 | tf_op jit(solution)/shard_map/top_step/top_step/pallas_call | solution.py:389
  (63 shorter events, 0.3 us)
Async XLA Ops:
  3.3 8.2 %copy-start.24 = (s32[1,2,512]{2,1,0:T(2,128)S(1)}, s32[1,2,512]{2,1,0:T(2,128)}, u32[]{:S(2)}) copy-start(s32[1,2,512]{2,1,0:T(2,128)} %param.33) | copy-start | bytes 12292
  3.3 12.3 %copy-start = (bf16[16384,128]{1,0:T(8,128)(2,1)S(1)}, bf16[16384,128]{1,0:T(8,128)(2,1)}, u32[]{:S(2)}) copy-start(bf16[16384,128]{1,0:T(8,128)(2,1)} %refs_3_.2) | copy-start | bytes 12582916
  3.3 12.3 %copy-start.2 = (bf16[4096,128]{1,0:T(8,128)(2,1)S(1)}, bf16[4096,128]{1,0:T(8,128)(2,1)}, u32[]{:S(2)}) copy-start(bf16[4096,128]{1,0:T(8,128)(2,1)} %refs_4_.1) | copy-start | bytes 3145732
  3.3 12.3 %copy-start.5 = (bf16[3,384,128]{2,1,0:T(8,128)(2,1)S(1)}, bf16[3,384,128]{2,1,0:T(8,128)(2,1)}, u32[]{:S(2)}) copy-start(bf16[3,384,128]{2,1,0:T(8,128)(2,1)} %refs_9_.5) | copy-start | bytes 884740
  3.3 12.3 %copy-start.6 = (bf16[3,256,128]{2,1,0:T(8,128)(2,1)S(1)}, bf16[3,256,128]{2,1,0:T(8,128)(2,1)}, u32[]{:S(2)}) copy-start(bf16[3,256,128]{2,1,0:T(8,128)(2,1)} %refs_11_.5) | copy-start | bytes 589828
  3.3 12.3 %copy-start.7 = (bf16[3,128,128]{2,1,0:T(8,128)(2,1)S(1)}, bf16[3,128,128]{2,1,0:T(8,128)(2,1)}, u32[]{:S(2)}) copy-start(bf16[3,128,128]{2,1,0:T(8,128)(2,1)} %refs_10_.5) | copy-start | bytes 294916
  3.4 12.3 %copy-start.8 = (bf16[3,128,128]{2,1,0:T(8,128)(2,1)S(1)}, bf16[3,128,128]{2,1,0:T(8,128)(2,1)}, u32[]{:S(2)}) copy-start(bf16[3,128,128]{2,1,0:T(8,128)(2,1)} %refs_12_.5) | copy-start | bytes 294916
  3.4 12.3 %copy-start.9 = (s32[16384]{0:T(1024)S(1)}, s32[16384]{0:T(1024)}, u32[]{:S(2)}) copy-start(s32[16384]{0:T(1024)} %refs_2_.4) | copy-start | bytes 196612
  3.4 12.3 %copy-start.10 = (s32[16384]{0:T(1024)S(1)}, s32[16384]{0:T(1024)}, u32[]{:S(2)}) copy-start(s32[16384]{0:T(1024)} %param.28) | copy-start | bytes 196612
  3.4 12.3 %copy-start.18 = (s32[1,2,512]{2,1,0:T(2,128)S(1)}, s32[1,2,512]{2,1,0:T(2,128)}, u32[]{:S(2)}) copy-start(s32[1,2,512]{2,1,0:T(2,128)} %refs_1_.6) | copy-start | bytes 12292
  3.4 12.3 %copy-start.19 = (f32[3,2,128]{2,1,0:T(2,128)S(1)}, f32[3,2,128]{2,1,0:T(2,128)}, u32[]{:S(2)}) copy-start(f32[3,2,128]{2,1,0:T(2,128)} %refs_13_.3) | copy-start | bytes 9220
  5.4 6.2 %collective-permute-start = (bf16[1024,128]{1,0:T(8,128)(2,1)S(1)}, bf16[1024,128]{1,0:T(8,128)(2,1)S(1)}, u32[]{:S(2)}, u32[]{:S(2)}) collective-permute-start(bf16[1024,128]{1,0:T(8,128)(2,1)S(1)} %get-tuple-element.14), channel_id=1, source_target_pairs={{0,1},{1,0},{2,3},{3,2},{4,5},{5,4},{6,7},{7,6},{8,9},{9,8},{10,11... | collective-permute-start | bytes 786440 | tf_op jit(solution)/shard_map/fine_border_rows/ppermute | solution.py:410
  5.9 9.8 %collective-permute-start.1 = (bf16[1024,128]{1,0:T(8,128)(2,1)S(1)}, bf16[1024,128]{1,0:T(8,128)(2,1)S(1)}, u32[]{:S(2)}, u32[]{:S(2)}) collective-permute-start(bf16[1024,128]{1,0:T(8,128)(2,1)S(1)} %get-tuple-element.15), channel_id=1, source_target_pairs={{1,2},{3,4},{5,6},{7,8},{9,10},{11,12},{13,14},{15,0},{2,1},{4,3},... | collective-permute-start | bytes 786440 | tf_op jit(solution)/shard_map/fine_border_rows/ppermute | solution.py:410
  15.7 24.6 %copy-start.11 = (s32[4096]{0:T(1024)S(1)}, s32[4096]{0:T(1024)}, u32[]{:S(2)}) copy-start(s32[4096]{0:T(1024)} %param.35) | copy-start | bytes 49156
  15.7 24.6 %copy-start.12 = (s32[4096]{0:T(1024)S(1)}, s32[4096]{0:T(1024)}, u32[]{:S(2)}) copy-start(s32[4096]{0:T(1024)} %param.34) | copy-start | bytes 49156
  35.8 5.9 %collective-permute-start.2 = (bf16[512,128]{1,0:T(8,128)(2,1)S(1)}, bf16[512,128]{1,0:T(8,128)(2,1)S(1)}, u32[]{:S(2)}, u32[]{:S(2)}) collective-permute-start(bf16[512,128]{1,0:T(8,128)(2,1)S(1)} %get-tuple-element.17), channel_id=1, source_target_pairs={{0,1},{1,0},{2,3},{3,2},{4,5},{5,4},{6,7},{7,6},{8,9},{9,8},{10,11... | collective-permute-start | bytes 393224 | tf_op jit(solution)/shard_map/fine_step/ppermute | solution.py:410
  35.9 7.2 %collective-permute-start.3 = (bf16[512,128]{1,0:T(8,128)(2,1)S(1)}, bf16[512,128]{1,0:T(8,128)(2,1)S(1)}, u32[]{:S(2)}, u32[]{:S(2)}) collective-permute-start(bf16[512,128]{1,0:T(8,128)(2,1)S(1)} %get-tuple-element.18), channel_id=1, source_target_pairs={{1,2},{3,4},{5,6},{7,8},{9,10},{11,12},{13,14},{15,0},{2,1},{4,3},... | collective-permute-start | bytes 393224 | tf_op jit(solution)/shard_map/fine_step/ppermute | solution.py:410
  40.3 10.0 %copy-start.3 = (bf16[2048,128]{1,0:T(8,128)(2,1)S(1)}, bf16[2048,128]{1,0:T(8,128)(2,1)}, u32[]{:S(2)}) copy-start(bf16[2048,128]{1,0:T(8,128)(2,1)} %refs_2_.5) | copy-start | bytes 1572868
  40.3 10.0 %copy-start.14 = (s32[2048]{0:T(1024)S(1)}, s32[2048]{0:T(1024)}, u32[]{:S(2)}) copy-start(s32[2048]{0:T(1024)} %refs_1_.8) | copy-start | bytes 24580
  40.3 10.0 %copy-start.15 = (s32[2048]{0:T(1024)S(1)}, s32[2048]{0:T(1024)}, u32[]{:S(2)}) copy-start(s32[2048]{0:T(1024)} %param.38) | copy-start | bytes 24580
  40.4 10.0 %copy-start.20 = (s32[512]{0:T(512)S(1)}, s32[512]{0:T(512)}, u32[]{:S(2)}) copy-start(s32[512]{0:T(512)} %param.41) | copy-start | bytes 6148
  40.4 10.0 %copy-start.21 = (s32[512]{0:T(512)S(1)}, s32[512]{0:T(512)}, u32[]{:S(2)}) copy-start(s32[512]{0:T(512)} %param.40) | copy-start | bytes 6148
  44.2 4.5 %collective-permute-start.4 = (bf16[128,128]{1,0:T(8,128)(2,1)S(1)}, bf16[128,128]{1,0:T(8,128)(2,1)S(1)}, u32[]{:S(2)}, u32[]{:S(2)}) collective-permute-start(bf16[128,128]{1,0:T(8,128)(2,1)S(1)} %get-tuple-element.20), channel_id=1, source_target_pairs={{0,1},{1,0},{2,3},{3,2},{4,5},{5,4},{6,7},{7,6},{8,9},{9,8},{10,11... | collective-permute-start | bytes 98312 | tf_op jit(solution)/shard_map/coarse_input/ppermute | solution.py:410
  44.2 6.1 %collective-permute-start.5 = (bf16[128,128]{1,0:T(8,128)(2,1)S(1)}, bf16[128,128]{1,0:T(8,128)(2,1)S(1)}, u32[]{:S(2)}, u32[]{:S(2)}) collective-permute-start(bf16[128,128]{1,0:T(8,128)(2,1)S(1)} %get-tuple-element.21), channel_id=1, source_target_pairs={{1,2},{3,4},{5,6},{7,8},{9,10},{11,12},{13,14},{15,0},{2,1},{4,3},... | collective-permute-start | bytes 98312 | tf_op jit(solution)/shard_map/coarse_input/ppermute | solution.py:410
  54.0 4.5 %collective-permute-start.6 = (f32[72,128]{1,0:T(8,128)S(1)}, f32[72,128]{1,0:T(8,128)S(1)}, u32[]{:S(2)}, u32[]{:S(2)}) collective-permute-start(f32[72,128]{1,0:T(8,128)S(1)} %get-tuple-element.23), channel_id=1, source_target_pairs={{0,1},{1,0},{2,3},{3,2},{4,5},{5,4},{6,7},{7,6},{8,9},{9,8},{10,11... | collective-permute-start | bytes 110600 | tf_op jit(solution)/shard_map/coarse_step/ppermute | solution.py:410
  54.0 6.2 %collective-permute-start.7 = (f32[72,128]{1,0:T(8,128)S(1)}, f32[72,128]{1,0:T(8,128)S(1)}, u32[]{:S(2)}, u32[]{:S(2)}) collective-permute-start(f32[72,128]{1,0:T(8,128)S(1)} %get-tuple-element.24), channel_id=1, source_target_pairs={{1,2},{3,4},{5,6},{7,8},{9,10},{11,12},{13,14},{15,0},{2,1},{4,3},... | collective-permute-start | bytes 110600 | tf_op jit(solution)/shard_map/coarse_step/ppermute | solution.py:410
  60.3 5.7 %collective-permute-start.10 = (bf16[1,64,128]{2,1,0:T(8,128)(2,1)S(1)}, bf16[1,64,128]{2,1,0:T(8,128)(2,1)S(1)}, u32[]{:S(2)}, u32[]{:S(2)}) collective-permute-start(bf16[1,64,128]{2,1,0:T(8,128)(2,1)S(1)} %fusion.4), channel_id=1, source_target_pairs={{0,12},{1,13},{2,14},{3,15},{4,8},{5,9},{6,10},{7,11},{8,4},{9,5},... | collective-permute-start | bytes 49160 | tf_op jit(solution)/shard_map/top_step/ppermute | solution.py:424
  60.4 5.7 %collective-permute-start.9 = (bf16[1,64,128]{2,1,0:T(8,128)(2,1)S(1)}, bf16[1,64,128]{2,1,0:T(8,128)(2,1)S(1)}, u32[]{:S(2)}, u32[]{:S(2)}) collective-permute-start(bf16[1,64,128]{2,1,0:T(8,128)(2,1)S(1)} %fusion.4), channel_id=1, source_target_pairs={{0,8},{1,9},{2,10},{3,11},{4,12},{5,13},{6,14},{7,15},{8,0},{9,1},... | collective-permute-start | bytes 49160 | tf_op jit(solution)/shard_map/top_step/ppermute | solution.py:424
  60.5 6.0 %collective-permute-start.8 = (bf16[1,64,128]{2,1,0:T(8,128)(2,1)S(1)}, bf16[1,64,128]{2,1,0:T(8,128)(2,1)S(1)}, u32[]{:S(2)}, u32[]{:S(2)}) collective-permute-start(bf16[1,64,128]{2,1,0:T(8,128)(2,1)S(1)} %fusion.4), channel_id=1, source_target_pairs={{0,4},{1,5},{2,6},{3,7},{4,0},{5,1},{6,2},{7,3},{8,12},{9,13},{10,... | collective-permute-start | bytes 49160 | tf_op jit(solution)/shard_map/top_step/ppermute | solution.py:424
  66.6 4.1 %collective-permute-start.13 = (bf16[4,64,128]{2,1,0:T(8,128)(2,1)S(1)}, bf16[4,64,128]{2,1,0:T(8,128)(2,1)S(1)}, u32[]{:S(2)}, u32[]{:S(2)}) collective-permute-start(bf16[4,64,128]{2,1,0:T(8,128)(2,1)S(1)} %get-tuple-element.27), channel_id=1, source_target_pairs={{0,3},{1,2},{2,1},{3,0},{4,7},{5,6},{6,5},{7,4},{8,11},{9,10},{10,... | collective-permute-start | bytes 196616 | tf_op jit(solution)/shard_map/top_step/ppermute | solution.py:424
  68.7 4.3 %collective-permute-start.12 = (bf16[4,64,128]{2,1,0:T(8,128)(2,1)S(1)}, bf16[4,64,128]{2,1,0:T(8,128)(2,1)S(1)}, u32[]{:S(2)}, u32[]{:S(2)}) collective-permute-start(bf16[4,64,128]{2,1,0:T(8,128)(2,1)S(1)} %get-tuple-element.27), channel_id=1, source_target_pairs={{0,2},{1,3},{2,0},{3,1},{4,6},{5,7},{6,4},{7,5},{8,10},{9,11},{10,... | collective-permute-start | bytes 196616 | tf_op jit(solution)/shard_map/top_step/ppermute | solution.py:424
  68.7 4.3 %collective-permute-start.11 = (bf16[4,64,128]{2,1,0:T(8,128)(2,1)S(1)}, bf16[4,64,128]{2,1,0:T(8,128)(2,1)S(1)}, u32[]{:S(2)}, u32[]{:S(2)}) collective-permute-start(bf16[4,64,128]{2,1,0:T(8,128)(2,1)S(1)} %get-tuple-element.27), channel_id=1, source_target_pairs={{0,1},{1,0},{2,3},{3,2},{4,5},{5,4},{6,7},{7,6},{8,9},{9,8},{10,11... | collective-permute-start | bytes 196616 | tf_op jit(solution)/shard_map/top_step/ppermute | solution.py:424
  (7 other events, 36.9 us)

commit v5 on v4

--- a/solution.py
+++ b/solution.py
@@ -105,17 +105,13 @@
     b_ref[...] = buffer[aligned(count * (1 - place_ref[0]), count), :].astype(bf16)
 
 
-def fill_table(x_ref, place_ref, from_a, from_b, edge_in, table, receiver_part, w_pairs):
+def fill_border(x_ref, place_ref, from_a, from_b, edge_in, table, w_pairs):
     w_s = edge_in[:LANES, :]
     w_pairs[...] = jnp.zeros_like(w_pairs)
     w_pairs[:LANES, :LANES] = w_s
     w_pairs[LANES:, LANES:] = w_s
-
     count, border = x_ref.shape[0], from_a.shape[0]
     half = border // 2
-    both = mm(x_ref[...], jnp.concatenate([w_s, edge_in[LANES : 2 * LANES, :]], axis=1))
-    table[:count, :] = both[:, :LANES]
-    receiver_part[...] = both[:, LANES:].astype(bf16)
     for rows, first, scale in (
         (from_a, count + place_ref[0] * border, None),
         (from_b, count + (1 - place_ref[0]) * border, place_ref[1].astype(f32)),
@@ -127,11 +123,21 @@
         table[aligned(first + half, half), :] = both[:, LANES:]
 
 
+def fill_own(x_ref, edge_in, table, receiver_part):
+    both = mm(x_ref[...], jnp.concatenate([edge_in[:LANES, :], edge_in[LANES : 2 * LANES, :]], axis=1))
+    table[: x_ref.shape[0], :] = both[:, :LANES]
+    receiver_part[...] = both[:, LANES:].astype(bf16)
+
+
+def prepare_kernel(x_ref, edge_in, edge_out, node_in, node_out, gain_ref, sender_part, receiver_part):
+    fill_own(x_ref, edge_in, sender_part, receiver_part)
+
+
 def fine_kernel(
-    place_ref, pool_index, sender_ref, edge_ref, x_ref, from_a, from_b, receiver_ref,
-    edge_in, edge_out, node_in, node_out, gain_ref,
+    place_ref, pool_index, sender_ref, edge_ref, x_ref, from_a, from_b, sender_part,
+    receiver_part, receiver_ref, edge_in, edge_out, node_in, node_out, gain_ref,
     new_ref, a_ref, b_ref,
-    table, receiver_part, new32, buffer, aggregate, node_hidden,
+    table, new32, buffer, aggregate, node_hidden,
     gathered0, gathered1, hidden0, hidden1, message0, message1,
     index0, index1, index2, index3, index_sem, w_out, w_node_out, spread_of, w_pairs,
 ):
@@ -154,7 +160,8 @@
     for k in range(GROUP):
         index_copy(k, k).start()
     fill_weights(edge_out, node_out, w_out, w_node_out, spread_of)
-    fill_table(x_ref, place_ref, from_a, from_b, edge_in, table, receiver_part, w_pairs)
+    table[: x_ref.shape[0], :] = sender_part[...]
+    fill_border(x_ref, place_ref, from_a, from_b, edge_in, table, w_pairs)
     index_copy(0, 0).wait()
     gather_block(0, gathered0)
 
@@ -280,7 +287,8 @@
     blocks, _, block = receiver_ref.shape
     nodes = x_ref.shape[0] // blocks
     fill_weights(edge_out, node_out, w_out, w_node_out, spread_of)
-    fill_table(x_ref, place_ref, from_a, from_b, edge_in, table, receiver_part, w_pairs)
+    fill_own(x_ref, edge_in, table, receiver_part)
+    fill_border(x_ref, place_ref, from_a, from_b, edge_in, table, w_pairs)
     keep = {}
 
     def gather_part(t, part):
@@ -459,6 +467,10 @@
             us=3.0,
         )
         from_a, from_b = swap_with_neighbours(for_a, for_b)
+        prepared = call(
+            prepare_kernel, "fine_prepare", [rows_of(fine_total, f32), rows_of(fine_total)],
+            [whole_vmem] + weight_specs, [], (fine_latent,) + weights, level=0, us=2.0,
+        )
         lift_picks = call(
             lift_kernel, "lift_picks", rows_of(fine_total, bf16, coarse_total), [whole_vmem], [],
             (fine_parent.reshape(fine_total // coarse_total, 1, coarse_total),),
@@ -469,10 +481,9 @@
         fine_new, for_a, for_b = call(
             fine_kernel, "fine_step",
             [rows_of(fine_total), rows_of(slots), rows_of(slots)],
-            [whole_smem, whole_smem, left_in_hbm] + [whole_vmem] * 5 + weight_specs,
+            [whole_smem, whole_smem, left_in_hbm] + [whole_vmem] * 7 + weight_specs,
             [
                 pltpu.VMEM((fine_total + 2 * border, LANES), f32),
-                pltpu.VMEM((fine_total, LANES), bf16),
                 pltpu.VMEM((fine_total, LANES), f32),
                 pltpu.VMEM((2 * slots, LANES), f32),
                 pltpu.VMEM((GROUP * nodes, LANES), bf16),
@@ -484,7 +495,7 @@
             + [pltpu.SemaphoreType.DMA((GROUP,))]
             + weight_scratch,
             (
-                place, pool_rows, fine_sender, fine_edges, fine_latent, from_a, from_b,
+                place, pool_rows, fine_sender, fine_edges, fine_latent, from_a, from_b, *prepared,
                 fine_receiver.reshape(blocks, 1, block),
             )
             + weights,

time: 77.8 us -> 77.5 us (level)
  waiting for transfers between devices: 13.3 us -> 12.5 us
    ppermute x4, waiting for transfers between devices: 8.75 us -> 7.9 us  [swap_with_neighbours(): lax.ppermute(for_b, 'dom', pairs_b)]
    pallas_call x7 -> x8, Pallas kernels: 33.7 us -> 34 us  [call(): pl.pallas_call(with_level, name=name, out_shape=outs, in_specs=[pl.BlockS...]
  transfers between devices with their start and end apart: 14 -> 14, of which waited for: 8 -> 8; matrix products, arithmetic and copies ran while one was open for 0% -> 0% of each run, Pallas kernels for 3% -> 4%
where the time goes in v5:
time: 77.5 us; the launch traced here: 77.3 us
  Pallas kernels  34 us (44%)
  starting transfers between devices  26.7 us (34%)
  waiting for transfers between devices  12.5 us (16%)
  local copies, waits for them, and re-layouts  2.17 us (3%)
  between operations  1.71 us (2%)
    pallas_call x8, Pallas kernels, call(): pl.pallas_call(with_level, name=name, out_shape=outs, in_specs=[pl.BlockS...  34 us
    ppermute x4, starting transfers between devices, swap_with_neighbours(): lax.ppermute(for_b, 'dom', pairs_b)  19.2 us
    ppermute x4, waiting for transfers between devices, swap_with_neighbours(): lax.ppermute(for_b, 'dom', pairs_b)  7.9 us
    ppermute x6, starting transfers between devices, gather_all(): lax.ppermute(blocks, 'dom', [(i, i ^ j * stride) for i in range(count)])  6.78 us
    ppermute x6, waiting for transfers between devices, gather_all(): lax.ppermute(blocks, 'dom', [(i, i ^ j * stride) for i in range(count)])  4.54 us
    unnamed x50, local copies, waits for them, and re-layouts  2.05 us
  transfers between devices with their start and end apart: 14, of which 8 were waited for; matrix products, arithmetic and copies ran while one was open for 0% of the time, Pallas kernels for 4%

profile of v5, /device:TPU:0, one launch (start us, length us, event | category | flops | bytes accessed | tf_op | source)
XLA Modules:
  0.0 77.3 jit_solution(14561862151930410755)
XLA Ops:
  1.3 0.1 stack.43.refs_0_
  1.4 1.2 %copy-done.1 = bf16[4096,128]{1,0:T(8,128)(2,1)S(1)} copy-done((bf16[4096,128]{1,0:T(8,128)(2,1)S(1)}, bf16[4096,128]{1,0:T(8,128)(2,1)}, u32[]{:S(2)}) %copy-start.1) | copy-done | bytes 1048600
  2.6 0.7 copy-done.13
  3.4 1.9 %border_rows.1 = (bf16[1024,128]{1,0:T(8,128)(2,1)S(1)}, bf16[1024,128]{1,0:T(8,128)(2,1)S(1)}) custom-call(s32[5]{0:T(128)S(1)} %stack.43.refs_0_, s32[1,2,1024]{2,1,0:T(2,128)S(1)} %copy-done.13, bf16[4096,128]{1,0:T(8,128)(2,1)S(1)} %copy-done.1), custom_call_target="tpu_custom_call" | custom-call | flops 3000000000 | tf_op jit(solution)/shard_map/fine_border_rows/border_rows/pallas_call | solution.py:397
  5.4 0.5 collective-permute-start
  5.9 5.7 %collective-permute-start.1 = (bf16[1024,128]{1,0:T(8,128)(2,1)S(1)}, bf16[1024,128]{1,0:T(8,128)(2,1)S(1)}, u32[]{:S(2)}, u32[]{:S(2)}) collective-permute-start(bf16[1024,128]{1,0:T(8,128)(2,1)S(1)} %get-tuple-element.17), channel_id=1, source_target_pairs={{1,2},{3,4},{5,6},{7,8},{9,10},{11,12},{13,14},{15,0},{2,1},{4,3},... | collective-permute-start | bytes 786440 | tf_op jit(solution)/shard_map/fine_border_rows/ppermute | solution.py:418
  11.6 0.7 fine_prepare.1
  12.3 3.3 %collective-permute-done.1.refs_6_ = bf16[1024,128]{1,0:T(8,128)(2,1)S(1)} collective-permute-done((bf16[1024,128]{1,0:T(8,128)(2,1)S(1)}, bf16[1024,128]{1,0:T(8,128)(2,1)S(1)}, u32[]{:S(2)}, u32[]{:S(2)}) %collective-permute-start.1) | collective-permute-done | bytes 262176 | tf_op jit(solution)/shard_map/fine_border_rows/ppermute | solution.py:418
  15.7 19.7 %fine_step.1 = (bf16[4096,128]{1,0:T(8,128)(2,1)S(1)}, bf16[512,128]{1,0:T(8,128)(2,1)S(1)}, bf16[512,128]{1,0:T(8,128)(2,1)S(1)}) custom-call(s32[5]{0:T(128)S(1)} %stack.43.refs_0_, s32[1,2,512]{2,1,0:T(2,128)S(1)} %copy-done.18, s32[16384]{0:T(1024)S(1)} %copy-done.9, bf16[16384,128]{1,0:T(8,128)(2,1)S(1)} %copy-done, bf16[4096,128]{1,0:T(8,128)(2,1)S(1)} %copy-done.2, ...), custom_call_target="tpu_custom_call" | custom-call | flops 24000000000 | tf_op jit(solution)/shard_map/fine_step/fine_step/pallas_call | solution.py:397
  35.4 0.1 collective-permute-start.2
  35.5 4.5 %collective-permute-start.3 = (bf16[512,128]{1,0:T(8,128)(2,1)S(1)}, bf16[512,128]{1,0:T(8,128)(2,1)S(1)}, u32[]{:S(2)}, u32[]{:S(2)}) collective-permute-start(bf16[512,128]{1,0:T(8,128)(2,1)S(1)} %get-tuple-element.22), channel_id=1, source_target_pairs={{1,2},{3,4},{5,6},{7,8},{9,10},{11,12},{13,14},{15,0},{2,1},{4,3},... | collective-permute-start | bytes 393224 | tf_op jit(solution)/shard_map/fine_step/ppermute | solution.py:418
  40.0 1.2 %local_pool_step.1.refs_2_ = f32[512,256]{1,0:T(8,128)S(1)} custom-call(bf16[4096,128]{1,0:T(8,128)(2,1)S(1)} %get-tuple-element.20.refs_0_.refs_8_, s32[8,1,512]{2,1,0:T(1,128)S(1)} %bitcast.31, s32[8,1,512]{2,1,0:T(1,128)S(1)} %bitcast.30), custom_call_target="tpu_custom_call" | custom-call | flops 2000000000 | tf_op jit(solution)/shard_map/fine_step/local_pool_step/pallas_call | solution.py:397
  41.3 1.3 %collective-permute-done.3.refs_4_ = bf16[512,128]{1,0:T(8,128)(2,1)S(1)} collective-permute-done((bf16[512,128]{1,0:T(8,128)(2,1)S(1)}, bf16[512,128]{1,0:T(8,128)(2,1)S(1)}, u32[]{:S(2)}, u32[]{:S(2)}) %collective-permute-start.3) | collective-permute-done | bytes 131104 | tf_op jit(solution)/shard_map/fine_step/ppermute | solution.py:418
  42.6 1.1 %coarse_input.1 = (bf16[512,128]{1,0:T(8,128)(2,1)S(1)}, bf16[128,128]{1,0:T(8,128)(2,1)S(1)}, bf16[128,128]{1,0:T(8,128)(2,1)S(1)}) custom-call(s32[5]{0:T(128)S(1)} %stack.43.refs_0_, s32[1,2,128]{2,1,0:T(2,128)S(1)} %copy-done.22, f32[512,256]{1,0:T(8,128)S(1)} %local_pool_step.1.refs_2_, bf16[512,128]{1,0:T(8,128)(2,1)S(1)} %collective-permute-done.2.refs_3_, ...), custom_call_target="tpu_custom_call" | custom-call | flops 1000000000 | tf_op jit(solution)/shard_map/coarse_input/coarse_input/pallas_call | solution.py:397
  43.8 0.1 collective-permute-start.4
  43.9 4.5 %collective-permute-start.5 = (bf16[128,128]{1,0:T(8,128)(2,1)S(1)}, bf16[128,128]{1,0:T(8,128)(2,1)S(1)}, u32[]{:S(2)}, u32[]{:S(2)}) collective-permute-start(bf16[128,128]{1,0:T(8,128)(2,1)S(1)} %get-tuple-element.25), channel_id=1, source_target_pairs={{1,2},{3,4},{5,6},{7,8},{9,10},{11,12},{13,14},{15,0},{2,1},{4,3},... | collective-permute-start | bytes 98312 | tf_op jit(solution)/shard_map/coarse_input/ppermute | solution.py:418
  48.4 1.6 %collective-permute-done.5.refs_5_ = bf16[128,128]{1,0:T(8,128)(2,1)S(1)} collective-permute-done((bf16[128,128]{1,0:T(8,128)(2,1)S(1)}, bf16[128,128]{1,0:T(8,128)(2,1)S(1)}, u32[]{:S(2)}, u32[]{:S(2)}) %collective-permute-start.5) | collective-permute-done | bytes 32800 | tf_op jit(solution)/shard_map/coarse_input/ppermute | solution.py:418
  50.0 3.6 %coarse_step.1 = (bf16[512,128]{1,0:T(8,128)(2,1)S(1)}, f32[72,128]{1,0:T(8,128)S(1)}, f32[72,128]{1,0:T(8,128)S(1)}, f32[72,128]{1,0:T(8,128)S(1)}) custom-call(s32[5]{0:T(128)S(1)} %stack.43.refs_0_, s32[2048]{0:T(1024)S(1)} %copy-done.14, bf16[2048,128]{1,0:T(8,128)(2,1)S(1)} %copy-done.3, bf16[512,128]{1,0:T(8,128)(2,1)S(1)} %get-tuple-element.23.refs_3_, ...), custom_call_target="tpu_custom_call" | custom-call | flops 4000000000 | tf_op jit(solution)/shard_map/coarse_step/coarse_step/pallas_call | solution.py:397
  53.7 4.5 %collective-permute-start.7 = (f32[72,128]{1,0:T(8,128)S(1)}, f32[72,128]{1,0:T(8,128)S(1)}, u32[]{:S(2)}, u32[]{:S(2)}) collective-permute-start(f32[72,128]{1,0:T(8,128)S(1)} %get-tuple-element.28), channel_id=1, source_target_pairs={{1,2},{3,4},{5,6},{7,8},{9,10},{11,12},{13,14},{15,0},{2,1},{4,3},... | collective-permute-start | bytes 110600 | tf_op jit(solution)/shard_map/coarse_step/ppermute | solution.py:418
  58.2 1.7 %collective-permute-done.7 = f32[72,128]{1,0:T(8,128)S(1)} collective-permute-done((f32[72,128]{1,0:T(8,128)S(1)}, f32[72,128]{1,0:T(8,128)S(1)}, u32[]{:S(2)}, u32[]{:S(2)}) %collective-permute-start.7) | collective-permute-done | bytes 36896 | tf_op jit(solution)/shard_map/coarse_step/ppermute | solution.py:418
  59.9 0.1 fusion.4
  60.0 0.1 collective-permute-start.10
  60.1 4.3 %collective-permute-start.8 = (bf16[1,64,128]{2,1,0:T(8,128)(2,1)S(1)}, bf16[1,64,128]{2,1,0:T(8,128)(2,1)S(1)}, u32[]{:S(2)}, u32[]{:S(2)}) collective-permute-start(bf16[1,64,128]{2,1,0:T(8,128)(2,1)S(1)} %fusion.4), channel_id=1, source_target_pairs={{0,4},{1,5},{2,6},{3,7},{4,0},{5,1},{6,2},{7,3},{8,12},{9,13},{10,... | collective-permute-start | bytes 49160 | tf_op jit(solution)/shard_map/top_step/ppermute | solution.py:432
  64.4 0.1 fusion.3
  64.5 1.2 %collective-permute-done.10 = bf16[1,64,128]{2,1,0:T(8,128)(2,1)S(1)} collective-permute-done((bf16[1,64,128]{2,1,0:T(8,128)(2,1)S(1)}, bf16[1,64,128]{2,1,0:T(8,128)(2,1)S(1)}, u32[]{:S(2)}, u32[]{:S(2)}) %collective-permute-start.10) | collective-permute-done | bytes 16416 | tf_op jit(solution)/shard_map/top_step/ppermute | solution.py:432
  65.7 0.4 collective-permute-done.8
  66.2 2.1 %collective-permute-start.13 = (bf16[4,64,128]{2,1,0:T(8,128)(2,1)S(1)}, bf16[4,64,128]{2,1,0:T(8,128)(2,1)S(1)}, u32[]{:S(2)}, u32[]{:S(2)}) collective-permute-start(bf16[4,64,128]{2,1,0:T(8,128)(2,1)S(1)} %get-tuple-element.31), channel_id=1, source_target_pairs={{0,3},{1,2},{2,1},{3,0},{4,7},{5,6},{6,5},{7,4},{8,11},{9,10},{10,... | collective-permute-start | bytes 196616 | tf_op jit(solution)/shard_map/top_step/ppermute | solution.py:432
  68.3 0.2 collective-permute-start.11
  68.5 1.1 %lift_picks.1.refs_2_ = bf16[4096,512]{1,0:T(8,128)(2,1)S(1)} custom-call(s32[8,1,512]{2,1,0:T(1,128)S(1)} %bitcast.32), custom_call_target="tpu_custom_call" | custom-call | flops 3000000000 | tf_op jit(solution)/shard_map/fine_border_rows/lift_picks/pallas_call | solution.py:397
  69.7 0.6 collective-permute-done.13
  70.3 2.3 %collective-permute-done.12 = bf16[4,64,128]{2,1,0:T(8,128)(2,1)S(1)} collective-permute-done((bf16[4,64,128]{2,1,0:T(8,128)(2,1)S(1)}, bf16[4,64,128]{2,1,0:T(8,128)(2,1)S(1)}, u32[]{:S(2)}, u32[]{:S(2)}) %collective-permute-start.12) | collective-permute-done | bytes 65568 | tf_op jit(solution)/shard_map/top_step/ppermute | solution.py:432
  72.7 4.6 %top_step.1 = (bf16[4096,128]{1,0:T(8,128)(2,1)}, bf16[512,128]{1,0:T(8,128)(2,1)}) custom-call(s32[5]{0:T(128)S(1)} %stack.43.refs_0_, s32[2048]{0:T(1024)S(1)} %copy-done.16, bf16[4096,512]{1,0:T(8,128)(2,1)S(1)} %lift_picks.1.refs_2_, bf16[2048,128]{1,0:T(8,128)(2,1)S(1)} %copy-done.4, bf16[1024,128]{1,0:T(8,128)(2,1)S(1)} %bitcast.28, ...), custom_call_target="tpu_custom_call" | custom-call | flops 5000000000 | tf_op jit(solution)/shard_map/top_step/top_step/pallas_call | solution.py:397
  (64 shorter events, 0.4 us)
Async XLA Ops:
  3.3 8.2 %copy-start.24 = (s32[1,2,512]{2,1,0:T(2,128)S(1)}, s32[1,2,512]{2,1,0:T(2,128)}, u32[]{:S(2)}) copy-start(s32[1,2,512]{2,1,0:T(2,128)} %param.33) | copy-start | bytes 12292
  3.3 8.3 %copy-start.2 = (bf16[4096,128]{1,0:T(8,128)(2,1)S(1)}, bf16[4096,128]{1,0:T(8,128)(2,1)}, u32[]{:S(2)}) copy-start(bf16[4096,128]{1,0:T(8,128)(2,1)} %refs_4_.3) | copy-start | bytes 3145732
  3.3 8.3 %copy-start.5 = (bf16[3,384,128]{2,1,0:T(8,128)(2,1)S(1)}, bf16[3,384,128]{2,1,0:T(8,128)(2,1)}, u32[]{:S(2)}) copy-start(bf16[3,384,128]{2,1,0:T(8,128)(2,1)} %refs_9_.3) | copy-start | bytes 884740
  3.3 8.3 %copy-start.6 = (bf16[3,256,128]{2,1,0:T(8,128)(2,1)S(1)}, bf16[3,256,128]{2,1,0:T(8,128)(2,1)}, u32[]{:S(2)}) copy-start(bf16[3,256,128]{2,1,0:T(8,128)(2,1)} %refs_11_.5) | copy-start | bytes 589828
  3.3 8.3 %copy-start.7 = (bf16[3,128,128]{2,1,0:T(8,128)(2,1)S(1)}, bf16[3,128,128]{2,1,0:T(8,128)(2,1)}, u32[]{:S(2)}) copy-start(bf16[3,128,128]{2,1,0:T(8,128)(2,1)} %refs_10_.5) | copy-start | bytes 294916
  3.3 8.3 %copy-start.8 = (bf16[3,128,128]{2,1,0:T(8,128)(2,1)S(1)}, bf16[3,128,128]{2,1,0:T(8,128)(2,1)}, u32[]{:S(2)}) copy-start(bf16[3,128,128]{2,1,0:T(8,128)(2,1)} %refs_12_.5) | copy-start | bytes 294916
  3.4 8.3 %copy-start.19 = (f32[3,2,128]{2,1,0:T(2,128)S(1)}, f32[3,2,128]{2,1,0:T(2,128)}, u32[]{:S(2)}) copy-start(f32[3,2,128]{2,1,0:T(2,128)} %refs_13_.5) | copy-start | bytes 9220
  5.3 10.3 %copy-start = (bf16[16384,128]{1,0:T(8,128)(2,1)S(1)}, bf16[16384,128]{1,0:T(8,128)(2,1)}, u32[]{:S(2)}) copy-start(bf16[16384,128]{1,0:T(8,128)(2,1)} %refs_3_.4) | copy-start | bytes 12582916
  5.3 10.3 %copy-start.9 = (s32[16384]{0:T(1024)S(1)}, s32[16384]{0:T(1024)}, u32[]{:S(2)}) copy-start(s32[16384]{0:T(1024)} %refs_2_.6) | copy-start | bytes 196612
  5.3 10.3 %copy-start.10 = (s32[16384]{0:T(1024)S(1)}, s32[16384]{0:T(1024)}, u32[]{:S(2)}) copy-start(s32[16384]{0:T(1024)} %param.28) | copy-start | bytes 196612
  5.3 10.3 %copy-start.18 = (s32[1,2,512]{2,1,0:T(2,128)S(1)}, s32[1,2,512]{2,1,0:T(2,128)}, u32[]{:S(2)}) copy-start(s32[1,2,512]{2,1,0:T(2,128)} %refs_1_.8) | copy-start | bytes 12292
  5.4 7.0 %collective-permute-start = (bf16[1024,128]{1,0:T(8,128)(2,1)S(1)}, bf16[1024,128]{1,0:T(8,128)(2,1)S(1)}, u32[]{:S(2)}, u32[]{:S(2)}) collective-permute-start(bf16[1024,128]{1,0:T(8,128)(2,1)S(1)} %get-tuple-element.16), channel_id=1, source_target_pairs={{0,1},{1,0},{2,3},{3,2},{4,5},{5,4},{6,7},{7,6},{8,9},{9,8},{10,11... | collective-permute-start | bytes 786440 | tf_op jit(solution)/shard_map/fine_border_rows/ppermute | solution.py:418
  5.9 9.8 %collective-permute-start.1 = (bf16[1024,128]{1,0:T(8,128)(2,1)S(1)}, bf16[1024,128]{1,0:T(8,128)(2,1)S(1)}, u32[]{:S(2)}, u32[]{:S(2)}) collective-permute-start(bf16[1024,128]{1,0:T(8,128)(2,1)S(1)} %get-tuple-element.17), channel_id=1, source_target_pairs={{1,2},{3,4},{5,6},{7,8},{9,10},{11,12},{13,14},{15,0},{2,1},{4,3},... | collective-permute-start | bytes 786440 | tf_op jit(solution)/shard_map/fine_border_rows/ppermute | solution.py:418
  15.7 24.3 %copy-start.11 = (s32[4096]{0:T(1024)S(1)}, s32[4096]{0:T(1024)}, u32[]{:S(2)}) copy-start(s32[4096]{0:T(1024)} %param.35) | copy-start | bytes 49156
  15.7 24.3 %copy-start.12 = (s32[4096]{0:T(1024)S(1)}, s32[4096]{0:T(1024)}, u32[]{:S(2)}) copy-start(s32[4096]{0:T(1024)} %param.34) | copy-start | bytes 49156
  35.4 5.9 %collective-permute-start.2 = (bf16[512,128]{1,0:T(8,128)(2,1)S(1)}, bf16[512,128]{1,0:T(8,128)(2,1)S(1)}, u32[]{:S(2)}, u32[]{:S(2)}) collective-permute-start(bf16[512,128]{1,0:T(8,128)(2,1)S(1)} %get-tuple-element.21), channel_id=1, source_target_pairs={{0,1},{1,0},{2,3},{3,2},{4,5},{5,4},{6,7},{7,6},{8,9},{9,8},{10,11... | collective-permute-start | bytes 393224 | tf_op jit(solution)/shard_map/fine_step/ppermute | solution.py:418
  35.5 7.2 %collective-permute-start.3 = (bf16[512,128]{1,0:T(8,128)(2,1)S(1)}, bf16[512,128]{1,0:T(8,128)(2,1)S(1)}, u32[]{:S(2)}, u32[]{:S(2)}) collective-permute-start(bf16[512,128]{1,0:T(8,128)(2,1)S(1)} %get-tuple-element.22), channel_id=1, source_target_pairs={{1,2},{3,4},{5,6},{7,8},{9,10},{11,12},{13,14},{15,0},{2,1},{4,3},... | collective-permute-start | bytes 393224 | tf_op jit(solution)/shard_map/fine_step/ppermute | solution.py:418
  40.0 10.0 %copy-start.3 = (bf16[2048,128]{1,0:T(8,128)(2,1)S(1)}, bf16[2048,128]{1,0:T(8,128)(2,1)}, u32[]{:S(2)}) copy-start(bf16[2048,128]{1,0:T(8,128)(2,1)} %refs_2_.7) | copy-start | bytes 1572868
  40.0 10.0 %copy-start.14 = (s32[2048]{0:T(1024)S(1)}, s32[2048]{0:T(1024)}, u32[]{:S(2)}) copy-start(s32[2048]{0:T(1024)} %refs_1_.10) | copy-start | bytes 24580
  40.0 10.0 %copy-start.15 = (s32[2048]{0:T(1024)S(1)}, s32[2048]{0:T(1024)}, u32[]{:S(2)}) copy-start(s32[2048]{0:T(1024)} %param.38) | copy-start | bytes 24580
  40.0 10.0 %copy-start.20 = (s32[512]{0:T(512)S(1)}, s32[512]{0:T(512)}, u32[]{:S(2)}) copy-start(s32[512]{0:T(512)} %param.41) | copy-start | bytes 6148
  40.0 10.0 %copy-start.21 = (s32[512]{0:T(512)S(1)}, s32[512]{0:T(512)}, u32[]{:S(2)}) copy-start(s32[512]{0:T(512)} %param.40) | copy-start | bytes 6148
  43.8 4.6 %collective-permute-start.4 = (bf16[128,128]{1,0:T(8,128)(2,1)S(1)}, bf16[128,128]{1,0:T(8,128)(2,1)S(1)}, u32[]{:S(2)}, u32[]{:S(2)}) collective-permute-start(bf16[128,128]{1,0:T(8,128)(2,1)S(1)} %get-tuple-element.24), channel_id=1, source_target_pairs={{0,1},{1,0},{2,3},{3,2},{4,5},{5,4},{6,7},{7,6},{8,9},{9,8},{10,11... | collective-permute-start | bytes 98312 | tf_op jit(solution)/shard_map/coarse_input/ppermute | solution.py:418
  43.9 6.1 %collective-permute-start.5 = (bf16[128,128]{1,0:T(8,128)(2,1)S(1)}, bf16[128,128]{1,0:T(8,128)(2,1)S(1)}, u32[]{:S(2)}, u32[]{:S(2)}) collective-permute-start(bf16[128,128]{1,0:T(8,128)(2,1)S(1)} %get-tuple-element.25), channel_id=1, source_target_pairs={{1,2},{3,4},{5,6},{7,8},{9,10},{11,12},{13,14},{15,0},{2,1},{4,3},... | collective-permute-start | bytes 98312 | tf_op jit(solution)/shard_map/coarse_input/ppermute | solution.py:418
  53.6 4.6 %collective-permute-start.6 = (f32[72,128]{1,0:T(8,128)S(1)}, f32[72,128]{1,0:T(8,128)S(1)}, u32[]{:S(2)}, u32[]{:S(2)}) collective-permute-start(f32[72,128]{1,0:T(8,128)S(1)} %get-tuple-element.27), channel_id=1, source_target_pairs={{0,1},{1,0},{2,3},{3,2},{4,5},{5,4},{6,7},{7,6},{8,9},{9,8},{10,11... | collective-permute-start | bytes 110600 | tf_op jit(solution)/shard_map/coarse_step/ppermute | solution.py:418
  53.7 6.2 %collective-permute-start.7 = (f32[72,128]{1,0:T(8,128)S(1)}, f32[72,128]{1,0:T(8,128)S(1)}, u32[]{:S(2)}, u32[]{:S(2)}) collective-permute-start(f32[72,128]{1,0:T(8,128)S(1)} %get-tuple-element.28), channel_id=1, source_target_pairs={{1,2},{3,4},{5,6},{7,8},{9,10},{11,12},{13,14},{15,0},{2,1},{4,3},... | collective-permute-start | bytes 110600 | tf_op jit(solution)/shard_map/coarse_step/ppermute | solution.py:418
  60.0 5.8 %collective-permute-start.10 = (bf16[1,64,128]{2,1,0:T(8,128)(2,1)S(1)}, bf16[1,64,128]{2,1,0:T(8,128)(2,1)S(1)}, u32[]{:S(2)}, u32[]{:S(2)}) collective-permute-start(bf16[1,64,128]{2,1,0:T(8,128)(2,1)S(1)} %fusion.4), channel_id=1, source_target_pairs={{0,12},{1,13},{2,14},{3,15},{4,8},{5,9},{6,10},{7,11},{8,4},{9,5},... | collective-permute-start | bytes 49160 | tf_op jit(solution)/shard_map/top_step/ppermute | solution.py:432
  60.0 5.7 %collective-permute-start.9 = (bf16[1,64,128]{2,1,0:T(8,128)(2,1)S(1)}, bf16[1,64,128]{2,1,0:T(8,128)(2,1)S(1)}, u32[]{:S(2)}, u32[]{:S(2)}) collective-permute-start(bf16[1,64,128]{2,1,0:T(8,128)(2,1)S(1)} %fusion.4), channel_id=1, source_target_pairs={{0,8},{1,9},{2,10},{3,11},{4,12},{5,13},{6,14},{7,15},{8,0},{9,1},... | collective-permute-start | bytes 49160 | tf_op jit(solution)/shard_map/top_step/ppermute | solution.py:432
  60.1 6.0 %collective-permute-start.8 = (bf16[1,64,128]{2,1,0:T(8,128)(2,1)S(1)}, bf16[1,64,128]{2,1,0:T(8,128)(2,1)S(1)}, u32[]{:S(2)}, u32[]{:S(2)}) collective-permute-start(bf16[1,64,128]{2,1,0:T(8,128)(2,1)S(1)} %fusion.4), channel_id=1, source_target_pairs={{0,4},{1,5},{2,6},{3,7},{4,0},{5,1},{6,2},{7,3},{8,12},{9,13},{10,... | collective-permute-start | bytes 49160 | tf_op jit(solution)/shard_map/top_step/ppermute | solution.py:432
  66.2 4.1 %collective-permute-start.13 = (bf16[4,64,128]{2,1,0:T(8,128)(2,1)S(1)}, bf16[4,64,128]{2,1,0:T(8,128)(2,1)S(1)}, u32[]{:S(2)}, u32[]{:S(2)}) collective-permute-start(bf16[4,64,128]{2,1,0:T(8,128)(2,1)S(1)} %get-tuple-element.31), channel_id=1, source_target_pairs={{0,3},{1,2},{2,1},{3,0},{4,7},{5,6},{6,5},{7,4},{8,11},{9,10},{10,... | collective-permute-start | bytes 196616 | tf_op jit(solution)/shard_map/top_step/ppermute | solution.py:432
  68.3 4.3 %collective-permute-start.12 = (bf16[4,64,128]{2,1,0:T(8,128)(2,1)S(1)}, bf16[4,64,128]{2,1,0:T(8,128)(2,1)S(1)}, u32[]{:S(2)}, u32[]{:S(2)}) collective-permute-start(bf16[4,64,128]{2,1,0:T(8,128)(2,1)S(1)} %get-tuple-element.31), channel_id=1, source_target_pairs={{0,2},{1,3},{2,0},{3,1},{4,6},{5,7},{6,4},{7,5},{8,10},{9,11},{10,... | collective-permute-start | bytes 196616 | tf_op jit(solution)/shard_map/top_step/ppermute | solution.py:432
  68.3 4.3 %collective-permute-start.11 = (bf16[4,64,128]{2,1,0:T(8,128)(2,1)S(1)}, bf16[4,64,128]{2,1,0:T(8,128)(2,1)S(1)}, u32[]{:S(2)}, u32[]{:S(2)}) collective-permute-start(bf16[4,64,128]{2,1,0:T(8,128)(2,1)S(1)} %get-tuple-element.31), channel_id=1, source_target_pairs={{0,1},{1,0},{2,3},{3,2},{4,5},{5,4},{6,7},{7,6},{8,9},{9,8},{10,11... | collective-permute-start | bytes 196616 | tf_op jit(solution)/shard_map/top_step/ppermute | solution.py:432
  (7 other events, 37.0 us)
